TPU v7x, 256 devices: a whole 4x4x8 slice. The times are simulated.
256 devices in a mesh: basin: 4 (over x), tile: 64 (over y, z, core).
Axes of the slice: x: 4, y: 4, z: 8, core: 2. Of those that a mesh axis runs over, the one named last changes fastest.
Arguments:
- depth_start: float32 [4, 4096, 512], P('basin', 'tile'), may hold values from -6 to 6
- roughness: float32 [4, 4096, 512], P('basin', 'tile'), may hold values from 0.025 to 0.25
- depth_seed: float32 [4, 4096, 512], P('basin', 'tile'), may hold values from -6 to 6
- zone_label: int32 [4, 4096, 512], P('basin', 'tile'), may hold values from 0 to 32511, as said below
- owner_slot: int32 [32512], replicated, may hold values from 0 to 32511, each once
- retention: float32 [128, 8192], P('basin', 'tile'), may hold values from 0 to 1
- forcing: float32 [128, 8192], P('basin', 'tile'), may hold values from -0.6 to 0.6
- levee_cell: int32 [128, 8192], P('basin', 'tile'), may hold values from 0 to 32767
Outputs:
- zone_gradient: float32 [32512], P(('basin', 'tile'))
- zone_curvature: float32 [32512], P(('basin', 'tile'))
- reach_adjoint: float32 [128, 8192], P('basin', 'tile')
Inputs may be any that keep to these rules, and one draw needn't show every extreme that they name: `zone_label`: seven cells in eight of the rows b, (t * 64) to (t * 64 + 63) take zones of the band (b * 64 + t) * 127 onward, 127 wide, lower ones more often; the others any zone. `owner_slot`: each zone once. `levee_cell`: Row-major index of a cell within rows (j // 128) * 64 to (j // 128) * 64 + 63 of basin i // 32.
All inputs are finite; a program needn't handle non-finite values.
Results may differ from a plain program's by a relative error of at most 0.0003.
Values sent between devices are 32-bit elements; how exact they have to be, the bound alone decides.
No kernel may reach another device: no remote copies, remote signals or barrier semaphores. Data moves between devices by JAX's collectives and lax.ppermute only.
A program may use at most 64 MiB of HBM per device.

v0:
```python
import functools

import jax
import jax.numpy as jnp
from jax import lax
from jax.experimental import pallas as pl
from jax.experimental.pallas import tpu as pltpu
from jax.sharding import PartitionSpec as P

STEPS = 4
HALO = STEPS
SPAN = 127
LANES = 128

courant = 0.24
rough_ref = 0.025
levee_gain = 0.1

VMEM = pl.BlockSpec(memory_space=pltpu.VMEM)
ROOMY = pltpu.CompilerParams(vmem_limit_bytes=48 * 2**20)


def iota_bf16(shape, offset=0):
    ids = lax.broadcasted_iota(jnp.int32, shape, len(shape) - 2)
    if len(shape) == 3:
        ids = ids + shape[1] * lax.broadcasted_iota(jnp.int32, shape, 0)
    return (ids + offset).astype(jnp.float32).astype(jnp.bfloat16)


def spread_rows(row):
    return jnp.broadcast_to(row, (16, row.shape[1])).astype(jnp.bfloat16)


def one_hot(spread, count, weights=None):
    width = spread.shape[1]
    ids = iota_bf16((count // 16, 16, width))
    hit = spread[None] == ids
    zero = jnp.zeros((), jnp.bfloat16)
    if weights is None:
        return jnp.where(hit, jnp.ones((), jnp.bfloat16), zero).reshape(count, width)
    return [jnp.where(hit, w[None], zero).reshape(count, width) for w in weights]


def slot_kernel(owner_ref, label_ref, device_ref, lane_ref, table_ref, turned_ref):
    table_ref[...] = jnp.zeros(table_ref.shape, jnp.float32)
    table_ref[0 : owner_ref.shape[0], :] = owner_ref[...].astype(jnp.float32)
    slots = jnp.transpose(table_ref[...])
    owners = jnp.floor((slots + 0.5) * (1.0 / SPAN))
    turned_ref[0:LANES, :] = owners.astype(jnp.bfloat16)
    turned_ref[LANES : 2 * LANES, :] = (slots - owners * SPAN).astype(jnp.bfloat16)

    def one_row(row, carry):
        label = label_ref[pl.ds(row, 1), :]
        width = label.shape[1]
        group = one_hot(spread_rows((label // LANES).astype(jnp.float32)), 256)
        found = jnp.dot(turned_ref[...], group, preferred_element_type=jnp.float32)
        hit = (label % LANES) == lax.broadcasted_iota(jnp.int32, (LANES, width), 0)
        device_ref[pl.ds(row, 1), :] = jnp.sum(
            jnp.where(hit, found[:LANES], 0.0), axis=0, keepdims=True
        )
        lane_ref[pl.ds(row, 1), :] = jnp.sum(
            jnp.where(hit, found[LANES:], 0.0), axis=0, keepdims=True
        )
        return carry

    lax.fori_loop(0, label_ref.shape[0], one_row, 0, unroll=4)


def slots_of(owner_slot, label):
    shape = jax.ShapeDtypeStruct(label.shape, jnp.float32)
    return pl.pallas_call(
        slot_kernel,
        out_shape=(shape, shape),
        in_specs=[VMEM, VMEM],
        out_specs=(VMEM, VMEM),
        scratch_shapes=[
            pltpu.VMEM((256, LANES), jnp.float32),
            pltpu.VMEM((256, 256), jnp.bfloat16),
        ],
        compiler_params=ROOMY,
        cost_estimate=pl.CostEstimate(
            flops=2 * 256 * 256 * label.size, bytes_accessed=16 * label.size, transcendentals=0
        ),
        name="slot_lookup",
    )(owner_slot.reshape(-1, LANES), label)


def below(x):
    return pltpu.roll(x, x.shape[0] - 1, 0)


def above(x):
    return pltpu.roll(x, 1, 0)


def rightward(x):
    return pltpu.roll(x, x.shape[1] - 1, 1)


def leftward(x):
    return pltpu.roll(x, 1, 1)


def window_kernel(depth_ref, rough_ref_, seed_ref, low_ref, high_ref, grad_ref, adjoint_ref):
    def extended(part, ref):
        start = part * HALO
        return jnp.concatenate(
            [low_ref[start : start + HALO, :], ref[...], high_ref[start : start + HALO, :]], axis=0
        )

    depth = extended(0, depth_ref)
    rough = extended(1, rough_ref_)
    adjoint = extended(2, seed_ref)
    rows, columns = depth.shape
    conduct = jnp.where(rough > 0, rough_ref / jnp.where(rough > 0, rough, 1.0), 0.0)
    not_last = lax.broadcasted_iota(jnp.int32, (rows, columns), 1) < columns - 1
    under = below(conduct)
    beside = rightward(conduct)
    down_face = (conduct > 0) & (under > 0)
    side_face = (conduct > 0) & (beside > 0) & not_last
    down_weight = jnp.where(down_face, (0.5 * courant) * (conduct + under), 0.0)
    side_weight = jnp.where(side_face, (0.5 * courant) * (conduct + beside), 0.0)

    def steps(field):
        return below(field) - field, rightward(field) - field

    def advanced(field, down_step, side_step):
        down_flux = down_weight * down_step
        side_flux = side_weight * side_step
        return field + ((down_flux - above(down_flux)) + (side_flux - leftward(side_flux)))

    depth_steps = []
    for section in range(STEPS):
        depth_steps.append(steps(depth))
        if section < STEPS - 1:
            depth = advanced(depth, *depth_steps[-1])
    down_total = jnp.zeros((rows, columns), jnp.float32)
    side_total = jnp.zeros((rows, columns), jnp.float32)
    for section in reversed(range(STEPS)):
        down_step, side_step = steps(adjoint)
        down_total = down_total + depth_steps[section][0] * down_step
        side_total = side_total + depth_steps[section][1] * side_step
        adjoint = advanced(adjoint, down_step, side_step)
    down_total = jnp.where(down_face, down_total, 0.0)
    side_total = jnp.where(side_face, side_total, 0.0)
    total = (down_total + above(down_total)) + (side_total + leftward(side_total))
    own = slice(HALO, rows - HALO)
    grad_ref[...] = ((0.5 * courant) * conduct * total)[own]
    adjoint_ref[...] = adjoint[own]


def window(depth, rough, seed, low, high):
    shape = jax.ShapeDtypeStruct(depth.shape, jnp.float32)
    return pl.pallas_call(
        window_kernel,
        out_shape=(shape, shape),
        in_specs=[VMEM] * 5,
        out_specs=(VMEM, VMEM),
        compiler_params=ROOMY,
        name="adjoint_window",
    )(depth, rough, seed, low, high)


def halves(x):
    upper = x.astype(jnp.bfloat16).astype(jnp.float32)
    return upper, x - upper


ZONE_ROWS = 8


def zone_kernel(grad_ref, device_ref, lane_ref, out_ref):
    out_ref[...] = jnp.zeros(out_ref.shape, jnp.float32)

    def some_rows(index, carry):
        left = []
        right = []
        for offset in range(ZONE_ROWS):
            row = pl.ds(index * ZONE_ROWS + offset, 1)
            grad = grad_ref[row, :]
            left.append(one_hot(spread_rows(device_ref[row, :]), 256))
            weights = [spread_rows(part) for part in halves(grad) + halves(grad * grad)]
            right.append(
                jnp.concatenate(one_hot(spread_rows(lane_ref[row, :]), LANES, weights), axis=0)
            )
        both = lax.dot_general(
            jnp.concatenate(left, axis=1),
            jnp.concatenate(right, axis=1),
            (((1,), (1,)), ((), ())),
            preferred_element_type=jnp.float32,
        )
        out_ref[...] += jnp.concatenate(
            [
                both[:, 0:LANES] + both[:, LANES : 2 * LANES],
                both[:, 2 * LANES : 3 * LANES] + both[:, 3 * LANES :],
            ],
            axis=1,
        )
        return carry

    lax.fori_loop(0, grad_ref.shape[0] // ZONE_ROWS, some_rows, 0)


def zone_partials(grad, device, lane):
    return pl.pallas_call(
        zone_kernel,
        out_shape=jax.ShapeDtypeStruct((256, 2 * LANES), jnp.float32),
        in_specs=[VMEM] * 3,
        out_specs=VMEM,
        compiler_params=ROOMY,
        cost_estimate=pl.CostEstimate(
            flops=2 * 256 * 512 * grad.size, bytes_accessed=12 * grad.size, transcendentals=0
        ),
        name="zone_partials",
    )(grad, device, lane)


def reach_kernel(adjoint_ref, cell_ref, keep_ref, forcing_ref, rate_ref, push_ref, edge_ref):
    rows, columns = adjoint_ref.shape
    upper, lower = halves(adjoint_ref[...])
    table = jnp.concatenate([upper, lower], axis=0).astype(jnp.bfloat16)
    reaches = cell_ref.shape[0]
    width = cell_ref.shape[1]
    values = []
    for reach in range(0, reaches, 4):
        cells = jnp.concatenate([cell_ref[reach + i : reach + i + 1, :] for i in range(4)], axis=1)
        column = (cells % columns).astype(jnp.float32)
        hot = jnp.concatenate(
            [one_hot(spread_rows(column - part * 256.0), 256) for part in range(columns // 256)],
            axis=0,
        )
        picked = jnp.dot(table, hot, preferred_element_type=jnp.float32)
        picked = picked[:rows] + picked[rows:]
        row_hit = (cells // columns) == lax.broadcasted_iota(jnp.int32, (rows, 4 * width), 0)
        found = jnp.sum(jnp.where(row_hit, picked, 0.0), axis=0, keepdims=True)
        values += [found[:, i * width : (i + 1) * width] for i in range(4)]
    rate = jnp.ones((1, width), jnp.float32)
    push = jnp.zeros((1, width), jnp.float32)
    for reach in reversed(range(reaches)):
        keep = keep_ref[reach : reach + 1, :]
        push = keep * push + (forcing_ref[reach : reach + 1, :] + levee_gain * values[reach])
        rate = keep * rate
        rate_ref[reach : reach + 1, :] = rate
        push_ref[reach : reach + 1, :] = push
    edge_ref[0:1, :] = rate
    edge_ref[1:2, :] = push


def reach_maps(adjoint, cells, keep, forcing):
    shape = jax.ShapeDtypeStruct(cells.shape, jnp.float32)
    return pl.pallas_call(
        reach_kernel,
        out_shape=(shape, shape, jax.ShapeDtypeStruct((2, cells.shape[1]), jnp.float32)),
        in_specs=[VMEM] * 4,
        out_specs=(VMEM, VMEM, VMEM),
        compiler_params=ROOMY,
        name="reach_maps",
    )(adjoint, cells, keep, forcing)


def moved(value, axis, steps):
    count = lax.axis_size(axis)
    pairs = [(i, i + steps) for i in range(count) if 0 <= i + steps < count]
    return lax.ppermute(value, axis, pairs)


def per_device(
    depth_start, roughness, depth_seed, zone_label, owner_slot, retention, forcing, levee_cell
):
    depth, rough, seed, label = depth_start[0], roughness[0], depth_seed[0], zone_label[0]
    rows = depth.shape[0]
    low = moved(jnp.concatenate([x[rows - HALO :] for x in (depth, rough, seed)]), "tile", 1)
    high = moved(jnp.concatenate([x[:HALO] for x in (depth, rough, seed)]), "tile", -1)
    device, lane = slots_of(owner_slot, label)
    grad, adjoint = window(depth, rough, seed, low, high)
    partials = zone_partials(grad, device, lane)
    arrived = lax.all_to_all(partials, ("basin", "tile"), 0, 0, tiled=True)
    rate, push, edge = reach_maps(adjoint, levee_cell, retention, forcing)
    incoming = jnp.zeros((edge.shape[1],), jnp.float32)
    edges = [moved(edge, "basin", -hop) for hop in range(1, lax.axis_size("basin"))]
    for from_below in reversed(edges):
        incoming = from_below[0] * incoming + from_below[1]
    reach_adjoint = rate * incoming[None, :] + push
    sums = jnp.sum(arrived, axis=0)
    return (sums[:SPAN], sums[LANES : LANES + SPAN], reach_adjoint)


def solution(mesh):
    in_specs = (
        P("basin", "tile", None),
        P("basin", "tile", None),
        P("basin", "tile", None),
        P("basin", "tile", None),
        P(),
        P("basin", "tile"),
        P("basin", "tile"),
        P("basin", "tile"),
    )
    out_specs = (P(("basin", "tile")), P(("basin", "tile")), P("basin", "tile"))
    return jax.shard_map(
        per_device, mesh=mesh, in_specs=in_specs, out_specs=out_specs, check_vma=False
    )
```

profile of v0, /device:TPU:1, one launch (start us, length us, event | category | flops | bytes accessed | tf_op | source)
XLA Modules:
  0.0 63.7 jit_solution(9153762177816859917)
XLA Ops:
  0.6 0.0 copy-start.6
  0.6 0.8 %slice_bitcast_fusion.2 = (f32[4,512]{1,0:T(4,128)S(1)}, f32[4,512]{1,0:T(4,128)S(1)}) fusion(f32[1,64,512]{2,1,0:T(8,128)} %param.8), kind=kLoop, calls=%fused_computation.5 | loop fusion | bytes 32768 | tf_op jit(solution)/shard_map/slice | solution.py:273
  1.4 0.8 %slice_bitcast_fusion = (f32[4,512]{1,0:T(4,128)S(1)}, f32[4,512]{1,0:T(4,128)S(1)}, f32[4,512]{1,0:T(4,128)S(1)}, f32[4,512]{1,0:T(4,128)S(1)}) fusion(f32[1,64,512]{2,1,0:T(8,128)} %param.10, f32[1,64,512]{2,1,0:T(8,128)} %param.9), kind=kLoop, calls=%fused_computation.3 | loop fusion | bytes 65536 | tf_op jit(solution)/shard_map/slice | solution.py:273
  2.2 4.9 %collective-permute-start = (f32[12,512]{1,0:T(8,128)S(1)}, f32[12,512]{1,0:T(8,128)S(1)}, u32[]{:S(2)}, u32[]{:S(2)}) collective-permute-start(f32[12,512]{1,0:T(8,128)S(1)} %pad_maximum_fusion), channel_id=1, source_target_pairs={{0,1},{1,2},{2,3},{3,4},{4,5},{5,6},{6,7},{7,8},{8,9},{9,10},{10,1... | collective-permute-start | bytes 73736 | tf_op jit(solution)/shard_map/ppermute | solution.py:264
  7.2 1.9 %collective-permute-start.1 = (f32[12,512]{1,0:T(8,128)S(1)}, f32[12,512]{1,0:T(8,128)S(1)}, u32[]{:S(2)}, u32[]{:S(2)}) collective-permute-start(f32[12,512]{1,0:T(8,128)S(1)} %pad_maximum_fusion.1), channel_id=1, source_target_pairs={{1,0},{2,1},{3,2},{4,3},{5,4},{6,5},{7,6},{8,7},{9,8},{10,9},{11,1... | collective-permute-start | bytes 73736 | tf_op jit(solution)/shard_map/ppermute | solution.py:264
  9.1 0.0 copy-done.6
  9.1 0.0 copy-start.7
  9.1 0.9 %copy-done.7 = s32[1,64,512]{2,1,0:T(8,128)S(1)} copy-done((s32[1,64,512]{2,1,0:T(8,128)S(1)}, s32[1,64,512]{2,1,0:T(8,128)}, u32[]{:S(2)}) %copy-start.7) | copy-done | bytes 131096
  10.0 8.6 %slot_lookup.1 = (f32[64,512]{1,0:T(8,128)S(1)}, f32[64,512]{1,0:T(8,128)S(1)}) custom-call(s32[254,128]{1,0:T(8,128)S(1)} %bitcast.24, s32[64,512]{1,0:T(8,128)S(1)} %bitcast.25), custom_call_target="tpu_custom_call" | custom-call | flops 4294967296 | bytes 524288 | tf_op jit(solution)/shard_map/slot_lookup/pallas_call | solution.py:71
  18.6 0.0 collective-permute-done.low_ref
  18.6 0.0 collective-permute-done.1.high_ref
  18.6 0.0 copy-done
  18.7 0.0 copy-done.1
  18.7 0.0 copy-done.2
  18.7 1.3 %adjoint_window.1 = (f32[64,512]{1,0:T(8,128)S(1)}, f32[64,512]{1,0:T(8,128)S(1)}) custom-call(f32[64,512]{1,0:T(8,128)S(1)} %bitcast.21, f32[64,512]{1,0:T(8,128)S(1)} %bitcast.22, f32[64,512]{1,0:T(8,128)S(1)} %bitcast.23, f32[12,512]{1,0:T(8,128)S(1)} %collective-permute-done.low_ref, f32[12,512]{1,0:T(8,128)S(1)} %collective-permute-done.1.high_ref), custom_call_target="tpu_custom_call" | custom-call | tf_op jit(solution)/shard_map/adjoint_window/pallas_call | solution.py:154
  20.0 10.3 %zone_partials.1 = f32[256,256]{1,0:T(8,128)S(1)} custom-call(f32[64,512]{1,0:T(8,128)S(1)} %get-tuple-element.10.grad_ref, f32[64,512]{1,0:T(8,128)S(1)} %get-tuple-element.11.device_ref, f32[64,512]{1,0:T(8,128)S(1)} %get-tuple-element.12.lane_ref), custom_call_target="tpu_custom_call" | custom-call | flops 8589934592 | bytes 393216 | tf_op jit(solution)/shard_map/zone_partials/pallas_call | solution.py:205
  30.3 1.0 %copy.11 = f32[256,1,256]{2,1,0:T(1,128)} copy(f32[256,1,256]{2,0,1:T(8,128)S(1)} %bitcast.20) | data formatting | bytes 524288 | tf_op jit(solution)/shard_map/all_to_all | solution.py:277
  31.3 15.6 %all-to-all-start = ((f32[256,1,256]{2,1,0:T(1,128)}), f32[256,1,256]{2,1,0:T(1,128)S(1)}, u32[]{:S(2)}, u32[]{:S(2)}) async-start(f32[256,1,256]{2,1,0:T(1,128)} %copy.11), calls=%async_computation | async-start | bytes 524288 | tf_op jit(solution)/shard_map/all_to_all | solution.py:277
  46.9 0.0 copy-done.3
  46.9 0.0 copy-done.4
  46.9 0.0 copy-done.5
  46.9 0.8 %reach_maps.1 = (f32[32,128]{1,0:T(8,128)S(1)}, f32[32,128]{1,0:T(8,128)S(1)}, f32[2,128]{1,0:T(2,128)S(1)}) custom-call(f32[64,512]{1,0:T(8,128)S(1)} %get-tuple-element.13.adjoint_ref, s32[32,128]{1,0:T(8,128)S(1)} %copy-done.3, f32[32,128]{1,0:T(8,128)S(1)} %copy-done.4, f32[32,128]{1,0:T(8,128)S(1)} %copy-done.5), custom_call_target="tpu_custom_call" | custom-call | tf_op jit(solution)/shard_map/reach_maps/pallas_call | solution.py:251
  47.8 1.3 %collective-permute-start.4 = (f32[2,128]{1,0:T(2,128)S(1)}, f32[2,128]{1,0:T(2,128)S(1)}, u32[]{:S(2)}, u32[]{:S(2)}) collective-permute-start(f32[2,128]{1,0:T(2,128)S(1)} %get-tuple-element.15), channel_id=1, source_target_pairs={{192,0},{193,1},{194,2},{195,3},{196,4},{197,5},{198,6},{199,7},{2... | collective-permute-start | bytes 3080 | tf_op jit(solution)/shard_map/ppermute | solution.py:264
  49.1 1.3 %collective-permute-start.3 = (f32[2,128]{1,0:T(2,128)S(1)}, f32[2,128]{1,0:T(2,128)S(1)}, u32[]{:S(2)}, u32[]{:S(2)}) collective-permute-start(f32[2,128]{1,0:T(2,128)S(1)} %get-tuple-element.15), channel_id=1, source_target_pairs={{128,0},{192,64},{129,1},{193,65},{130,2},{194,66},{131,3},{195,67... | collective-permute-start | bytes 3080 | tf_op jit(solution)/shard_map/ppermute | solution.py:264
  50.4 1.3 %collective-permute-start.2 = (f32[2,128]{1,0:T(2,128)S(1)}, f32[2,128]{1,0:T(2,128)S(1)}, u32[]{:S(2)}, u32[]{:S(2)}) collective-permute-start(f32[2,128]{1,0:T(2,128)S(1)} %get-tuple-element.15), channel_id=1, source_target_pairs={{64,0},{128,64},{192,128},{65,1},{129,65},{193,129},{66,2},{130,66... | collective-permute-start | bytes 3080 | tf_op jit(solution)/shard_map/ppermute | solution.py:264
  51.7 1.9 %collective-permute-done.4 = f32[2,128]{1,0:T(2,128)S(1)} collective-permute-done((f32[2,128]{1,0:T(2,128)S(1)}, f32[2,128]{1,0:T(2,128)S(1)}, u32[]{:S(2)}, u32[]{:S(2)}) %collective-permute-start.4) | collective-permute-done | bytes 1056 | tf_op jit(solution)/shard_map/ppermute | solution.py:264
  53.6 1.6 %collective-permute-done.3 = f32[2,128]{1,0:T(2,128)S(1)} collective-permute-done((f32[2,128]{1,0:T(2,128)S(1)}, f32[2,128]{1,0:T(2,128)S(1)}, u32[]{:S(2)}, u32[]{:S(2)}) %collective-permute-start.3) | collective-permute-done | bytes 1056 | tf_op jit(solution)/shard_map/ppermute | solution.py:264
  55.2 0.0 collective-permute-done.2
  55.2 0.6 multiply_add_fusion
  55.8 7.1 %all-to-all-done = f32[256,1,256]{2,1,0:T(1,128)S(1)} async-done(((f32[256,1,256]{2,1,0:T(1,128)}), f32[256,1,256]{2,1,0:T(1,128)S(1)}, u32[]{:S(2)}, u32[]{:S(2)}) %all-to-all-start) | async-done | bytes 262176 | tf_op jit(solution)/shard_map/all_to_all | solution.py:277
  62.9 0.3 reduce_sum.9
  63.2 0.5 fusion
  (9 shorter events, 0.0 us)
Async XLA Ops:
  0.6 8.5 %copy-start.6 = (s32[32512]{0:T(1024)S(1)}, s32[32512]{0:T(1024)}, u32[]{:S(2)}) copy-start(s32[32512]{0:T(1024)} %param.12) | copy-start | bytes 390148
  2.2 16.4 %collective-permute-start = (f32[12,512]{1,0:T(8,128)S(1)}, f32[12,512]{1,0:T(8,128)S(1)}, u32[]{:S(2)}, u32[]{:S(2)}) collective-permute-start(f32[12,512]{1,0:T(8,128)S(1)} %pad_maximum_fusion), channel_id=1, source_target_pairs={{0,1},{1,2},{2,3},{3,4},{4,5},{5,6},{6,7},{7,8},{8,9},{9,10},{10,1... | collective-permute-start | bytes 73736 | tf_op jit(solution)/shard_map/ppermute | solution.py:264
  7.2 11.5 %collective-permute-start.1 = (f32[12,512]{1,0:T(8,128)S(1)}, f32[12,512]{1,0:T(8,128)S(1)}, u32[]{:S(2)}, u32[]{:S(2)}) collective-permute-start(f32[12,512]{1,0:T(8,128)S(1)} %pad_maximum_fusion.1), channel_id=1, source_target_pairs={{1,0},{2,1},{3,2},{4,3},{5,4},{6,5},{7,6},{8,7},{9,8},{10,9},{11,1... | collective-permute-start | bytes 73736 | tf_op jit(solution)/shard_map/ppermute | solution.py:264
  9.1 0.9 %copy-start.7 = (s32[1,64,512]{2,1,0:T(8,128)S(1)}, s32[1,64,512]{2,1,0:T(8,128)}, u32[]{:S(2)}) copy-start(s32[1,64,512]{2,1,0:T(8,128)} %param.11) | copy-start | bytes 393220
  10.0 8.6 %copy-start = (f32[1,64,512]{2,1,0:T(8,128)S(1)}, f32[1,64,512]{2,1,0:T(8,128)}, u32[]{:S(2)}) copy-start(f32[1,64,512]{2,1,0:T(8,128)} %param.8) | copy-start | bytes 393220
  10.0 8.6 %copy-start.1 = (f32[1,64,512]{2,1,0:T(8,128)S(1)}, f32[1,64,512]{2,1,0:T(8,128)}, u32[]{:S(2)}) copy-start(f32[1,64,512]{2,1,0:T(8,128)} %param.9) | copy-start | bytes 393220
  10.0 8.6 %copy-start.2 = (f32[1,64,512]{2,1,0:T(8,128)S(1)}, f32[1,64,512]{2,1,0:T(8,128)}, u32[]{:S(2)}) copy-start(f32[1,64,512]{2,1,0:T(8,128)} %param.10) | copy-start | bytes 393220
  31.3 15.6 %copy-start.3 = (s32[32,128]{1,0:T(8,128)S(1)}, s32[32,128]{1,0:T(8,128)}, u32[]{:S(2)}) copy-start(s32[32,128]{1,0:T(8,128)} %cell_ref.1) | copy-start | bytes 49156
  31.3 15.6 %copy-start.4 = (f32[32,128]{1,0:T(8,128)S(1)}, f32[32,128]{1,0:T(8,128)}, u32[]{:S(2)}) copy-start(f32[32,128]{1,0:T(8,128)} %keep_ref.1) | copy-start | bytes 49156
  31.3 15.6 %copy-start.5 = (f32[32,128]{1,0:T(8,128)S(1)}, f32[32,128]{1,0:T(8,128)}, u32[]{:S(2)}) copy-start(f32[32,128]{1,0:T(8,128)} %forcing_ref.1) | copy-start | bytes 49156
  31.3 31.6 %all-to-all-start = ((f32[256,1,256]{2,1,0:T(1,128)}), f32[256,1,256]{2,1,0:T(1,128)S(1)}, u32[]{:S(2)}, u32[]{:S(2)}) async-start(f32[256,1,256]{2,1,0:T(1,128)} %copy.11), calls=%async_computation | async-start | bytes 524288 | tf_op jit(solution)/shard_map/all_to_all | solution.py:277
  47.8 5.8 %collective-permute-start.4 = (f32[2,128]{1,0:T(2,128)S(1)}, f32[2,128]{1,0:T(2,128)S(1)}, u32[]{:S(2)}, u32[]{:S(2)}) collective-permute-start(f32[2,128]{1,0:T(2,128)S(1)} %get-tuple-element.15), channel_id=1, source_target_pairs={{192,0},{193,1},{194,2},{195,3},{196,4},{197,5},{198,6},{199,7},{2... | collective-permute-start | bytes 3080 | tf_op jit(solution)/shard_map/ppermute | solution.py:264
  49.1 6.1 %collective-permute-start.3 = (f32[2,128]{1,0:T(2,128)S(1)}, f32[2,128]{1,0:T(2,128)S(1)}, u32[]{:S(2)}, u32[]{:S(2)}) collective-permute-start(f32[2,128]{1,0:T(2,128)S(1)} %get-tuple-element.15), channel_id=1, source_target_pairs={{128,0},{192,64},{129,1},{193,65},{130,2},{194,66},{131,3},{195,67... | collective-permute-start | bytes 3080 | tf_op jit(solution)/shard_map/ppermute | solution.py:264
  50.4 4.8 %collective-permute-start.2 = (f32[2,128]{1,0:T(2,128)S(1)}, f32[2,128]{1,0:T(2,128)S(1)}, u32[]{:S(2)}, u32[]{:S(2)}) collective-permute-start(f32[2,128]{1,0:T(2,128)S(1)} %get-tuple-element.15), channel_id=1, source_target_pairs={{64,0},{128,64},{192,128},{65,1},{129,65},{193,129},{66,2},{130,66... | collective-permute-start | bytes 3080 | tf_op jit(solution)/shard_map/ppermute | solution.py:264
where the time goes:
time: 64.2 us; the launch traced here: 63.7 us
  starting transfers between devices  26.3 us (41%)
  Pallas kernels  21.1 us (33%)
  waiting for transfers between devices  10.6 us (17%)
  local copies, waits for them, and re-layouts  3.98 us (6%)
  other arithmetic  0.93 us (1%)
  between operations  0.81 us (1%)
    all_to_all x1, starting transfers between devices, per_device(): arrived = lax.all_to_all(partials, ('basin', 'tile'), 0, 0, tiled=True)  15.6 us
    ppermute x5, starting transfers between devices, moved(): return lax.ppermute(value, axis, pairs)  10.7 us
    pallas_call x1, Pallas kernels, zone_partials(): pl.pallas_call(zone_kernel, out_shape=jax.ShapeDtypeStruct((256, 2 * LANE...  10.3 us
    pallas_call x1, Pallas kernels, slots_of(): pl.pallas_call(slot_kernel, out_shape=(shape, shape), in_specs=[VMEM, VME...  8.59 us
    all_to_all x1, waiting for transfers between devices, per_device(): arrived = lax.all_to_all(partials, ('basin', 'tile'), 0, 0, tiled=True)  7.07 us
    ppermute x5, waiting for transfers between devices, moved(): return lax.ppermute(value, axis, pairs)  3.53 us
    slice x2, local copies, waits for them, and re-layouts, per_device(): x[:HALO]  1.55 us
    pallas_call x1, Pallas kernels, window(): pl.pallas_call(window_kernel, out_shape=(shape, shape), in_specs=[VMEM] *...  1.3 us
  transfers between devices with their start and end apart: 6, of which 3 were waited for; matrix products, arithmetic and copies ran while one was open for 1% of the time, Pallas kernels for 15%

commit v1 on v0

--- a/solution.py
+++ b/solution.py
@@ -41,48 +41,155 @@
     return [jnp.where(hit, w[None], zero).reshape(count, width) for w in weights]
 
 
-def slot_kernel(owner_ref, label_ref, device_ref, lane_ref, table_ref, turned_ref):
-    table_ref[...] = jnp.zeros(table_ref.shape, jnp.float32)
+def stacked(x):
+    return jnp.concatenate(
+        [x[:, start : start + LANES] for start in range(0, x.shape[1], LANES)], axis=0
+    )
+
+
+def from_below(x, distance):
+    return pltpu.roll(x, x.shape[0] - distance, 0)
+
+
+def front_kernel(depth_ref, rough_ref_, seed_ref, low_ref, high_ref):
+    for part, ref in enumerate((depth_ref, rough_ref_, seed_ref)):
+        rows = slice(part * HALO, (part + 1) * HALO)
+        low_ref[rows, :] = ref[ref.shape[0] - HALO :, :]
+        high_ref[rows, :] = ref[0:HALO, :]
+
+
+def edges_to_send(depth, rough, seed):
+    shape = jax.ShapeDtypeStruct((3 * HALO, depth.shape[1]), jnp.float32)
+    return pl.pallas_call(
+        front_kernel,
+        out_shape=(shape, shape),
+        in_specs=[VMEM] * 3,
+        out_specs=(VMEM, VMEM),
+        compiler_params=ROOMY,
+        name="edge_rows",
+    )(depth, rough, seed)
+
+
+ABSENT = 2**15 - 1
+CHUNK = 16
+
+
+def slot_kernel(
+    place_ref,
+    owner_ref,
+    label_ref,
+    moves_ref,
+    device_ref,
+    lane_ref,
+    home_ref,
+    chunks_ref,
+    table_ref,
+    turned_ref,
+    packed_ref,
+):
+    first_zone = place_ref[0]
+    first_device = place_ref[1].astype(jnp.float32)
+    table_ref[...] = jnp.full(table_ref.shape, 256.0 * SPAN, jnp.float32)
     table_ref[0 : owner_ref.shape[0], :] = owner_ref[...].astype(jnp.float32)
-    slots = jnp.transpose(table_ref[...])
-    owners = jnp.floor((slots + 0.5) * (1.0 / SPAN))
+
+    def placed(slots):
+        owners = jnp.floor((slots + 0.5) * (1.0 / SPAN))
+        lanes = slots - owners * SPAN
+        turned = owners - first_device
+        turned = jnp.where(turned < 0, turned + 256.0, turned)
+        return jnp.where(owners < 256.0, turned, 256.0), lanes
+
+    owners, lanes = placed(jnp.transpose(table_ref[...]))
     turned_ref[0:LANES, :] = owners.astype(jnp.bfloat16)
-    turned_ref[LANES : 2 * LANES, :] = (slots - owners * SPAN).astype(jnp.bfloat16)
-
-    def one_row(row, carry):
-        label = label_ref[pl.ds(row, 1), :]
-        width = label.shape[1]
-        group = one_hot(spread_rows((label // LANES).astype(jnp.float32)), 256)
-        found = jnp.dot(turned_ref[...], group, preferred_element_type=jnp.float32)
-        hit = (label % LANES) == lax.broadcasted_iota(jnp.int32, (LANES, width), 0)
-        device_ref[pl.ds(row, 1), :] = jnp.sum(
-            jnp.where(hit, found[:LANES], 0.0), axis=0, keepdims=True
-        )
-        lane_ref[pl.ds(row, 1), :] = jnp.sum(
-            jnp.where(hit, found[LANES:], 0.0), axis=0, keepdims=True
-        )
+    turned_ref[LANES : 2 * LANES, :] = lanes.astype(jnp.bfloat16)
+
+    home_row = first_zone // LANES
+    shift = first_zone % LANES
+    back = jnp.where(shift == 0, 0, LANES - shift)
+    pair = table_ref[pl.ds(home_row, 1), :], table_ref[pl.ds(home_row + 1, 1), :]
+    pair = [pltpu.roll(jnp.broadcast_to(row, (8, LANES)), back, 1) for row in pair]
+    spot = lax.broadcasted_iota(jnp.int32, (8, LANES), 1)
+    home = jnp.where(spot + shift < LANES, pair[0], pair[1])
+    home_device, home_lane = placed(jnp.where(spot < SPAN, home, 256.0 * SPAN))
+    top = lax.broadcasted_iota(jnp.int32, (8, LANES), 0) == 0
+    home_ref[...] = jnp.where(top, home_device, home_lane)
+
+    label = stacked(label_ref[...])
+    count = label.shape[0]
+    offset = label - first_zone
+    at_home = (offset >= 0) & (offset < SPAN)
+    at_home_count = jnp.where(at_home, 1.0, 0.0)
+    row_ids = lax.broadcasted_iota(jnp.int32, (count, count), 0)
+    column_ids = lax.broadcasted_iota(jnp.int32, (count, count), 1)
+    earlier = jnp.where(column_ids < row_ids, 1.0, 0.0).astype(jnp.bfloat16)
+    gaps = jnp.dot(
+        earlier, at_home_count.astype(jnp.bfloat16), preferred_element_type=jnp.float32
+    ).astype(jnp.int32)
+    packed = jnp.where(at_home, ABSENT, gaps * (ABSENT + 1) + label)
+    moves = jnp.zeros(packed.shape, jnp.int32)
+    bit = 0
+    while 2**bit < count:
+        marker = (ABSENT + 1) * 2**bit
+        near = from_below(packed, 2**bit)
+        taken = (near & marker) != 0
+        left = (packed & marker) != 0
+        packed = jnp.where(taken, near, jnp.where(left, ABSENT, packed))
+        moves = jnp.where(taken, moves + 2**bit, moves)
+        bit += 1
+    moves_ref[...] = moves
+    packed_ref[...] = packed & ABSENT
+    most = count - jnp.min(jnp.sum(at_home_count, axis=0, keepdims=True)).astype(jnp.int32)
+    chunks = (most + CHUNK - 1) // CHUNK
+    chunks_ref[0] = chunks
+
+    def one_chunk(index, carry):
+        for quarter in range(CHUNK // 4):
+            start = index * CHUNK + quarter * 4
+            group_label = jnp.concatenate(
+                [packed_ref[pl.ds(start + i, 1), :] for i in range(4)], axis=1
+            )
+            width = group_label.shape[1]
+            group = one_hot(spread_rows((group_label >> 7).astype(jnp.float32)), 256)
+            found = jnp.dot(turned_ref[...], group, preferred_element_type=jnp.float32)
+            hit = (group_label & 127) == lax.broadcasted_iota(jnp.int32, (LANES, width), 0)
+            for half, ref in enumerate((device_ref, lane_ref)):
+                part = found[half * LANES : (half + 1) * LANES]
+                part = jnp.sum(jnp.where(hit, part, 0.0), axis=0, keepdims=True)
+                for i in range(4):
+                    ref[pl.ds(start + i, 1), :] = part[:, i * LANES : (i + 1) * LANES]
         return carry
 
-    lax.fori_loop(0, label_ref.shape[0], one_row, 0, unroll=4)
-
-
-def slots_of(owner_slot, label):
-    shape = jax.ShapeDtypeStruct(label.shape, jnp.float32)
+    lax.fori_loop(0, chunks, one_chunk, 0)
+
+
+SMEM = pl.BlockSpec(memory_space=pltpu.SMEM)
+
+
+def slots_of(place, owner_slot, label):
+    count = label.size // LANES
+    stack = jax.ShapeDtypeStruct((count, LANES), jnp.float32)
     return pl.pallas_call(
         slot_kernel,
-        out_shape=(shape, shape),
-        in_specs=[VMEM, VMEM],
-        out_specs=(VMEM, VMEM),
+        out_shape=(
+            jax.ShapeDtypeStruct((count, LANES), jnp.int32),
+            stack,
+            stack,
+            jax.ShapeDtypeStruct((8, LANES), jnp.float32),
+            jax.ShapeDtypeStruct((1,), jnp.int32),
+        ),
+        in_specs=[SMEM, VMEM, VMEM],
+        out_specs=(VMEM, VMEM, VMEM, VMEM, SMEM),
         scratch_shapes=[
             pltpu.VMEM((256, LANES), jnp.float32),
             pltpu.VMEM((256, 256), jnp.bfloat16),
+            pltpu.VMEM((count, LANES), jnp.int32),
         ],
         compiler_params=ROOMY,
         cost_estimate=pl.CostEstimate(
-            flops=2 * 256 * 256 * label.size, bytes_accessed=16 * label.size, transcendentals=0
+            flops=2 * 256 * 256 * label.size // 4, bytes_accessed=16 * label.size, transcendentals=0
         ),
         name="slot_lookup",
-    )(owner_slot.reshape(-1, LANES), label)
+    )(place, owner_slot.reshape(-1, LANES), label)
 
 
 def below(x):
@@ -166,53 +273,178 @@
     return upper, x - upper
 
 
-ZONE_ROWS = 8
-
-
-def zone_kernel(grad_ref, device_ref, lane_ref, out_ref):
-    out_ref[...] = jnp.zeros(out_ref.shape, jnp.float32)
-
-    def some_rows(index, carry):
+HOME_ROWS = 8
+
+
+def zone_sums(device_rows, lane_rows, grad_rows, square_rows):
+    left = []
+    right = []
+    for device, lane, grad, square in zip(device_rows, lane_rows, grad_rows, square_rows):
+        left.append(one_hot(spread_rows(device), 256))
+        weights = [spread_rows(part) for part in halves(grad) + halves(square)]
+        right.append(jnp.concatenate(one_hot(spread_rows(lane), LANES, weights), axis=0))
+    both = lax.dot_general(
+        jnp.concatenate(left, axis=1),
+        jnp.concatenate(right, axis=1),
+        (((1,), (1,)), ((), ())),
+        preferred_element_type=jnp.float32,
+    )
+    return jnp.concatenate(
+        [
+            both[:, 0:LANES] + both[:, LANES : 2 * LANES],
+            both[:, 2 * LANES : 3 * LANES] + both[:, 3 * LANES :],
+        ],
+        axis=1,
+    )
+
+
+def home_products(label_row, grad_row):
+    width = label_row.shape[1]
+    group = jnp.broadcast_to((label_row >> 3).astype(jnp.float32), (16, width))
+    within = jnp.broadcast_to((label_row & 7).astype(jnp.float32), (16, width))
+    ids = lax.broadcasted_iota(jnp.int32, (16, width), 0)
+    zero = jnp.zeros((), jnp.bfloat16)
+    group_hit = group.astype(jnp.bfloat16) == ids.astype(jnp.float32).astype(jnp.bfloat16)
+    left = jnp.where(group_hit, jnp.ones((), jnp.bfloat16), zero)
+    within_hit = within.astype(jnp.bfloat16) == (ids & 7).astype(jnp.float32).astype(jnp.bfloat16)
+    right = []
+    for value in (grad_row, grad_row * grad_row):
+        pair = [jnp.broadcast_to(part, (8, width)) for part in halves(value)]
+        weights = jnp.concatenate(pair, axis=0).astype(jnp.bfloat16)
+        right.append(jnp.where(within_hit, weights, zero))
+    return left, jnp.concatenate(right, axis=0)
+
+
+def zone_kernel(
+    place_ref,
+    chunks_ref,
+    grad_ref,
+    label_ref,
+    moves_ref,
+    device_ref,
+    lane_ref,
+    home_ref,
+    edge_ref,
+    own_ref,
+    first_ref,
+    second_ref,
+    third_ref,
+    total_ref,
+    stray_ref,
+    offset_ref,
+):
+    offset_ref[...] = label_ref[...] - place_ref[0]
+    grad = stacked(grad_ref[...])
+    moves = moves_ref[...]
+    bit = 0
+    while 2**bit < grad.shape[0]:
+        grad = jnp.where((moves & 2**bit) != 0, from_below(grad, 2**bit), grad)
+        bit += 1
+    stray_ref[...] = grad
+
+    def home_rows(index, total):
         left = []
         right = []
-        for offset in range(ZONE_ROWS):
-            row = pl.ds(index * ZONE_ROWS + offset, 1)
-            grad = grad_ref[row, :]
-            left.append(one_hot(spread_rows(device_ref[row, :]), 256))
-            weights = [spread_rows(part) for part in halves(grad) + halves(grad * grad)]
-            right.append(
-                jnp.concatenate(one_hot(spread_rows(lane_ref[row, :]), LANES, weights), axis=0)
-            )
-        both = lax.dot_general(
+        for step in range(HOME_ROWS):
+            row = pl.ds(index * HOME_ROWS + step, 1)
+            one_left, one_right = home_products(offset_ref[row, :], grad_ref[row, :])
+            left.append(one_left)
+            right.append(one_right)
+        return total + lax.dot_general(
             jnp.concatenate(left, axis=1),
             jnp.concatenate(right, axis=1),
             (((1,), (1,)), ((), ())),
             preferred_element_type=jnp.float32,
         )
-        out_ref[...] += jnp.concatenate(
-            [
-                both[:, 0:LANES] + both[:, LANES : 2 * LANES],
-                both[:, 2 * LANES : 3 * LANES] + both[:, 3 * LANES :],
-            ],
-            axis=1,
+
+    home = lax.fori_loop(
+        0,
+        grad_ref.shape[0] // HOME_ROWS,
+        home_rows,
+        jnp.zeros((16, 32), jnp.float32),
+        unroll=True,
+    )
+    part = lax.broadcasted_iota(jnp.int32, (32, 2 * LANES), 0)
+    zone = lax.broadcasted_iota(jnp.int32, (32, 2 * LANES), 1)
+    chosen = ((part & 7) == (zone & 7)) & ((part >= 16) == (zone >= LANES))
+    home = jnp.dot(
+        home,
+        jnp.where(chosen, 1.0, 0.0),
+        precision=lax.Precision.HIGHEST,
+        preferred_element_type=jnp.float32,
+    )
+    group = lax.broadcasted_iota(jnp.int32, (16, 2 * LANES), 0)
+    zone = lax.broadcasted_iota(jnp.int32, (16, 2 * LANES), 1)
+    home = jnp.sum(jnp.where(((zone >> 3) & 15) == group, home, 0.0), axis=0, keepdims=True)
+    total_ref[...] = zone_sums(
+        [home_ref[0:1, :]], [home_ref[1:2, :]], [home[:, :LANES]], [home[:, LANES:]]
+    )
+
+    def one_chunk(index, carry):
+        rows = [pl.ds(index * CHUNK + step, 1) for step in range(CHUNK)]
+        grads = [stray_ref[row, :] for row in rows]
+        total_ref[...] += zone_sums(
+            [device_ref[row, :] for row in rows],
+            [lane_ref[row, :] for row in rows],
+            grads,
+            [grad * grad for grad in grads],
         )
         return carry
 
-    lax.fori_loop(0, grad_ref.shape[0] // ZONE_ROWS, some_rows, 0)
-
-
-def zone_partials(grad, device, lane):
+    lax.fori_loop(0, chunks_ref[0], one_chunk, 0)
+    tiles = own_ref.shape[0]
+    own_ref[...] = total_ref[0:tiles, :]
+    edge = jnp.broadcast_to(
+        jnp.concatenate([edge_ref[0:1, :], edge_ref[1:2, :]], axis=1), (8, 2 * LANES)
+    )
+    for step, ref in enumerate((first_ref, second_ref, third_ref), 1):
+        ref[0:tiles, :] = total_ref[step * tiles : (step + 1) * tiles, :]
+        ref[tiles : tiles + 8, :] = edge
+
+
+def zone_partials(place, chunks, grad, label, moves, device, lane, home, edge):
+    sent = jax.ShapeDtypeStruct((72, 2 * LANES), jnp.float32)
     return pl.pallas_call(
         zone_kernel,
-        out_shape=jax.ShapeDtypeStruct((256, 2 * LANES), jnp.float32),
-        in_specs=[VMEM] * 3,
-        out_specs=VMEM,
+        out_shape=(jax.ShapeDtypeStruct((64, 2 * LANES), jnp.float32), sent, sent, sent),
+        in_specs=[SMEM, SMEM] + [VMEM] * 7,
+        out_specs=(VMEM,) * 4,
+        scratch_shapes=[
+            pltpu.VMEM((256, 2 * LANES), jnp.float32),
+            pltpu.VMEM((grad.size // LANES, LANES), jnp.float32),
+            pltpu.VMEM(grad.shape, jnp.int32),
+        ],
         compiler_params=ROOMY,
-        cost_estimate=pl.CostEstimate(
-            flops=2 * 256 * 512 * grad.size, bytes_accessed=12 * grad.size, transcendentals=0
+        name="zone_partials",
+    )(place, chunks, grad, label, moves, device, lane, home, edge)
+
+
+def arrival_kernel(place_ref, own_ref, first_ref, second_ref, third_ref, sums_ref, incoming_ref):
+    tiles = own_ref.shape[0]
+    sums = own_ref[...] + first_ref[0:tiles, :]
+    sums = sums + (second_ref[0:tiles, :] + third_ref[0:tiles, :])
+    sums_ref[...] = sums.reshape(sums_ref.shape)
+    basin = place_ref[1] // tiles
+    incoming = jnp.zeros((8, LANES), jnp.float32)
+    for hop, ref in ((3, first_ref), (2, second_ref), (1, third_ref)):
+        edge = ref[tiles : tiles + 8, :]
+        there = jnp.where(basin + hop < 4, 1.0, 0.0)
+        incoming = there * (edge[:, :LANES] * incoming + edge[:, LANES:])
+    incoming_ref[...] = incoming
+
+
+def arrivals(place, own, *others):
+    return pl.pallas_call(
+        arrival_kernel,
+        out_shape=(
+            jax.ShapeDtypeStruct((own.shape[0], 1, own.shape[1]), jnp.float32),
+            jax.ShapeDtypeStruct((8, LANES), jnp.float32),
         ),
-        name="zone_partials",
-    )(grad, device, lane)
+        in_specs=[SMEM] + [VMEM] * 4,
+        out_specs=(VMEM, VMEM),
+        compiler_params=ROOMY,
+        name="arrivals",
+    )(place, own, *others)
 
 
 def reach_kernel(adjoint_ref, cell_ref, keep_ref, forcing_ref, rate_ref, push_ref, edge_ref):
@@ -224,14 +456,14 @@
     values = []
     for reach in range(0, reaches, 4):
         cells = jnp.concatenate([cell_ref[reach + i : reach + i + 1, :] for i in range(4)], axis=1)
-        column = (cells % columns).astype(jnp.float32)
+        column = (cells & (columns - 1)).astype(jnp.float32)
         hot = jnp.concatenate(
             [one_hot(spread_rows(column - part * 256.0), 256) for part in range(columns // 256)],
             axis=0,
         )
         picked = jnp.dot(table, hot, preferred_element_type=jnp.float32)
         picked = picked[:rows] + picked[rows:]
-        row_hit = (cells // columns) == lax.broadcasted_iota(jnp.int32, (rows, 4 * width), 0)
+        row_hit = (cells >> 9) == lax.broadcasted_iota(jnp.int32, (rows, 4 * width), 0)
         found = jnp.sum(jnp.where(row_hit, picked, 0.0), axis=0, keepdims=True)
         values += [found[:, i * width : (i + 1) * width] for i in range(4)]
     rate = jnp.ones((1, width), jnp.float32)
@@ -264,24 +496,31 @@
     return lax.ppermute(value, axis, pairs)
 
 
+def turned(value, axis, steps):
+    count = lax.axis_size(axis)
+    return lax.ppermute(value, axis, [(i, (i + steps) % count) for i in range(count)])
+
+
 def per_device(
     depth_start, roughness, depth_seed, zone_label, owner_slot, retention, forcing, levee_cell
 ):
     depth, rough, seed, label = depth_start[0], roughness[0], depth_seed[0], zone_label[0]
-    rows = depth.shape[0]
-    low = moved(jnp.concatenate([x[rows - HALO :] for x in (depth, rough, seed)]), "tile", 1)
-    high = moved(jnp.concatenate([x[:HALO] for x in (depth, rough, seed)]), "tile", -1)
-    device, lane = slots_of(owner_slot, label)
+    tiles = lax.axis_size("tile")
+    first_device = lax.axis_index("basin") * tiles
+    place = jnp.stack([(first_device + lax.axis_index("tile")) * SPAN, first_device])
+    place = place.astype(jnp.int32)
+    to_next, to_last = edges_to_send(depth, rough, seed)
+    low = moved(to_next, "tile", 1)
+    high = moved(to_last, "tile", -1)
+    moves, device, lane, home, chunks = slots_of(place, owner_slot, label)
     grad, adjoint = window(depth, rough, seed, low, high)
-    partials = zone_partials(grad, device, lane)
-    arrived = lax.all_to_all(partials, ("basin", "tile"), 0, 0, tiled=True)
     rate, push, edge = reach_maps(adjoint, levee_cell, retention, forcing)
-    incoming = jnp.zeros((edge.shape[1],), jnp.float32)
-    edges = [moved(edge, "basin", -hop) for hop in range(1, lax.axis_size("basin"))]
-    for from_below in reversed(edges):
-        incoming = from_below[0] * incoming + from_below[1]
-    reach_adjoint = rate * incoming[None, :] + push
-    sums = jnp.sum(arrived, axis=0)
+    own, *others = zone_partials(place, chunks, grad, label, moves, device, lane, home, edge)
+    others = [turned(part, "basin", step) for step, part in enumerate(others, 1)]
+    sums, incoming = arrivals(place, own, *others)
+    arrived = lax.all_to_all(sums, "tile", 0, 0, tiled=True)
+    reach_adjoint = rate * incoming[:1] + push
+    sums = jnp.sum(arrived, axis=(0, 1))
     return (sums[:SPAN], sums[LANES : LANES + SPAN], reach_adjoint)
 
 

time: 64.2 us -> 55.2 us (0.86); the launches traced: 63.7 us -> 55.4 us
  Pallas kernels: 21.1 us -> 11.6 us
  starting transfers between devices: 26.3 us -> 27.5 us
  waiting for transfers between devices: 10.6 us -> 11.4 us
  local copies, waits for them, and re-layouts: 3.98 us -> 3.27 us
    pallas_call x2 -> x4, Pallas kernels: 18.9 us -> 9.5 us  [the longest x1 5.13 us: zone_partials(): pl.pallas_call(zone_kernel, out_shape=(jax.ShapeDtypeStruct((64, 2 * LANE...]
    ppermute x0 -> x3, starting transfers between devices: none -> 4.89 us  [turned(): lax.ppermute(value, axis, [(i, (i + steps) % count) for i in range(count)])]
    ppermute x5 -> x2, starting transfers between devices: 10.7 us -> 6.99 us  [moved(): return lax.ppermute(value, axis, pairs)]
    ppermute x5 -> x2, waiting for transfers between devices: 3.53 us -> 0.01 us  [moved(): return lax.ppermute(value, axis, pairs)]
    ppermute x0 -> x3, waiting for transfers between devices: none -> 2.25 us  [turned(): lax.ppermute(value, axis, [(i, (i + steps) % count) for i in range(count)])]
    all_to_all x1, waiting for transfers between devices: 7.07 us -> 9.18 us  [per_device(): arrived = lax.all_to_all(sums, 'tile', 0, 0, tiled=True)]
    unnamed x16 -> x22, local copies, waits for them, and re-layouts: 0.93 us -> 2.75 us
    slice x2 -> x0, local copies, waits for them, and re-layouts: 1.55 us -> none  [per_device(): x[:HALO]]
  transfers between devices with their start and end apart: 6 -> 6, of which waited for: 3 -> 3; matrix products, arithmetic and copies ran while one was open for 1% -> 1% of each run, Pallas kernels for 15% -> 6%
where the time goes in v1:
time: 55.2 us; the launch traced here: 55.4 us
  starting transfers between devices  27.5 us (50%)
  Pallas kernels  11.6 us (21%)
  waiting for transfers between devices  11.4 us (21%)
  local copies, waits for them, and re-layouts  3.27 us (6%)
  between operations  0.81 us (1%)
  other arithmetic  0.78 us (1%)
    all_to_all x1, starting transfers between devices, per_device(): arrived = lax.all_to_all(sums, 'tile', 0, 0, tiled=True)  15.7 us
    all_to_all x1, waiting for transfers between devices, per_device(): arrived = lax.all_to_all(sums, 'tile', 0, 0, tiled=True)  9.18 us
    ppermute x2, starting transfers between devices, moved(): return lax.ppermute(value, axis, pairs)  6.99 us
    pallas_call x1, Pallas kernels, zone_partials(): pl.pallas_call(zone_kernel, out_shape=(jax.ShapeDtypeStruct((64, 2 * LANE...  5.13 us
    ppermute x3, starting transfers between devices, turned(): lax.ppermute(value, axis, [(i, (i + steps) % count) for i in range(count)])  4.89 us
    pallas_call x1, Pallas kernels, slots_of(): pl.pallas_call(slot_kernel, out_shape=(jax.ShapeDtypeStruct((count, LANES...  3.16 us
    unnamed x22, local copies, waits for them, and re-layouts  2.75 us
    ppermute x3, waiting for transfers between devices, turned(): lax.ppermute(value, axis, [(i, (i + steps) % count) for i in range(count)])  2.25 us
  transfers between devices with their start and end apart: 6, of which 3 were waited for; matrix products, arithmetic and copies ran while one was open for 1% of the time, Pallas kernels for 6%

profile of v1, /device:TPU:1, one launch (start us, length us, event | category | flops | bytes accessed | tf_op | source)
XLA Modules:
  0.0 55.4 jit_solution(6043291534593962530)
XLA Ops:
  0.6 0.0 copy-start
  0.6 0.9 %copy-done = f32[1,64,512]{2,1,0:T(8,128)S(1)} copy-done((f32[1,64,512]{2,1,0:T(8,128)S(1)}, f32[1,64,512]{2,1,0:T(8,128)}, u32[]{:S(2)}) %copy-start) | copy-done | bytes 131096
  1.5 0.9 %copy-done.2 = f32[1,64,512]{2,1,0:T(8,128)S(1)} copy-done((f32[1,64,512]{2,1,0:T(8,128)S(1)}, f32[1,64,512]{2,1,0:T(8,128)}, u32[]{:S(2)}) %copy-start.2) | copy-done | bytes 131096
  2.4 0.9 %copy-done.4 = f32[1,64,512]{2,1,0:T(8,128)S(1)} copy-done((f32[1,64,512]{2,1,0:T(8,128)S(1)}, f32[1,64,512]{2,1,0:T(8,128)}, u32[]{:S(2)}) %copy-start.4) | copy-done | bytes 131096
  3.4 5.1 %collective-permute-start = (f32[12,512]{1,0:T(8,128)S(1)}, f32[12,512]{1,0:T(8,128)S(1)}, u32[]{:S(2)}, u32[]{:S(2)}) collective-permute-start(f32[12,512]{1,0:T(8,128)S(1)} %get-tuple-element.22), channel_id=1, source_target_pairs={{0,1},{1,2},{2,3},{3,4},{4,5},{5,6},{6,7},{7,8},{8,9},{9,10},{10,1... | collective-permute-start | bytes 73736 | tf_op jit(solution)/shard_map/ppermute | solution.py:496
  8.4 1.9 %collective-permute-start.1 = (f32[12,512]{1,0:T(8,128)S(1)}, f32[12,512]{1,0:T(8,128)S(1)}, u32[]{:S(2)}, u32[]{:S(2)}) collective-permute-start(f32[12,512]{1,0:T(8,128)S(1)} %get-tuple-element.23), channel_id=1, source_target_pairs={{1,0},{2,1},{3,2},{4,3},{5,4},{6,5},{7,6},{8,7},{9,8},{10,9},{11,1... | collective-permute-start | bytes 73736 | tf_op jit(solution)/shard_map/ppermute | solution.py:496
  10.4 0.1 pad_add_fusion.place_ref
  10.5 0.0 copy-done.6
  10.5 0.0 copy-done.10
  10.5 0.0 copy-start.5
  10.5 3.2 %slot_lookup.1 = (s32[256,128]{1,0:T(8,128)S(1)}, f32[256,128]{1,0:T(8,128)S(1)}, f32[256,128]{1,0:T(8,128)S(1)}, f32[8,128]{1,0:T(8,128)S(1)}, s32[1]{0:T(128)}) custom-call(s32[2]{0:T(128)S(1)} %pad_add_fusion.place_ref, s32[254,128]{1,0:T(8,128)S(1)} %bitcast.17, s32[64,512]{1,0:T(8,128)S(1)} %bitcast.15), custom_call_target="tpu_custom_call" | custom-call | flops 1073741824 | bytes 524288 | tf_op jit(solution)/shard_map/slot_lookup/pallas_call | solution.py:171
  13.6 0.0 copy-start.7
  13.7 0.0 copy-start.8
  13.7 0.0 copy-start.9
  13.7 0.0 collective-permute-done.low_ref
  13.7 0.0 collective-permute-done.1.high_ref
  13.7 0.0 copy-done.1
  13.7 1.3 %adjoint_window.1 = (f32[64,512]{1,0:T(8,128)S(1)}, f32[64,512]{1,0:T(8,128)S(1)}) custom-call(f32[64,512]{1,0:T(8,128)S(1)} %bitcast.10, f32[64,512]{1,0:T(8,128)S(1)} %bitcast.12, f32[64,512]{1,0:T(8,128)S(1)} %bitcast.14, f32[12,512]{1,0:T(8,128)S(1)} %collective-permute-done.low_ref, f32[12,512]{1,0:T(8,128)S(1)} %collective-permute-done.1.high_ref), custom_call_target="tpu_custom_call" | custom-call | tf_op jit(solution)/shard_map/adjoint_window/pallas_call | solution.py:261
  15.1 0.8 %reach_maps.1 = (f32[32,128]{1,0:T(8,128)S(1)}, f32[32,128]{1,0:T(8,128)S(1)}, f32[2,128]{1,0:T(2,128)S(1)}) custom-call(f32[64,512]{1,0:T(8,128)S(1)} %get-tuple-element.29.adjoint_ref, s32[32,128]{1,0:T(8,128)S(1)} %copy-done.7, f32[32,128]{1,0:T(8,128)S(1)} %copy-done.8, f32[32,128]{1,0:T(8,128)S(1)} %copy-done.9), custom_call_target="tpu_custom_call" | custom-call | tf_op jit(solution)/shard_map/reach_maps/pallas_call | solution.py:483
  15.9 5.1 %zone_partials.1 = (f32[64,256]{1,0:T(8,128)S(1)}, f32[72,256]{1,0:T(8,128)S(1)}, f32[72,256]{1,0:T(8,128)S(1)}, f32[72,256]{1,0:T(8,128)S(1)}) custom-call(s32[2]{0:T(128)S(1)} %pad_add_fusion.place_ref, s32[1]{0:T(128)} %get-tuple-element.21.chunks_ref, f32[64,512]{1,0:T(8,128)S(1)} %get-tuple-element.24.grad_ref, s32[64,512]{1,0:T(8,128)S(1)} %bitcast.16, ...), custom_call_target="tpu_custom_call" | custom-call | tf_op jit(solution)/shard_map/zone_partials/pallas_call | solution.py:407
  21.0 1.3 %collective-permute-start.2 = (f32[72,256]{1,0:T(8,128)S(1)}, f32[72,256]{1,0:T(8,128)S(1)}, u32[]{:S(2)}, u32[]{:S(2)}) collective-permute-start(f32[72,256]{1,0:T(8,128)S(1)} %get-tuple-element.32), channel_id=1, source_target_pairs={{0,64},{64,128},{128,192},{192,0},{1,65},{65,129},{129,193},{193,1... | collective-permute-start | bytes 221192 | tf_op jit(solution)/shard_map/ppermute | solution.py:501
  22.3 2.4 %collective-permute-start.3 = (f32[72,256]{1,0:T(8,128)S(1)}, f32[72,256]{1,0:T(8,128)S(1)}, u32[]{:S(2)}, u32[]{:S(2)}) collective-permute-start(f32[72,256]{1,0:T(8,128)S(1)} %get-tuple-element.33), channel_id=1, source_target_pairs={{0,128},{64,192},{128,0},{192,64},{1,129},{65,193},{129,1},{193,65... | collective-permute-start | bytes 221192 | tf_op jit(solution)/shard_map/ppermute | solution.py:501
  24.8 1.2 %collective-permute-start.4 = (f32[72,256]{1,0:T(8,128)S(1)}, f32[72,256]{1,0:T(8,128)S(1)}, u32[]{:S(2)}, u32[]{:S(2)}) collective-permute-start(f32[72,256]{1,0:T(8,128)S(1)} %get-tuple-element.34), channel_id=1, source_target_pairs={{0,192},{64,0},{128,64},{192,128},{1,193},{65,1},{129,65},{193,129... | collective-permute-start | bytes 221192 | tf_op jit(solution)/shard_map/ppermute | solution.py:501
  25.9 0.0 collective-permute-done.2.first_ref
  25.9 2.2 %collective-permute-done.3.second_ref = f32[72,256]{1,0:T(8,128)S(1)} collective-permute-done((f32[72,256]{1,0:T(8,128)S(1)}, f32[72,256]{1,0:T(8,128)S(1)}, u32[]{:S(2)}, u32[]{:S(2)}) %collective-permute-start.3) | collective-permute-done | bytes 73760 | tf_op jit(solution)/shard_map/ppermute | solution.py:501
  28.1 0.1 collective-permute-done.4.third_ref
  28.2 1.2 %arrivals.1 = (f32[64,1,256]{2,1,0:T(1,128)}, f32[8,128]{1,0:T(8,128)S(1)}) custom-call(s32[2]{0:T(128)S(1)} %pad_add_fusion.place_ref, f32[64,256]{1,0:T(8,128)S(1)} %get-tuple-element.31.own_ref, f32[72,256]{1,0:T(8,128)S(1)} %collective-permute-done.2.first_ref, f32[72,256]{1,0:T(8,128)S(1)} %collective-permute-done.3.second_ref, ...), custom_call_target="tpu_custom_call" | custom-call | tf_op jit(solution)/shard_map/arrivals/pallas_call | solution.py:437
  29.4 15.7 %all-to-all-start = ((f32[64,1,256]{2,1,0:T(1,128)}), f32[64,1,256]{2,1,0:T(1,128)S(1)}, u32[]{:S(2)}, u32[]{:S(2)}) async-start(f32[64,1,256]{2,1,0:T(1,128)} %get-tuple-element.35), calls=%async_computation | async-start | bytes 131072 | tf_op jit(solution)/shard_map/all_to_all | solution.py:521
  45.0 0.6 %multiply_add_fusion = f32[32,128]{1,0:T(8,128)} fusion(f32[32,128]{1,0:T(8,128)S(1)} %get-tuple-element.38, f32[32,128]{1,0:T(8,128)S(1)} %get-tuple-element.36, f32[128]{0:T(128)S(1)} %slice_bitcast_fusion), kind=kLoop, calls=%fused_computation | loop fusion | flops 8192 | bytes 49664 | tf_op jit(solution)/shard_map/add | solution.py:522
  45.6 9.2 %all-to-all-done = f32[64,1,256]{2,1,0:T(1,128)S(1)} async-done(((f32[64,1,256]{2,1,0:T(1,128)}), f32[64,1,256]{2,1,0:T(1,128)S(1)}, u32[]{:S(2)}, u32[]{:S(2)}) %all-to-all-start) | async-done | bytes 65568 | tf_op jit(solution)/shard_map/all_to_all | solution.py:521
  54.8 0.1 reduce_sum.9
  54.9 0.5 fusion
  (13 shorter events, 0.0 us)
Async XLA Ops:
  0.6 0.9 %copy-start = (f32[1,64,512]{2,1,0:T(8,128)S(1)}, f32[1,64,512]{2,1,0:T(8,128)}, u32[]{:S(2)}) copy-start(f32[1,64,512]{2,1,0:T(8,128)} %param.8) | copy-start | bytes 393220
  1.5 0.9 %copy-start.2 = (f32[1,64,512]{2,1,0:T(8,128)S(1)}, f32[1,64,512]{2,1,0:T(8,128)}, u32[]{:S(2)}) copy-start(f32[1,64,512]{2,1,0:T(8,128)} %param.9) | copy-start | bytes 393220
  2.4 0.9 %copy-start.4 = (f32[1,64,512]{2,1,0:T(8,128)S(1)}, f32[1,64,512]{2,1,0:T(8,128)}, u32[]{:S(2)}) copy-start(f32[1,64,512]{2,1,0:T(8,128)} %param.10) | copy-start | bytes 393220
  3.3 7.1 %copy-start.6 = (s32[1,64,512]{2,1,0:T(8,128)S(1)}, s32[1,64,512]{2,1,0:T(8,128)}, u32[]{:S(2)}) copy-start(s32[1,64,512]{2,1,0:T(8,128)} %param.11) | copy-start | bytes 393220
  3.3 7.1 %copy-start.10 = (s32[32512]{0:T(1024)S(1)}, s32[32512]{0:T(1024)}, u32[]{:S(2)}) copy-start(s32[32512]{0:T(1024)} %param.12) | copy-start | bytes 390148
  3.4 10.3 %collective-permute-start = (f32[12,512]{1,0:T(8,128)S(1)}, f32[12,512]{1,0:T(8,128)S(1)}, u32[]{:S(2)}, u32[]{:S(2)}) collective-permute-start(f32[12,512]{1,0:T(8,128)S(1)} %get-tuple-element.22), channel_id=1, source_target_pairs={{0,1},{1,2},{2,3},{3,4},{4,5},{5,6},{6,7},{7,8},{8,9},{9,10},{10,1... | collective-permute-start | bytes 73736 | tf_op jit(solution)/shard_map/ppermute | solution.py:496
  8.4 5.3 %collective-permute-start.1 = (f32[12,512]{1,0:T(8,128)S(1)}, f32[12,512]{1,0:T(8,128)S(1)}, u32[]{:S(2)}, u32[]{:S(2)}) collective-permute-start(f32[12,512]{1,0:T(8,128)S(1)} %get-tuple-element.23), channel_id=1, source_target_pairs={{1,0},{2,1},{3,2},{4,3},{5,4},{6,5},{7,6},{8,7},{9,8},{10,9},{11,1... | collective-permute-start | bytes 73736 | tf_op jit(solution)/shard_map/ppermute | solution.py:496
  10.5 3.2 %copy-start.1 = (f32[1,64,512]{2,1,0:T(8,128)S(1)}, f32[1,64,512]{2,1,0:T(8,128)}, u32[]{:S(2)}) copy-start(f32[1,64,512]{2,1,0:T(8,128)} %param.8) | copy-start | bytes 393220
  10.5 3.3 %copy-start.3 = (f32[1,64,512]{2,1,0:T(8,128)S(1)}, f32[1,64,512]{2,1,0:T(8,128)}, u32[]{:S(2)}) copy-start(f32[1,64,512]{2,1,0:T(8,128)} %param.9) | copy-start | bytes 393220
  10.5 3.3 %copy-start.5 = (f32[1,64,512]{2,1,0:T(8,128)S(1)}, f32[1,64,512]{2,1,0:T(8,128)}, u32[]{:S(2)}) copy-start(f32[1,64,512]{2,1,0:T(8,128)} %param.10) | copy-start | bytes 393220
  13.6 1.4 %copy-start.7 = (s32[32,128]{1,0:T(8,128)S(1)}, s32[32,128]{1,0:T(8,128)}, u32[]{:S(2)}) copy-start(s32[32,128]{1,0:T(8,128)} %cell_ref.1) | copy-start | bytes 49156
  13.7 1.4 %copy-start.8 = (f32[32,128]{1,0:T(8,128)S(1)}, f32[32,128]{1,0:T(8,128)}, u32[]{:S(2)}) copy-start(f32[32,128]{1,0:T(8,128)} %keep_ref.1) | copy-start | bytes 49156
  13.7 1.4 %copy-start.9 = (f32[32,128]{1,0:T(8,128)S(1)}, f32[32,128]{1,0:T(8,128)}, u32[]{:S(2)}) copy-start(f32[32,128]{1,0:T(8,128)} %forcing_ref.1) | copy-start | bytes 49156
  21.0 4.9 %collective-permute-start.2 = (f32[72,256]{1,0:T(8,128)S(1)}, f32[72,256]{1,0:T(8,128)S(1)}, u32[]{:S(2)}, u32[]{:S(2)}) collective-permute-start(f32[72,256]{1,0:T(8,128)S(1)} %get-tuple-element.32), channel_id=1, source_target_pairs={{0,64},{64,128},{128,192},{192,0},{1,65},{65,129},{129,193},{193,1... | collective-permute-start | bytes 221192 | tf_op jit(solution)/shard_map/ppermute | solution.py:501
  22.3 5.8 %collective-permute-start.3 = (f32[72,256]{1,0:T(8,128)S(1)}, f32[72,256]{1,0:T(8,128)S(1)}, u32[]{:S(2)}, u32[]{:S(2)}) collective-permute-start(f32[72,256]{1,0:T(8,128)S(1)} %get-tuple-element.33), channel_id=1, source_target_pairs={{0,128},{64,192},{128,0},{192,64},{1,129},{65,193},{129,1},{193,65... | collective-permute-start | bytes 221192 | tf_op jit(solution)/shard_map/ppermute | solution.py:501
  24.8 3.4 %collective-permute-start.4 = (f32[72,256]{1,0:T(8,128)S(1)}, f32[72,256]{1,0:T(8,128)S(1)}, u32[]{:S(2)}, u32[]{:S(2)}) collective-permute-start(f32[72,256]{1,0:T(8,128)S(1)} %get-tuple-element.34), channel_id=1, source_target_pairs={{0,192},{64,0},{128,64},{192,128},{1,193},{65,1},{129,65},{193,129... | collective-permute-start | bytes 221192 | tf_op jit(solution)/shard_map/ppermute | solution.py:501
  29.4 25.4 %all-to-all-start = ((f32[64,1,256]{2,1,0:T(1,128)}), f32[64,1,256]{2,1,0:T(1,128)S(1)}, u32[]{:S(2)}, u32[]{:S(2)}) async-start(f32[64,1,256]{2,1,0:T(1,128)} %get-tuple-element.35), calls=%async_computation | async-start | bytes 131072 | tf_op jit(solution)/shard_map/all_to_all | solution.py:521

commit v2 on v1

--- a/solution.py
+++ b/solution.py
@@ -51,31 +51,61 @@
     return pltpu.roll(x, x.shape[0] - distance, 0)
 
 
-def front_kernel(depth_ref, rough_ref_, seed_ref, low_ref, high_ref):
-    for part, ref in enumerate((depth_ref, rough_ref_, seed_ref)):
+HBM = pl.BlockSpec(memory_space=pltpu.HBM)
+
+
+FETCH = pltpu.CompilerParams(vmem_limit_bytes=55800000)
+
+
+def front_kernel(*refs):
+    count = (len(refs) - 3) // 2
+    sources, kept = refs[:count], refs[count : 2 * count]
+    chip_ref, away_ref, arrived = refs[2 * count :]
+    copies = [
+        pltpu.make_async_copy(source, place, arrived.at[index])
+        for index, (source, place) in enumerate(zip(sources, kept))
+    ]
+    for copy in copies:
+        copy.start()
+    first_core = lax.axis_index("core") == 0
+    for part in range(3):
+        copies[part].wait()
+        ref = kept[part]
         rows = slice(part * HALO, (part + 1) * HALO)
-        low_ref[rows, :] = ref[ref.shape[0] - HALO :, :]
-        high_ref[rows, :] = ref[0:HALO, :]
-
-
-def edges_to_send(depth, rough, seed):
-    shape = jax.ShapeDtypeStruct((3 * HALO, depth.shape[1]), jnp.float32)
+        top = ref[0:HALO, :]
+        bottom = ref[ref.shape[0] - HALO :, :]
+        chip_ref[rows, :] = jnp.where(first_core, bottom, top)
+        away_ref[rows, :] = jnp.where(first_core, top, bottom)
+    for copy in copies[3:]:
+        copy.wait()
+
+
+def fetched(*arrays):
+    edge = jax.ShapeDtypeStruct((3 * HALO, arrays[0].shape[1]), jnp.float32)
+    kept = tuple(jax.ShapeDtypeStruct(x.shape, x.dtype) for x in arrays)
     return pl.pallas_call(
         front_kernel,
-        out_shape=(shape, shape),
-        in_specs=[VMEM] * 3,
-        out_specs=(VMEM, VMEM),
-        compiler_params=ROOMY,
-        name="edge_rows",
-    )(depth, rough, seed)
+        out_shape=kept + (edge, edge),
+        in_specs=[HBM] * len(arrays),
+        out_specs=(VMEM,) * (len(arrays) + 2),
+        scratch_shapes=[pltpu.SemaphoreType.DMA((len(arrays),))],
+        compiler_params=FETCH,
+        name="fetch_and_edges",
+    )(*arrays)
 
 
 ABSENT = 2**15 - 1
+
+
+def own_first_zone():
+    chip = lax.axis_index("basin") * lax.axis_size("chip") + lax.axis_index("chip")
+    return (chip * lax.axis_size("core") + lax.axis_index("core")) * SPAN
+
+
 CHUNK = 16
 
 
 def slot_kernel(
-    place_ref,
     owner_ref,
     label_ref,
     moves_ref,
@@ -87,17 +117,17 @@
     turned_ref,
     packed_ref,
 ):
-    first_zone = place_ref[0]
-    first_device = place_ref[1].astype(jnp.float32)
+    first_zone = own_first_zone()
+    core = lax.axis_index("core").astype(jnp.float32)
     table_ref[...] = jnp.full(table_ref.shape, 256.0 * SPAN, jnp.float32)
     table_ref[0 : owner_ref.shape[0], :] = owner_ref[...].astype(jnp.float32)
 
     def placed(slots):
         owners = jnp.floor((slots + 0.5) * (1.0 / SPAN))
         lanes = slots - owners * SPAN
-        turned = owners - first_device
-        turned = jnp.where(turned < 0, turned + 256.0, turned)
-        return jnp.where(owners < 256.0, turned, 256.0), lanes
+        chips = jnp.floor(owners * 0.5)
+        swapped = jnp.abs((owners - 2.0 * chips) - core)
+        return jnp.where(owners < 256.0, chips + 128.0 * swapped, 256.0), lanes
 
     owners, lanes = placed(jnp.transpose(table_ref[...]))
     turned_ref[0:LANES, :] = owners.astype(jnp.bfloat16)
@@ -165,7 +195,7 @@
 SMEM = pl.BlockSpec(memory_space=pltpu.SMEM)
 
 
-def slots_of(place, owner_slot, label):
+def slots_of(owner_slot, label):
     count = label.size // LANES
     stack = jax.ShapeDtypeStruct((count, LANES), jnp.float32)
     return pl.pallas_call(
@@ -177,7 +207,7 @@
             jax.ShapeDtypeStruct((8, LANES), jnp.float32),
             jax.ShapeDtypeStruct((1,), jnp.int32),
         ),
-        in_specs=[SMEM, VMEM, VMEM],
+        in_specs=[VMEM, VMEM],
         out_specs=(VMEM, VMEM, VMEM, VMEM, SMEM),
         scratch_shapes=[
             pltpu.VMEM((256, LANES), jnp.float32),
@@ -189,7 +219,7 @@
             flops=2 * 256 * 256 * label.size // 4, bytes_accessed=16 * label.size, transcendentals=0
         ),
         name="slot_lookup",
-    )(place, owner_slot.reshape(-1, LANES), label)
+    )(owner_slot, label)
 
 
 def below(x):
@@ -208,12 +238,15 @@
     return pltpu.roll(x, 1, 1)
 
 
-def window_kernel(depth_ref, rough_ref_, seed_ref, low_ref, high_ref, grad_ref, adjoint_ref):
+def window_kernel(depth_ref, rough_ref_, seed_ref, chip_ref, away_ref, grad_ref, adjoint_ref):
+    first_core = lax.axis_index("core") == 0
+
     def extended(part, ref):
-        start = part * HALO
-        return jnp.concatenate(
-            [low_ref[start : start + HALO, :], ref[...], high_ref[start : start + HALO, :]], axis=0
-        )
+        rows = slice(part * HALO, (part + 1) * HALO)
+        chip, away = chip_ref[rows, :], away_ref[rows, :]
+        low = jnp.where(first_core, away, chip)
+        high = jnp.where(first_core, chip, away)
+        return jnp.concatenate([low, ref[...], high], axis=0)
 
     depth = extended(0, depth_ref)
     rough = extended(1, rough_ref_)
@@ -256,7 +289,7 @@
     adjoint_ref[...] = adjoint[own]
 
 
-def window(depth, rough, seed, low, high):
+def window(depth, rough, seed, chip, away):
     shape = jax.ShapeDtypeStruct(depth.shape, jnp.float32)
     return pl.pallas_call(
         window_kernel,
@@ -265,7 +298,7 @@
         out_specs=(VMEM, VMEM),
         compiler_params=ROOMY,
         name="adjoint_window",
-    )(depth, rough, seed, low, high)
+    )(depth, rough, seed, chip, away)
 
 
 def halves(x):
@@ -316,7 +349,6 @@
 
 
 def zone_kernel(
-    place_ref,
     chunks_ref,
     grad_ref,
     label_ref,
@@ -324,16 +356,13 @@
     device_ref,
     lane_ref,
     home_ref,
-    edge_ref,
     own_ref,
-    first_ref,
-    second_ref,
-    third_ref,
+    other_ref,
     total_ref,
     stray_ref,
     offset_ref,
 ):
-    offset_ref[...] = label_ref[...] - place_ref[0]
+    offset_ref[...] = label_ref[...] - own_first_zone()
     grad = stacked(grad_ref[...])
     moves = moves_ref[...]
     bit = 0
@@ -392,23 +421,17 @@
         return carry
 
     lax.fori_loop(0, chunks_ref[0], one_chunk, 0)
-    tiles = own_ref.shape[0]
-    own_ref[...] = total_ref[0:tiles, :]
-    edge = jnp.broadcast_to(
-        jnp.concatenate([edge_ref[0:1, :], edge_ref[1:2, :]], axis=1), (8, 2 * LANES)
-    )
-    for step, ref in enumerate((first_ref, second_ref, third_ref), 1):
-        ref[0:tiles, :] = total_ref[step * tiles : (step + 1) * tiles, :]
-        ref[tiles : tiles + 8, :] = edge
-
-
-def zone_partials(place, chunks, grad, label, moves, device, lane, home, edge):
-    sent = jax.ShapeDtypeStruct((72, 2 * LANES), jnp.float32)
+    own_ref[...] = total_ref[0:LANES, :]
+    other_ref[...] = total_ref[LANES:, :]
+
+
+def zone_partials(chunks, grad, label, moves, device, lane, home):
+    half = jax.ShapeDtypeStruct((LANES, 2 * LANES), jnp.float32)
     return pl.pallas_call(
         zone_kernel,
-        out_shape=(jax.ShapeDtypeStruct((64, 2 * LANES), jnp.float32), sent, sent, sent),
-        in_specs=[SMEM, SMEM] + [VMEM] * 7,
-        out_specs=(VMEM,) * 4,
+        out_shape=(half, half),
+        in_specs=[SMEM] + [VMEM] * 6,
+        out_specs=(VMEM,) * 2,
         scratch_shapes=[
             pltpu.VMEM((256, 2 * LANES), jnp.float32),
             pltpu.VMEM((grad.size // LANES, LANES), jnp.float32),
@@ -416,35 +439,59 @@
         ],
         compiler_params=ROOMY,
         name="zone_partials",
-    )(place, chunks, grad, label, moves, device, lane, home, edge)
-
-
-def arrival_kernel(place_ref, own_ref, first_ref, second_ref, third_ref, sums_ref, incoming_ref):
-    tiles = own_ref.shape[0]
-    sums = own_ref[...] + first_ref[0:tiles, :]
-    sums = sums + (second_ref[0:tiles, :] + third_ref[0:tiles, :])
-    sums_ref[...] = sums.reshape(sums_ref.shape)
-    basin = place_ref[1] // tiles
-    incoming = jnp.zeros((8, LANES), jnp.float32)
-    for hop, ref in ((3, first_ref), (2, second_ref), (1, third_ref)):
-        edge = ref[tiles : tiles + 8, :]
-        there = jnp.where(basin + hop < 4, 1.0, 0.0)
-        incoming = there * (edge[:, :LANES] * incoming + edge[:, LANES:])
-    incoming_ref[...] = incoming
-
-
-def arrivals(place, own, *others):
-    return pl.pallas_call(
-        arrival_kernel,
-        out_shape=(
-            jax.ShapeDtypeStruct((own.shape[0], 1, own.shape[1]), jnp.float32),
-            jax.ShapeDtypeStruct((8, LANES), jnp.float32),
-        ),
-        in_specs=[SMEM] + [VMEM] * 4,
-        out_specs=(VMEM, VMEM),
+    )(chunks, grad, label, moves, device, lane, home)
+
+
+def parcel_kernel(own_ref, other_ref, edge_ref, out_ref):
+    chips = own_ref.shape[0]
+    sums = own_ref[...] + other_ref[...]
+    out_ref[pl.ds(0, chips, stride=4), :] = sums[:, :LANES]
+    out_ref[pl.ds(1, chips, stride=4), :] = sums[:, LANES:]
+    for part in range(2):
+        edge = jnp.broadcast_to(edge_ref[part : part + 1, :], (chips, LANES))
+        out_ref[pl.ds(2 + part, chips, stride=4), :] = edge
+
+
+def parcels(own, other, edge):
+    return pl.pallas_call(
+        parcel_kernel,
+        out_shape=jax.ShapeDtypeStruct((4 * own.shape[0], LANES), jnp.float32),
+        in_specs=[VMEM] * 3,
+        out_specs=VMEM,
         compiler_params=ROOMY,
-        name="arrivals",
-    )(place, own, *others)
+        name="parcels",
+    )(own, other, edge)
+
+
+def result_kernel(arrived_ref, rate_ref, push_ref, grad_ref, curve_ref, reach_ref):
+    rows = arrived_ref.shape[0]
+    sums = arrived_ref[0:8, :]
+    for start in range(8, rows, 8):
+        sums = sums + arrived_ref[start : start + 8, :]
+    grad_ref[...] = (sums[0:1, :] + sums[4:5, :])[:, :SPAN]
+    curve_ref[...] = (sums[1:2, :] + sums[5:6, :])[:, :SPAN]
+    basin, chip = lax.axis_index("basin"), lax.axis_index("chip")
+    basins, chips = lax.axis_size("basin"), lax.axis_size("chip")
+    incoming = jnp.zeros((1, LANES), jnp.float32)
+    for hop in reversed(range(1, basins)):
+        there = jnp.where(basin + hop < basins, 1.0, 0.0)
+        row = 4 * (jnp.minimum(basin + hop, basins - 1) * chips + chip)
+        rate = arrived_ref[pl.ds(row + 2, 1), :]
+        push = arrived_ref[pl.ds(row + 3, 1), :]
+        incoming = there * (rate * incoming + push)
+    reach_ref[...] = rate_ref[...] * incoming + push_ref[...]
+
+
+def results(arrived, rate, push):
+    zone = jax.ShapeDtypeStruct((1, SPAN), jnp.float32)
+    return pl.pallas_call(
+        result_kernel,
+        out_shape=(zone, zone, jax.ShapeDtypeStruct(rate.shape, jnp.float32)),
+        in_specs=[VMEM] * 3,
+        out_specs=(VMEM,) * 3,
+        compiler_params=ROOMY,
+        name="results",
+    )(arrived, rate, push)
 
 
 def reach_kernel(adjoint_ref, cell_ref, keep_ref, forcing_ref, rate_ref, push_ref, edge_ref):
@@ -490,52 +537,52 @@
     )(adjoint, cells, keep, forcing)
 
 
-def moved(value, axis, steps):
-    count = lax.axis_size(axis)
-    pairs = [(i, i + steps) for i in range(count) if 0 <= i + steps < count]
-    return lax.ppermute(value, axis, pairs)
-
-
-def turned(value, axis, steps):
-    count = lax.axis_size(axis)
-    return lax.ppermute(value, axis, [(i, (i + steps) % count) for i in range(count)])
+def swapped(value):
+    return lax.ppermute(value, "core", [(0, 1), (1, 0)])
+
+
+def exchanged_away(value):
+    chips, cores = lax.axis_size("chip"), lax.axis_size("core")
+    edges = [(i, i + 1) for i in range(1, chips * cores - 1, 2)]
+    return lax.ppermute(value, ("chip", "core"), edges + [(j, i) for i, j in edges])
 
 
 def per_device(
     depth_start, roughness, depth_seed, zone_label, owner_slot, retention, forcing, levee_cell
 ):
-    depth, rough, seed, label = depth_start[0], roughness[0], depth_seed[0], zone_label[0]
-    tiles = lax.axis_size("tile")
-    first_device = lax.axis_index("basin") * tiles
-    place = jnp.stack([(first_device + lax.axis_index("tile")) * SPAN, first_device])
-    place = place.astype(jnp.int32)
-    to_next, to_last = edges_to_send(depth, rough, seed)
-    low = moved(to_next, "tile", 1)
-    high = moved(to_last, "tile", -1)
-    moves, device, lane, home, chunks = slots_of(place, owner_slot, label)
-    grad, adjoint = window(depth, rough, seed, low, high)
+    depth, rough, seed, label, owner_slot, to_chip, to_away = fetched(
+        depth_start[0],
+        roughness[0],
+        depth_seed[0],
+        zone_label[0],
+        owner_slot.reshape(-1, LANES),
+    )
+    from_away = exchanged_away(to_away)
+    from_chip = swapped(to_chip)
+    moves, device, lane, home, chunks = slots_of(owner_slot, label)
+    grad, adjoint = window(depth, rough, seed, from_chip, from_away)
+    own, other = zone_partials(chunks, grad, label, moves, device, lane, home)
+    other = swapped(other)
     rate, push, edge = reach_maps(adjoint, levee_cell, retention, forcing)
-    own, *others = zone_partials(place, chunks, grad, label, moves, device, lane, home, edge)
-    others = [turned(part, "basin", step) for step, part in enumerate(others, 1)]
-    sums, incoming = arrivals(place, own, *others)
-    arrived = lax.all_to_all(sums, "tile", 0, 0, tiled=True)
-    reach_adjoint = rate * incoming[:1] + push
-    sums = jnp.sum(arrived, axis=(0, 1))
-    return (sums[:SPAN], sums[LANES : LANES + SPAN], reach_adjoint)
+    sent = parcels(own, other, edge).reshape(-1, 4, LANES)
+    arrived = lax.all_to_all(sent, ("basin", "chip"), 0, 0, tiled=True)
+    grad, curve, reach_adjoint = results(arrived.reshape(-1, LANES), rate, push)
+    return (grad.reshape(-1), curve.reshape(-1), reach_adjoint)
 
 
 def solution(mesh):
-    in_specs = (
-        P("basin", "tile", None),
-        P("basin", "tile", None),
-        P("basin", "tile", None),
-        P("basin", "tile", None),
-        P(),
-        P("basin", "tile"),
-        P("basin", "tile"),
-        P("basin", "tile"),
-    )
-    out_specs = (P(("basin", "tile")), P(("basin", "tile")), P("basin", "tile"))
+    basins, tiles = mesh.devices.shape
+    fine = jax.sharding.Mesh(
+        mesh.devices.reshape(basins, tiles // 2, 2), ("basin", "chip", "core")
+    )
+    tile = ("chip", "core")
+    cells = P("basin", tile, None)
+    reaches = P("basin", tile)
+    zones = P(("basin", "chip", "core"))
     return jax.shard_map(
-        per_device, mesh=mesh, in_specs=in_specs, out_specs=out_specs, check_vma=False
-    )
+        per_device,
+        mesh=fine,
+        in_specs=(cells, cells, cells, cells, P(), reaches, reaches, reaches),
+        out_specs=(zones, zones, reaches),
+        check_vma=False,
+    )

time: 55.2 us -> 48 us (0.87); the launches traced: 55.4 us -> 47.7 us
  blocking collectives: 0 us -> 29.1 us
  starting transfers between devices: 27.5 us -> 5.33 us
  waiting for transfers between devices: 11.4 us -> 1.13 us
  local copies, waits for them, and re-layouts: 3.27 us -> 0.02 us
  other arithmetic: 0.78 us -> 0 us
    all_to_all x0 -> x1, blocking collectives: none -> 29.1 us  [per_device(): arrived = lax.all_to_all(sent, ('basin', 'chip'), 0, 0, tiled=True)]
    all_to_all x1 -> x0, starting transfers between devices: 15.7 us -> none  [per_device(): arrived = lax.all_to_all(sums, 'tile', 0, 0, tiled=True)]
    all_to_all x1 -> x0, waiting for transfers between devices: 9.18 us -> none  [per_device(): arrived = lax.all_to_all(sums, 'tile', 0, 0, tiled=True)]
    ppermute x5 -> x3, starting transfers between devices: 11.9 us -> 5.33 us  [the longest x2 3.42 us: swapped(): return lax.ppermute(value, 'core', [(0, 1), (1, 0)])]
    unnamed x22 -> x6, local copies, waits for them, and re-layouts: 2.75 us -> 0.02 us
    ppermute x5 -> x3, waiting for transfers between devices: 2.26 us -> 1.13 us  [the longest x1 0.64 us: exchanged_away(): lax.ppermute(value, ('chip', 'core'), edges + [(j, i) for i, j in edges])]
    add x1 -> x0, other arithmetic: 0.61 us -> none  [per_device(): reach_adjoint = rate * incoming[:1] + push]
    pallas_call x3 -> x4, Pallas kernels: 6.34 us -> 6.51 us  [the longest x1 4.6 us: zone_partials(): pl.pallas_call(zone_kernel, out_shape=(half, half), in_specs=[SMEM] + [VM...]
  transfers between devices with their start and end apart: 6 -> 3, of which waited for: 3 -> 2; matrix products, arithmetic and copies ran while one was open for 1% -> 0% of each run, Pallas kernels for 6% -> 7%
where the time goes in v2:
time: 48 us; the launch traced here: 47.7 us
  blocking collectives  29.1 us (61%)
  Pallas kernels  11.3 us (24%)
  starting transfers between devices  5.33 us (11%)
  waiting for transfers between devices  1.13 us (2%)
  between operations  0.74 us (2%)
    all_to_all x1, blocking collectives, per_device(): arrived = lax.all_to_all(sent, ('basin', 'chip'), 0, 0, tiled=True)  29.1 us
    pallas_call x1, Pallas kernels, zone_partials(): pl.pallas_call(zone_kernel, out_shape=(half, half), in_specs=[SMEM] + [VM...  4.6 us
    ppermute x2, starting transfers between devices, swapped(): return lax.ppermute(value, 'core', [(0, 1), (1, 0)])  3.42 us
    pallas_call x1, Pallas kernels, slots_of(): pl.pallas_call(slot_kernel, out_shape=(jax.ShapeDtypeStruct((count, LANES...  2.64 us
    ppermute x1, starting transfers between devices, exchanged_away(): lax.ppermute(value, ('chip', 'core'), edges + [(j, i) for i, j in edges])  1.91 us
    pallas_call x1, Pallas kernels, window(): pl.pallas_call(window_kernel, out_shape=(shape, shape), in_specs=[VMEM] *...  1.33 us
    pallas_call x1, Pallas kernels, fetched(): pl.pallas_call(front_kernel, out_shape=kept + (edge, edge), in_specs=[HBM...  1.21 us
  transfers between devices with their start and end apart: 3, of which 2 were waited for; matrix products, arithmetic and copies ran while one was open for 0% of the time, Pallas kernels for 7%

profile of v2, /device:TPU:1, one launch (start us, length us, event | category | flops | bytes accessed | tf_op | source)
XLA Modules:
  0.0 47.7 jit_solution(7056681721826042572)
XLA Ops:
  0.6 1.2 %fetch_and_edges.1 = (f32[64,512]{1,0:T(8,128)S(1)}, f32[64,512]{1,0:T(8,128)S(1)}, f32[64,512]{1,0:T(8,128)S(1)}, s32[64,512]{1,0:T(8,128)S(1)}, s32[254,128]{1...) custom-call(f32[64,512]{1,0:T(8,128)} %bitcast.11, f32[64,512]{1,0:T(8,128)} %bitcast.12, ...), custom_call_target="tpu_custom_call" | custom-call | tf_op jit(solution)/shard_map/fetch_and_edges/pallas_call | solution.py:86
  1.8 3.3 %collective-permute-start = (f32[12,512]{1,0:T(8,128)S(1)}, f32[12,512]{1,0:T(8,128)S(1)}, u32[]{:S(2)}, u32[]{:S(2)}) collective-permute-start(f32[12,512]{1,0:T(8,128)S(1)} %get-tuple-element.31), channel_id=1, source_target_pairs={{0,1},{1,0},{2,3},{3,2},{4,5},{5,4},{6,7},{7,6},{8,9},{9,8},{10,11... | collective-permute-start | bytes 73736 | tf_op jit(solution)/shard_map/ppermute | solution.py:541
  5.2 1.9 %collective-permute-start.1 = (f32[12,512]{1,0:T(8,128)S(1)}, f32[12,512]{1,0:T(8,128)S(1)}, u32[]{:S(2)}, u32[]{:S(2)}) collective-permute-start(f32[12,512]{1,0:T(8,128)S(1)} %get-tuple-element.32), channel_id=1, source_target_pairs={{1,2},{3,4},{5,6},{7,8},{9,10},{11,12},{13,14},{15,16},{17,18},{19... | collective-permute-start | bytes 73736 | tf_op jit(solution)/shard_map/ppermute | solution.py:547
  7.1 2.6 %slot_lookup.1 = (s32[256,128]{1,0:T(8,128)S(1)}, f32[256,128]{1,0:T(8,128)S(1)}, f32[256,128]{1,0:T(8,128)S(1)}, f32[8,128]{1,0:T(8,128)S(1)}, s32[1]{0:T(128)}) custom-call(s32[254,128]{1,0:T(8,128)S(1)} %get-tuple-element.25.owner_ref, s32[64,512]{1,0:T(8,128)S(1)} %get-tuple-element.26.label_ref), custom_call_target="tpu_custom_call" | custom-call | flops 1073741824 | bytes 524288 | tf_op jit(solution)/shard_map/slot_lookup/pallas_call | solution.py:201
  9.7 0.0 collective-permute-done.chip_ref
  9.8 0.6 %collective-permute-done.1.away_ref = f32[12,512]{1,0:T(8,128)S(1)} collective-permute-done((f32[12,512]{1,0:T(8,128)S(1)}, f32[12,512]{1,0:T(8,128)S(1)}, u32[]{:S(2)}, u32[]{:S(2)}) %collective-permute-start.1) | collective-permute-done | bytes 24608 | tf_op jit(solution)/shard_map/ppermute | solution.py:547
  10.4 1.3 %adjoint_window.1 = (f32[64,512]{1,0:T(8,128)S(1)}, f32[64,512]{1,0:T(8,128)S(1)}) custom-call(f32[64,512]{1,0:T(8,128)S(1)} %get-tuple-element.28.depth_ref, f32[64,512]{1,0:T(8,128)S(1)} %get-tuple-element.29.rough_ref_, f32[64,512]{1,0:T(8,128)S(1)} %get-tuple-element.30.seed_ref, f32[12,512]{1,0:T(8,128)S(1)} %collective-permute-done.chip_ref, ...), custom_call_target="tpu_custom_call" | custom-call | tf_op jit(solution)/shard_map/adjoint_window/pallas_call | solution.py:294
  11.7 0.0 copy-start
  11.7 0.0 copy-start.1
  11.8 0.0 copy-start.2
  11.8 4.6 %zone_partials.1 = (f32[128,256]{1,0:T(8,128)S(1)}, f32[128,256]{1,0:T(8,128)S(1)}) custom-call(s32[1]{0:T(128)} %get-tuple-element.27.chunks_ref, f32[64,512]{1,0:T(8,128)S(1)} %get-tuple-element.33.grad_ref, s32[64,512]{1,0:T(8,128)S(1)} %get-tuple-element.26.label_ref, s32[256,128]{1,0:T(8,128)S(1)} %get-tuple-element.34.moves_ref, ...), custom_call_target="tpu_custom_call" | custom-call | tf_op jit(solution)/shard_map/zone_partials/pallas_call | solution.py:430
  16.4 0.1 collective-permute-start.2
  16.5 0.0 copy-done
  16.5 0.0 copy-done.1
  16.5 0.0 copy-done.2
  16.5 0.8 %reach_maps.1 = (f32[32,128]{1,0:T(8,128)S(1)}, f32[32,128]{1,0:T(8,128)S(1)}, f32[2,128]{1,0:T(2,128)S(1)}) custom-call(f32[64,512]{1,0:T(8,128)S(1)} %get-tuple-element.40.adjoint_ref, s32[32,128]{1,0:T(8,128)S(1)} %copy-done, f32[32,128]{1,0:T(8,128)S(1)} %copy-done.1, f32[32,128]{1,0:T(8,128)S(1)} %copy-done.2), custom_call_target="tpu_custom_call" | custom-call | tf_op jit(solution)/shard_map/reach_maps/pallas_call | solution.py:530
  17.3 0.5 %collective-permute-done.2.other_ref = f32[128,256]{1,0:T(8,128)S(1)} collective-permute-done((f32[128,256]{1,0:T(8,128)S(1)}, f32[128,256]{1,0:T(8,128)S(1)}, u32[]{:S(2)}, u32[]{:S(2)}) %collective-permute-start.2) | collective-permute-done | bytes 131104 | tf_op jit(solution)/shard_map/ppermute | solution.py:541
  17.8 29.1 %all_to_all.5 = f32[128,4,128]{2,1,0:T(4,128)S(1)} all-to-all(f32[128,4,128]{2,1,0:T(4,128)S(1)} %bitcast.10), channel_id=1, replica_groups=mesh['basin'=4,'chip'=32,'core'=2] {'basin','chip'}, dimensions={0} | all-to-all | bytes 524288 | tf_op jit(solution)/shard_map/all_to_all | solution.py:568
  47.0 0.7 %results.1 = (f32[1,127]{1,0:T(1,128)}, f32[1,127]{1,0:T(1,128)}, f32[32,128]{1,0:T(8,128)}) custom-call(f32[512,128]{1,0:T(8,128)S(1)} %bitcast.9, f32[32,128]{1,0:T(8,128)S(1)} %get-tuple-element.42.rate_ref, f32[32,128]{1,0:T(8,128)S(1)} %get-tuple-element.43.push_ref), custom_call_target="tpu_custom_call" | custom-call | tf_op jit(solution)/shard_map/results/pallas_call | solution.py:487
  (1 shorter events, 0.0 us)
Async XLA Ops:
  1.8 7.9 %collective-permute-start = (f32[12,512]{1,0:T(8,128)S(1)}, f32[12,512]{1,0:T(8,128)S(1)}, u32[]{:S(2)}, u32[]{:S(2)}) collective-permute-start(f32[12,512]{1,0:T(8,128)S(1)} %get-tuple-element.31), channel_id=1, source_target_pairs={{0,1},{1,0},{2,3},{3,2},{4,5},{5,4},{6,7},{7,6},{8,9},{9,8},{10,11... | collective-permute-start | bytes 73736 | tf_op jit(solution)/shard_map/ppermute | solution.py:541
  5.2 5.2 %collective-permute-start.1 = (f32[12,512]{1,0:T(8,128)S(1)}, f32[12,512]{1,0:T(8,128)S(1)}, u32[]{:S(2)}, u32[]{:S(2)}) collective-permute-start(f32[12,512]{1,0:T(8,128)S(1)} %get-tuple-element.32), channel_id=1, source_target_pairs={{1,2},{3,4},{5,6},{7,8},{9,10},{11,12},{13,14},{15,16},{17,18},{19... | collective-permute-start | bytes 73736 | tf_op jit(solution)/shard_map/ppermute | solution.py:547
  11.7 4.7 %copy-start = (s32[32,128]{1,0:T(8,128)S(1)}, s32[32,128]{1,0:T(8,128)}, u32[]{:S(2)}) copy-start(s32[32,128]{1,0:T(8,128)} %cell_ref.1) | copy-start | bytes 49156
  11.7 4.7 %copy-start.1 = (f32[32,128]{1,0:T(8,128)S(1)}, f32[32,128]{1,0:T(8,128)}, u32[]{:S(2)}) copy-start(f32[32,128]{1,0:T(8,128)} %keep_ref.1) | copy-start | bytes 49156
  11.8 4.7 %copy-start.2 = (f32[32,128]{1,0:T(8,128)S(1)}, f32[32,128]{1,0:T(8,128)}, u32[]{:S(2)}) copy-start(f32[32,128]{1,0:T(8,128)} %forcing_ref.1) | copy-start | bytes 49156
  16.4 1.4 %collective-permute-start.2 = (f32[128,256]{1,0:T(8,128)S(1)}, f32[128,256]{1,0:T(8,128)S(1)}, u32[]{:S(2)}, u32[]{:S(2)}) collective-permute-start(f32[128,256]{1,0:T(8,128)S(1)} %get-tuple-element.39), channel_id=1, source_target_pairs={{0,1},{1,0},{2,3},{3,2},{4,5},{5,4},{6,7},{7,6},{8,9},{9,8},{10,11... | collective-permute-start | bytes 393224 | tf_op jit(solution)/shard_map/ppermute | solution.py:541

commit v3 on v2

--- a/solution.py
+++ b/solution.py
@@ -102,7 +102,8 @@
     return (chip * lax.axis_size("core") + lax.axis_index("core")) * SPAN
 
 
-CHUNK = 16
+BASE_ROWS = 48
+CHUNK = 8
 
 
 def slot_kernel(
@@ -112,7 +113,6 @@
     device_ref,
     lane_ref,
     home_ref,
-    chunks_ref,
     table_ref,
     turned_ref,
     packed_ref,
@@ -130,8 +130,8 @@
         return jnp.where(owners < 256.0, chips + 128.0 * swapped, 256.0), lanes
 
     owners, lanes = placed(jnp.transpose(table_ref[...]))
-    turned_ref[0:LANES, :] = owners.astype(jnp.bfloat16)
-    turned_ref[LANES : 2 * LANES, :] = lanes.astype(jnp.bfloat16)
+    turned_ref[:, 0:256] = (owners * LANES).astype(jnp.bfloat16)
+    turned_ref[:, 256:512] = lanes.astype(jnp.bfloat16)
 
     home_row = first_zone // LANES
     shift = first_zone % LANES
@@ -141,8 +141,8 @@
     spot = lax.broadcasted_iota(jnp.int32, (8, LANES), 1)
     home = jnp.where(spot + shift < LANES, pair[0], pair[1])
     home_device, home_lane = placed(jnp.where(spot < SPAN, home, 256.0 * SPAN))
-    top = lax.broadcasted_iota(jnp.int32, (8, LANES), 0) == 0
-    home_ref[...] = jnp.where(top, home_device, home_lane)
+    home_ref[0:1, :] = home_device[0:1]
+    home_ref[1:2, :] = home_lane[0:1]
 
     label = stacked(label_ref[...])
     count = label.shape[0]
@@ -169,30 +169,34 @@
     moves_ref[...] = moves
     packed_ref[...] = packed & ABSENT
     most = count - jnp.min(jnp.sum(at_home_count, axis=0, keepdims=True)).astype(jnp.int32)
-    chunks = (most + CHUNK - 1) // CHUNK
-    chunks_ref[0] = chunks
-
-    def one_chunk(index, carry):
-        for quarter in range(CHUNK // 4):
-            start = index * CHUNK + quarter * 4
-            group_label = jnp.concatenate(
-                [packed_ref[pl.ds(start + i, 1), :] for i in range(4)], axis=1
-            )
+    chunks = jnp.maximum((most - BASE_ROWS + CHUNK - 1) // CHUNK, 0)
+    home_ref[2:3, :] = jnp.full((1, LANES), chunks.astype(jnp.float32))
+
+    def look_up(first, rows):
+        for start in range(0, rows, 4):
+            places = [pl.ds(first + start + i, 1) for i in range(4)]
+            group_label = jnp.concatenate([packed_ref[place, :] for place in places], axis=1)
             width = group_label.shape[1]
             group = one_hot(spread_rows((group_label >> 7).astype(jnp.float32)), 256)
-            found = jnp.dot(turned_ref[...], group, preferred_element_type=jnp.float32)
+            found = jnp.dot(
+                turned_ref[...],
+                jnp.concatenate([group, group], axis=0),
+                preferred_element_type=jnp.float32,
+            )
             hit = (group_label & 127) == lax.broadcasted_iota(jnp.int32, (LANES, width), 0)
-            for half, ref in enumerate((device_ref, lane_ref)):
-                part = found[half * LANES : (half + 1) * LANES]
-                part = jnp.sum(jnp.where(hit, part, 0.0), axis=0, keepdims=True)
-                for i in range(4):
-                    ref[pl.ds(start + i, 1), :] = part[:, i * LANES : (i + 1) * LANES]
+            slot = jnp.sum(jnp.where(hit, found, 0.0), axis=0, keepdims=True)
+            owner = jnp.floor(slot * (1.0 / LANES))
+            lane = slot - owner * LANES
+            for i, place in enumerate(places):
+                device_ref[place, :] = owner[:, i * LANES : (i + 1) * LANES]
+                lane_ref[place, :] = lane[:, i * LANES : (i + 1) * LANES]
+
+    def one_chunk(index, carry):
+        look_up(BASE_ROWS + index * CHUNK, CHUNK)
         return carry
 
+    look_up(0, BASE_ROWS)
     lax.fori_loop(0, chunks, one_chunk, 0)
-
-
-SMEM = pl.BlockSpec(memory_space=pltpu.SMEM)
 
 
 def slots_of(owner_slot, label):
@@ -205,13 +209,12 @@
             stack,
             stack,
             jax.ShapeDtypeStruct((8, LANES), jnp.float32),
-            jax.ShapeDtypeStruct((1,), jnp.int32),
         ),
         in_specs=[VMEM, VMEM],
-        out_specs=(VMEM, VMEM, VMEM, VMEM, SMEM),
+        out_specs=(VMEM,) * 4,
         scratch_shapes=[
             pltpu.VMEM((256, LANES), jnp.float32),
-            pltpu.VMEM((256, 256), jnp.bfloat16),
+            pltpu.VMEM((LANES, 512), jnp.bfloat16),
             pltpu.VMEM((count, LANES), jnp.int32),
         ],
         compiler_params=ROOMY,
@@ -309,12 +312,12 @@
 HOME_ROWS = 8
 
 
-def zone_sums(device_rows, lane_rows, grad_rows, square_rows):
+def zone_sums(rows):
     left = []
     right = []
-    for device, lane, grad, square in zip(device_rows, lane_rows, grad_rows, square_rows):
+    for device, lane, *values in rows:
         left.append(one_hot(spread_rows(device), 256))
-        weights = [spread_rows(part) for part in halves(grad) + halves(square)]
+        weights = [spread_rows(part) for part in values]
         right.append(jnp.concatenate(one_hot(spread_rows(lane), LANES, weights), axis=0))
     both = lax.dot_general(
         jnp.concatenate(left, axis=1),
@@ -331,25 +334,13 @@
     )
 
 
-def home_products(label_row, grad_row):
-    width = label_row.shape[1]
-    group = jnp.broadcast_to((label_row >> 3).astype(jnp.float32), (16, width))
-    within = jnp.broadcast_to((label_row & 7).astype(jnp.float32), (16, width))
-    ids = lax.broadcasted_iota(jnp.int32, (16, width), 0)
-    zero = jnp.zeros((), jnp.bfloat16)
-    group_hit = group.astype(jnp.bfloat16) == ids.astype(jnp.float32).astype(jnp.bfloat16)
-    left = jnp.where(group_hit, jnp.ones((), jnp.bfloat16), zero)
-    within_hit = within.astype(jnp.bfloat16) == (ids & 7).astype(jnp.float32).astype(jnp.bfloat16)
-    right = []
-    for value in (grad_row, grad_row * grad_row):
-        pair = [jnp.broadcast_to(part, (8, width)) for part in halves(value)]
-        weights = jnp.concatenate(pair, axis=0).astype(jnp.bfloat16)
-        right.append(jnp.where(within_hit, weights, zero))
-    return left, jnp.concatenate(right, axis=0)
+def pair_rows(upper, lower):
+    width = upper.shape[1]
+    pair = [jnp.broadcast_to(part, (8, width)) for part in (upper, lower)]
+    return jnp.concatenate(pair, axis=0).astype(jnp.bfloat16)
 
 
 def zone_kernel(
-    chunks_ref,
     grad_ref,
     label_ref,
     moves_ref,
@@ -360,39 +351,53 @@
     other_ref,
     total_ref,
     stray_ref,
-    offset_ref,
+    cell_ref,
 ):
-    offset_ref[...] = label_ref[...] - own_first_zone()
-    grad = stacked(grad_ref[...])
+    offset = label_ref[...] - own_first_zone()
+    grad = grad_ref[...]
+    cell_ref[0] = (offset >> 3).astype(jnp.float32)
+    cell_ref[1] = (offset & 7).astype(jnp.float32)
+    cell_ref[2], cell_ref[3] = halves(grad)
+    cell_ref[4], cell_ref[5] = halves(grad * grad)
+    grad = stacked(grad)
     moves = moves_ref[...]
     bit = 0
     while 2**bit < grad.shape[0]:
         grad = jnp.where((moves & 2**bit) != 0, from_below(grad, 2**bit), grad)
         bit += 1
-    stray_ref[...] = grad
-
-    def home_rows(index, total):
+    stray_ref[0], stray_ref[1] = halves(grad)
+    stray_ref[2], stray_ref[3] = halves(grad * grad)
+    zero = jnp.zeros((), jnp.bfloat16)
+    width = grad_ref.shape[1]
+    ids = lax.broadcasted_iota(jnp.int32, (16, width), 0)
+    group_ids = ids.astype(jnp.float32).astype(jnp.bfloat16)
+    within_ids = (ids & 7).astype(jnp.float32).astype(jnp.bfloat16)
+
+    def home_rows(index):
         left = []
         right = []
         for step in range(HOME_ROWS):
             row = pl.ds(index * HOME_ROWS + step, 1)
-            one_left, one_right = home_products(offset_ref[row, :], grad_ref[row, :])
-            left.append(one_left)
-            right.append(one_right)
-        return total + lax.dot_general(
+            group_hit = spread_rows(cell_ref[0, row, :]) == group_ids
+            within_hit = spread_rows(cell_ref[1, row, :]) == within_ids
+            left.append(jnp.where(group_hit, jnp.ones((), jnp.bfloat16), zero))
+            weights = [
+                pair_rows(cell_ref[2 + part, row, :], cell_ref[3 + part, row, :])
+                for part in (0, 2)
+            ]
+            right.append(
+                jnp.concatenate([jnp.where(within_hit, w, zero) for w in weights], axis=0)
+            )
+        return lax.dot_general(
             jnp.concatenate(left, axis=1),
             jnp.concatenate(right, axis=1),
             (((1,), (1,)), ((), ())),
             preferred_element_type=jnp.float32,
         )
 
-    home = lax.fori_loop(
-        0,
-        grad_ref.shape[0] // HOME_ROWS,
-        home_rows,
-        jnp.zeros((16, 32), jnp.float32),
-        unroll=True,
-    )
+    home = home_rows(0)
+    for index in range(1, grad_ref.shape[0] // HOME_ROWS):
+        home = home + home_rows(index)
     part = lax.broadcasted_iota(jnp.int32, (32, 2 * LANES), 0)
     zone = lax.broadcasted_iota(jnp.int32, (32, 2 * LANES), 1)
     chosen = ((part & 7) == (zone & 7)) & ((part >= 16) == (zone >= LANES))
@@ -405,41 +410,44 @@
     group = lax.broadcasted_iota(jnp.int32, (16, 2 * LANES), 0)
     zone = lax.broadcasted_iota(jnp.int32, (16, 2 * LANES), 1)
     home = jnp.sum(jnp.where(((zone >> 3) & 15) == group, home, 0.0), axis=0, keepdims=True)
+    home = halves(home[:, :LANES]) + halves(home[:, LANES:])
+
+    def stray_rows(start, count):
+        rows = [pl.ds(start + step, 1) for step in range(count)]
+        return [
+            (device_ref[row, :], lane_ref[row, :], *(stray_ref[i, row, :] for i in range(4)))
+            for row in rows
+        ]
+
     total_ref[...] = zone_sums(
-        [home_ref[0:1, :]], [home_ref[1:2, :]], [home[:, :LANES]], [home[:, LANES:]]
+        stray_rows(0, BASE_ROWS) + [(home_ref[0:1, :], home_ref[1:2, :], *home)]
     )
 
     def one_chunk(index, carry):
-        rows = [pl.ds(index * CHUNK + step, 1) for step in range(CHUNK)]
-        grads = [stray_ref[row, :] for row in rows]
-        total_ref[...] += zone_sums(
-            [device_ref[row, :] for row in rows],
-            [lane_ref[row, :] for row in rows],
-            grads,
-            [grad * grad for grad in grads],
-        )
+        total_ref[...] += zone_sums(stray_rows(BASE_ROWS + index * CHUNK, CHUNK))
         return carry
 
-    lax.fori_loop(0, chunks_ref[0], one_chunk, 0)
+    chunks = jnp.max(home_ref[2:3, :]).astype(jnp.int32)
+    lax.fori_loop(0, chunks, one_chunk, 0)
     own_ref[...] = total_ref[0:LANES, :]
     other_ref[...] = total_ref[LANES:, :]
 
 
-def zone_partials(chunks, grad, label, moves, device, lane, home):
+def zone_partials(grad, label, moves, device, lane, home):
     half = jax.ShapeDtypeStruct((LANES, 2 * LANES), jnp.float32)
     return pl.pallas_call(
         zone_kernel,
         out_shape=(half, half),
-        in_specs=[SMEM] + [VMEM] * 6,
+        in_specs=[VMEM] * 6,
         out_specs=(VMEM,) * 2,
         scratch_shapes=[
             pltpu.VMEM((256, 2 * LANES), jnp.float32),
-            pltpu.VMEM((grad.size // LANES, LANES), jnp.float32),
-            pltpu.VMEM(grad.shape, jnp.int32),
+            pltpu.VMEM((4, grad.size // LANES, LANES), jnp.float32),
+            pltpu.VMEM((6,) + grad.shape, jnp.float32),
         ],
         compiler_params=ROOMY,
         name="zone_partials",
-    )(chunks, grad, label, moves, device, lane, home)
+    )(grad, label, moves, device, lane, home)
 
 
 def parcel_kernel(own_ref, other_ref, edge_ref, out_ref):
@@ -559,9 +567,9 @@
     )
     from_away = exchanged_away(to_away)
     from_chip = swapped(to_chip)
-    moves, device, lane, home, chunks = slots_of(owner_slot, label)
+    moves, device, lane, home = slots_of(owner_slot, label)
     grad, adjoint = window(depth, rough, seed, from_chip, from_away)
-    own, other = zone_partials(chunks, grad, label, moves, device, lane, home)
+    own, other = zone_partials(grad, label, moves, device, lane, home)
     other = swapped(other)
     rate, push, edge = reach_maps(adjoint, levee_cell, retention, forcing)
     sent = parcels(own, other, edge).reshape(-1, 4, LANES)

time: 48 us -> 46.8 us (0.975)
  Pallas kernels: 11.3 us -> 9.5 us
  waiting for transfers between devices: 1.13 us -> 2.1 us
    ppermute x1, waiting for transfers between devices: 0.64 us -> 1.61 us  [exchanged_away(): lax.ppermute(value, ('chip', 'core'), edges + [(j, i) for i, j in edges])]
    pallas_call x1, Pallas kernels: 2.64 us -> 1.68 us  [slots_of(): pl.pallas_call(slot_kernel, out_shape=(jax.ShapeDtypeStruct((count, LANES...]
    pallas_call x1, Pallas kernels: 4.6 us -> 3.76 us  [zone_partials(): pl.pallas_call(zone_kernel, out_shape=(half, half), in_specs=[VMEM] * 6,...]
  transfers between devices with their start and end apart: 3 -> 3, of which waited for: 2 -> 2; matrix products, arithmetic and copies ran while one was open for 0% -> 0% of each run, Pallas kernels for 7% -> 5%
where the time goes in v3:
time: 46.8 us; the launch traced here: 46.5 us
  blocking collectives  28.9 us (62%)
  Pallas kernels  9.5 us (20%)
  starting transfers between devices  5.33 us (11%)
  waiting for transfers between devices  2.1 us (4%)
  between operations  0.73 us (2%)
    all_to_all x1, blocking collectives, per_device(): arrived = lax.all_to_all(sent, ('basin', 'chip'), 0, 0, tiled=True)  28.9 us
    pallas_call x1, Pallas kernels, zone_partials(): pl.pallas_call(zone_kernel, out_shape=(half, half), in_specs=[VMEM] * 6,...  3.76 us
    ppermute x2, starting transfers between devices, swapped(): return lax.ppermute(value, 'core', [(0, 1), (1, 0)])  3.42 us
    ppermute x1, starting transfers between devices, exchanged_away(): lax.ppermute(value, ('chip', 'core'), edges + [(j, i) for i, j in edges])  1.91 us
    pallas_call x1, Pallas kernels, slots_of(): pl.pallas_call(slot_kernel, out_shape=(jax.ShapeDtypeStruct((count, LANES...  1.68 us
    ppermute x1, waiting for transfers between devices, exchanged_away(): lax.ppermute(value, ('chip', 'core'), edges + [(j, i) for i, j in edges])  1.61 us
    pallas_call x1, Pallas kernels, window(): pl.pallas_call(window_kernel, out_shape=(shape, shape), in_specs=[VMEM] *...  1.33 us
    pallas_call x1, Pallas kernels, fetched(): pl.pallas_call(front_kernel, out_shape=kept + (edge, edge), in_specs=[HBM...  1.21 us
  transfers between devices with their start and end apart: 3, of which 2 were waited for; matrix products, arithmetic and copies ran while one was open for 0% of the time, Pallas kernels for 5%

profile of v3, /device:TPU:1, one launch (start us, length us, event | category | flops | bytes accessed | tf_op | source)
XLA Modules:
  0.0 46.5 jit_solution(7098307008544194450)
XLA Ops:
  0.6 1.2 %fetch_and_edges.1 = (f32[64,512]{1,0:T(8,128)S(1)}, f32[64,512]{1,0:T(8,128)S(1)}, f32[64,512]{1,0:T(8,128)S(1)}, s32[64,512]{1,0:T(8,128)S(1)}, s32[254,128]{1...) custom-call(f32[64,512]{1,0:T(8,128)} %bitcast.11, f32[64,512]{1,0:T(8,128)} %bitcast.12, ...), custom_call_target="tpu_custom_call" | custom-call | tf_op jit(solution)/shard_map/fetch_and_edges/pallas_call | solution.py:86
  1.8 3.3 %collective-permute-start = (f32[12,512]{1,0:T(8,128)S(1)}, f32[12,512]{1,0:T(8,128)S(1)}, u32[]{:S(2)}, u32[]{:S(2)}) collective-permute-start(f32[12,512]{1,0:T(8,128)S(1)} %get-tuple-element.27), channel_id=1, source_target_pairs={{0,1},{1,0},{2,3},{3,2},{4,5},{5,4},{6,7},{7,6},{8,9},{9,8},{10,11... | collective-permute-start | bytes 73736 | tf_op jit(solution)/shard_map/ppermute | solution.py:549
  5.2 1.9 %collective-permute-start.1 = (f32[12,512]{1,0:T(8,128)S(1)}, f32[12,512]{1,0:T(8,128)S(1)}, u32[]{:S(2)}, u32[]{:S(2)}) collective-permute-start(f32[12,512]{1,0:T(8,128)S(1)} %get-tuple-element.28), channel_id=1, source_target_pairs={{1,2},{3,4},{5,6},{7,8},{9,10},{11,12},{13,14},{15,16},{17,18},{19... | collective-permute-start | bytes 73736 | tf_op jit(solution)/shard_map/ppermute | solution.py:555
  7.1 1.7 %slot_lookup.1 = (s32[256,128]{1,0:T(8,128)S(1)}, f32[256,128]{1,0:T(8,128)S(1)}, f32[256,128]{1,0:T(8,128)S(1)}, f32[8,128]{1,0:T(8,128)S(1)}) custom-call(s32[254,128]{1,0:T(8,128)S(1)} %get-tuple-element.31.owner_ref, s32[64,512]{1,0:T(8,128)S(1)} %get-tuple-element.30.label_ref), custom_call_target="tpu_custom_call" | custom-call | flops 1073741824 | bytes 524288 | tf_op jit(solution)/shard_map/slot_lookup/pallas_call | solution.py:205
  8.8 0.0 collective-permute-done.chip_ref
  8.8 1.6 %collective-permute-done.1.away_ref = f32[12,512]{1,0:T(8,128)S(1)} collective-permute-done((f32[12,512]{1,0:T(8,128)S(1)}, f32[12,512]{1,0:T(8,128)S(1)}, u32[]{:S(2)}, u32[]{:S(2)}) %collective-permute-start.1) | collective-permute-done | bytes 24608 | tf_op jit(solution)/shard_map/ppermute | solution.py:555
  10.4 1.3 %adjoint_window.1 = (f32[64,512]{1,0:T(8,128)S(1)}, f32[64,512]{1,0:T(8,128)S(1)}) custom-call(f32[64,512]{1,0:T(8,128)S(1)} %get-tuple-element.24.depth_ref, f32[64,512]{1,0:T(8,128)S(1)} %get-tuple-element.25.rough_ref_, f32[64,512]{1,0:T(8,128)S(1)} %get-tuple-element.26.seed_ref, f32[12,512]{1,0:T(8,128)S(1)} %collective-permute-done.chip_ref, ...), custom_call_target="tpu_custom_call" | custom-call | tf_op jit(solution)/shard_map/adjoint_window/pallas_call | solution.py:297
  11.7 0.0 copy-start
  11.7 0.0 copy-start.1
  11.8 0.0 copy-start.2
  11.8 3.8 %zone_partials.1 = (f32[128,256]{1,0:T(8,128)S(1)}, f32[128,256]{1,0:T(8,128)S(1)}) custom-call(f32[64,512]{1,0:T(8,128)S(1)} %get-tuple-element.29.grad_ref, s32[64,512]{1,0:T(8,128)S(1)} %get-tuple-element.30.label_ref, s32[256,128]{1,0:T(8,128)S(1)} %get-tuple-element.32.moves_ref, f32[256,128]{1,0:T(8,128)S(1)} %get-tuple-element.33.device_ref, ...), custom_call_target="tpu_custom_call" | custom-call | tf_op jit(solution)/shard_map/zone_partials/pallas_call | solution.py:438
  15.5 0.1 collective-permute-start.2
  15.6 0.0 copy-done
  15.6 0.0 copy-done.1
  15.7 0.0 copy-done.2
  15.7 0.8 %reach_maps.1 = (f32[32,128]{1,0:T(8,128)S(1)}, f32[32,128]{1,0:T(8,128)S(1)}, f32[2,128]{1,0:T(2,128)S(1)}) custom-call(f32[64,512]{1,0:T(8,128)S(1)} %get-tuple-element.38.adjoint_ref, s32[32,128]{1,0:T(8,128)S(1)} %copy-done, f32[32,128]{1,0:T(8,128)S(1)} %copy-done.1, f32[32,128]{1,0:T(8,128)S(1)} %copy-done.2), custom_call_target="tpu_custom_call" | custom-call | tf_op jit(solution)/shard_map/reach_maps/pallas_call | solution.py:538
  16.5 0.5 %collective-permute-done.2.other_ref = f32[128,256]{1,0:T(8,128)S(1)} collective-permute-done((f32[128,256]{1,0:T(8,128)S(1)}, f32[128,256]{1,0:T(8,128)S(1)}, u32[]{:S(2)}, u32[]{:S(2)}) %collective-permute-start.2) | collective-permute-done | bytes 131104 | tf_op jit(solution)/shard_map/ppermute | solution.py:549
  17.0 28.9 %all_to_all.5 = f32[128,4,128]{2,1,0:T(4,128)S(1)} all-to-all(f32[128,4,128]{2,1,0:T(4,128)S(1)} %bitcast.10), channel_id=1, replica_groups=mesh['basin'=4,'chip'=32,'core'=2] {'basin','chip'}, dimensions={0} | all-to-all | bytes 524288 | tf_op jit(solution)/shard_map/all_to_all | solution.py:576
  45.9 0.7 %results.1 = (f32[1,127]{1,0:T(1,128)}, f32[1,127]{1,0:T(1,128)}, f32[32,128]{1,0:T(8,128)}) custom-call(f32[512,128]{1,0:T(8,128)S(1)} %bitcast.9, f32[32,128]{1,0:T(8,128)S(1)} %get-tuple-element.40.rate_ref, f32[32,128]{1,0:T(8,128)S(1)} %get-tuple-element.41.push_ref), custom_call_target="tpu_custom_call" | custom-call | tf_op jit(solution)/shard_map/results/pallas_call | solution.py:495
  (1 shorter events, 0.0 us)
Async XLA Ops:
  1.8 6.9 %collective-permute-start = (f32[12,512]{1,0:T(8,128)S(1)}, f32[12,512]{1,0:T(8,128)S(1)}, u32[]{:S(2)}, u32[]{:S(2)}) collective-permute-start(f32[12,512]{1,0:T(8,128)S(1)} %get-tuple-element.27), channel_id=1, source_target_pairs={{0,1},{1,0},{2,3},{3,2},{4,5},{5,4},{6,7},{7,6},{8,9},{9,8},{10,11... | collective-permute-start | bytes 73736 | tf_op jit(solution)/shard_map/ppermute | solution.py:549
  5.2 5.2 %collective-permute-start.1 = (f32[12,512]{1,0:T(8,128)S(1)}, f32[12,512]{1,0:T(8,128)S(1)}, u32[]{:S(2)}, u32[]{:S(2)}) collective-permute-start(f32[12,512]{1,0:T(8,128)S(1)} %get-tuple-element.28), channel_id=1, source_target_pairs={{1,2},{3,4},{5,6},{7,8},{9,10},{11,12},{13,14},{15,16},{17,18},{19... | collective-permute-start | bytes 73736 | tf_op jit(solution)/shard_map/ppermute | solution.py:555
  11.7 3.9 %copy-start = (s32[32,128]{1,0:T(8,128)S(1)}, s32[32,128]{1,0:T(8,128)}, u32[]{:S(2)}) copy-start(s32[32,128]{1,0:T(8,128)} %cell_ref.1) | copy-start | bytes 49156
  11.7 3.9 %copy-start.1 = (f32[32,128]{1,0:T(8,128)S(1)}, f32[32,128]{1,0:T(8,128)}, u32[]{:S(2)}) copy-start(f32[32,128]{1,0:T(8,128)} %keep_ref.1) | copy-start | bytes 49156
  11.8 3.9 %copy-start.2 = (f32[32,128]{1,0:T(8,128)S(1)}, f32[32,128]{1,0:T(8,128)}, u32[]{:S(2)}) copy-start(f32[32,128]{1,0:T(8,128)} %forcing_ref.1) | copy-start | bytes 49156
  15.5 1.4 %collective-permute-start.2 = (f32[128,256]{1,0:T(8,128)S(1)}, f32[128,256]{1,0:T(8,128)S(1)}, u32[]{:S(2)}, u32[]{:S(2)}) collective-permute-start(f32[128,256]{1,0:T(8,128)S(1)} %get-tuple-element.37), channel_id=1, source_target_pairs={{0,1},{1,0},{2,3},{3,2},{4,5},{5,4},{6,7},{7,6},{8,9},{9,8},{10,11... | collective-permute-start | bytes 393224 | tf_op jit(solution)/shard_map/ppermute | solution.py:549

commit v4 on v3

--- a/solution.py
+++ b/solution.py
@@ -241,19 +241,7 @@
     return pltpu.roll(x, 1, 1)
 
 
-def window_kernel(depth_ref, rough_ref_, seed_ref, chip_ref, away_ref, grad_ref, adjoint_ref):
-    first_core = lax.axis_index("core") == 0
-
-    def extended(part, ref):
-        rows = slice(part * HALO, (part + 1) * HALO)
-        chip, away = chip_ref[rows, :], away_ref[rows, :]
-        low = jnp.where(first_core, away, chip)
-        high = jnp.where(first_core, chip, away)
-        return jnp.concatenate([low, ref[...], high], axis=0)
-
-    depth = extended(0, depth_ref)
-    rough = extended(1, rough_ref_)
-    adjoint = extended(2, seed_ref)
+def window(depth, rough, adjoint):
     rows, columns = depth.shape
     conduct = jnp.where(rough > 0, rough_ref / jnp.where(rough > 0, rough, 1.0), 0.0)
     not_last = lax.broadcasted_iota(jnp.int32, (rows, columns), 1) < columns - 1
@@ -287,21 +275,7 @@
     down_total = jnp.where(down_face, down_total, 0.0)
     side_total = jnp.where(side_face, side_total, 0.0)
     total = (down_total + above(down_total)) + (side_total + leftward(side_total))
-    own = slice(HALO, rows - HALO)
-    grad_ref[...] = ((0.5 * courant) * conduct * total)[own]
-    adjoint_ref[...] = adjoint[own]
-
-
-def window(depth, rough, seed, chip, away):
-    shape = jax.ShapeDtypeStruct(depth.shape, jnp.float32)
-    return pl.pallas_call(
-        window_kernel,
-        out_shape=(shape, shape),
-        in_specs=[VMEM] * 5,
-        out_specs=(VMEM, VMEM),
-        compiler_params=ROOMY,
-        name="adjoint_window",
-    )(depth, rough, seed, chip, away)
+    return (0.5 * courant) * conduct * total, adjoint
 
 
 def halves(x):
@@ -309,7 +283,7 @@
     return upper, x - upper
 
 
-HOME_ROWS = 8
+HOME_ROWS = 16
 
 
 def zone_sums(rows):
@@ -340,8 +314,81 @@
     return jnp.concatenate(pair, axis=0).astype(jnp.bfloat16)
 
 
+def set_cells(cell_ref, offset, grad):
+    cell_ref[0] = (offset >> 3).astype(jnp.float32)
+    cell_ref[1] = (offset & 7).astype(jnp.float32)
+    cell_ref[2], cell_ref[3] = halves(grad)
+    cell_ref[4], cell_ref[5] = halves(grad * grad)
+
+
+def home_products(cell_ref, first, count):
+    zero = jnp.zeros((), jnp.bfloat16)
+    width = cell_ref.shape[2]
+    ids = lax.broadcasted_iota(jnp.int32, (16, width), 0)
+    group_ids = ids.astype(jnp.float32).astype(jnp.bfloat16)
+    within_ids = (ids & 7).astype(jnp.float32).astype(jnp.bfloat16)
+    left = []
+    right = []
+    for step in range(count):
+        row = slice(first + step, first + step + 1)
+        group_hit = spread_rows(cell_ref[0, row, :]) == group_ids
+        within_hit = spread_rows(cell_ref[1, row, :]) == within_ids
+        left.append(jnp.where(group_hit, jnp.ones((), jnp.bfloat16), zero))
+        weights = [
+            pair_rows(cell_ref[2 + part, row, :], cell_ref[3 + part, row, :]) for part in (0, 2)
+        ]
+        right.append(jnp.concatenate([jnp.where(within_hit, w, zero) for w in weights], axis=0))
+    return lax.dot_general(
+        jnp.concatenate(left, axis=1),
+        jnp.concatenate(right, axis=1),
+        (((1,), (1,)), ((), ())),
+        preferred_element_type=jnp.float32,
+    )
+
+
+RIM = 2 * HALO
+
+
+def inner_kernel(
+    depth_ref, rough_ref_, seed_ref, label_ref, grad_ref, adjoint_ref, home_ref, cell_ref
+):
+    grad, adjoint = window(depth_ref[...], rough_ref_[...], seed_ref[...])
+    grad_ref[...] = grad
+    adjoint_ref[...] = adjoint
+    rows = grad.shape[0]
+    inside = slice(RIM, rows - RIM)
+    set_cells(cell_ref, (label_ref[...] - own_first_zone())[inside], grad[inside])
+    home = home_products(cell_ref, 0, HOME_ROWS)
+    for first in range(HOME_ROWS, rows - 2 * RIM, HOME_ROWS):
+        home = home + home_products(cell_ref, first, HOME_ROWS)
+    home_ref[...] = home
+
+
+def inner_part(depth, rough, seed, label):
+    shape = jax.ShapeDtypeStruct(depth.shape, jnp.float32)
+    return pl.pallas_call(
+        inner_kernel,
+        out_shape=(shape, shape, jax.ShapeDtypeStruct((16, 32), jnp.float32)),
+        in_specs=[VMEM] * 4,
+        out_specs=(VMEM,) * 3,
+        scratch_shapes=[pltpu.VMEM((6, depth.shape[0] - 2 * RIM, depth.shape[1]), jnp.float32)],
+        compiler_params=ROOMY,
+        cost_estimate=pl.CostEstimate(
+            flops=2 * 256 * 64 * depth.size, bytes_accessed=20 * depth.size, transcendentals=0
+        ),
+        name="inner_rows",
+    )(depth, rough, seed, label)
+
+
 def zone_kernel(
-    grad_ref,
+    depth_ref,
+    rough_ref_,
+    seed_ref,
+    chip_ref,
+    away_ref,
+    inner_grad_ref,
+    inner_adjoint_ref,
+    inner_home_ref,
     label_ref,
     moves_ref,
     device_ref,
@@ -349,16 +396,38 @@
     home_ref,
     own_ref,
     other_ref,
+    adjoint_ref,
     total_ref,
     stray_ref,
     cell_ref,
 ):
+    first_core = lax.axis_index("core") == 0
+    rows = depth_ref.shape[0]
+    near = RIM + HALO
+
+    def rim(part, ref):
+        halo = slice(part * HALO, (part + 1) * HALO)
+        chip, away = chip_ref[halo, :], away_ref[halo, :]
+        low = jnp.where(first_core, away, chip)
+        high = jnp.where(first_core, chip, away)
+        return jnp.concatenate([low, ref[0:near, :], ref[rows - near : rows, :], high], axis=0)
+
+    rim_grad, rim_adjoint = window(rim(0, depth_ref), rim(1, rough_ref_), rim(2, seed_ref))
+    top = slice(HALO, HALO + RIM)
+    bottom = slice(near + 2 * HALO, near + 2 * HALO + RIM)
+    inside = slice(RIM, rows - RIM)
+    adjoint_ref[...] = jnp.concatenate(
+        [rim_adjoint[top], inner_adjoint_ref[inside, :], rim_adjoint[bottom]], axis=0
+    )
     offset = label_ref[...] - own_first_zone()
-    grad = grad_ref[...]
-    cell_ref[0] = (offset >> 3).astype(jnp.float32)
-    cell_ref[1] = (offset & 7).astype(jnp.float32)
-    cell_ref[2], cell_ref[3] = halves(grad)
-    cell_ref[4], cell_ref[5] = halves(grad * grad)
+    set_cells(
+        cell_ref,
+        jnp.concatenate([offset[:RIM], offset[rows - RIM :]], axis=0),
+        jnp.concatenate([rim_grad[top], rim_grad[bottom]], axis=0),
+    )
+    grad = jnp.concatenate(
+        [rim_grad[top], inner_grad_ref[inside, :], rim_grad[bottom]], axis=0
+    )
     grad = stacked(grad)
     moves = moves_ref[...]
     bit = 0
@@ -367,37 +436,7 @@
         bit += 1
     stray_ref[0], stray_ref[1] = halves(grad)
     stray_ref[2], stray_ref[3] = halves(grad * grad)
-    zero = jnp.zeros((), jnp.bfloat16)
-    width = grad_ref.shape[1]
-    ids = lax.broadcasted_iota(jnp.int32, (16, width), 0)
-    group_ids = ids.astype(jnp.float32).astype(jnp.bfloat16)
-    within_ids = (ids & 7).astype(jnp.float32).astype(jnp.bfloat16)
-
-    def home_rows(index):
-        left = []
-        right = []
-        for step in range(HOME_ROWS):
-            row = pl.ds(index * HOME_ROWS + step, 1)
-            group_hit = spread_rows(cell_ref[0, row, :]) == group_ids
-            within_hit = spread_rows(cell_ref[1, row, :]) == within_ids
-            left.append(jnp.where(group_hit, jnp.ones((), jnp.bfloat16), zero))
-            weights = [
-                pair_rows(cell_ref[2 + part, row, :], cell_ref[3 + part, row, :])
-                for part in (0, 2)
-            ]
-            right.append(
-                jnp.concatenate([jnp.where(within_hit, w, zero) for w in weights], axis=0)
-            )
-        return lax.dot_general(
-            jnp.concatenate(left, axis=1),
-            jnp.concatenate(right, axis=1),
-            (((1,), (1,)), ((), ())),
-            preferred_element_type=jnp.float32,
-        )
-
-    home = home_rows(0)
-    for index in range(1, grad_ref.shape[0] // HOME_ROWS):
-        home = home + home_rows(index)
+    home = inner_home_ref[...] + home_products(cell_ref, 0, 2 * RIM)
     part = lax.broadcasted_iota(jnp.int32, (32, 2 * LANES), 0)
     zone = lax.broadcasted_iota(jnp.int32, (32, 2 * LANES), 1)
     chosen = ((part & 7) == (zone & 7)) & ((part >= 16) == (zone >= LANES))
@@ -433,21 +472,21 @@
     other_ref[...] = total_ref[LANES:, :]
 
 
-def zone_partials(grad, label, moves, device, lane, home):
+def zone_partials(depth, *others):
     half = jax.ShapeDtypeStruct((LANES, 2 * LANES), jnp.float32)
     return pl.pallas_call(
         zone_kernel,
-        out_shape=(half, half),
-        in_specs=[VMEM] * 6,
-        out_specs=(VMEM,) * 2,
+        out_shape=(half, half, jax.ShapeDtypeStruct(depth.shape, jnp.float32)),
+        in_specs=[VMEM] * (1 + len(others)),
+        out_specs=(VMEM,) * 3,
         scratch_shapes=[
             pltpu.VMEM((256, 2 * LANES), jnp.float32),
-            pltpu.VMEM((4, grad.size // LANES, LANES), jnp.float32),
-            pltpu.VMEM((6,) + grad.shape, jnp.float32),
+            pltpu.VMEM((4, depth.size // LANES, LANES), jnp.float32),
+            pltpu.VMEM((6, 2 * RIM, depth.shape[1]), jnp.float32),
         ],
         compiler_params=ROOMY,
         name="zone_partials",
-    )(grad, label, moves, device, lane, home)
+    )(depth, *others)
 
 
 def parcel_kernel(own_ref, other_ref, edge_ref, out_ref):
@@ -568,8 +607,10 @@
     from_away = exchanged_away(to_away)
     from_chip = swapped(to_chip)
     moves, device, lane, home = slots_of(owner_slot, label)
-    grad, adjoint = window(depth, rough, seed, from_chip, from_away)
-    own, other = zone_partials(grad, label, moves, device, lane, home)
+    inner = inner_part(depth, rough, seed, label)
+    own, other, adjoint = zone_partials(
+        depth, rough, seed, from_chip, from_away, *inner, label, moves, device, lane, home
+    )
     other = swapped(other)
     rate, push, edge = reach_maps(adjoint, levee_cell, retention, forcing)
     sent = parcels(own, other, edge).reshape(-1, 4, LANES)

time: 46.8 us -> 45 us (0.962)
  waiting for transfers between devices: 2.1 us -> 0.55 us
    ppermute x1, waiting for transfers between devices: 1.61 us -> 0.06 us  [exchanged_away(): lax.ppermute(value, ('chip', 'core'), edges + [(j, i) for i, j in edges])]
  transfers between devices with their start and end apart: 3 -> 3, of which waited for: 2 -> 2; matrix products, arithmetic and copies ran while one was open for 0% -> 0% of each run, Pallas kernels for 5% -> 9%
where the time goes in v4:
time: 45 us
  blocking collectives  29.2 us (65%)
  Pallas kernels  9.15 us (20%)
  starting transfers between devices  5.33 us (12%)
  between operations  0.7 us (2%)
  waiting for transfers between devices  0.55 us (1%)
    all_to_all x1, blocking collectives, per_device(): arrived = lax.all_to_all(sent, ('basin', 'chip'), 0, 0, tiled=True)  29.2 us
    ppermute x2, starting transfers between devices, swapped(): return lax.ppermute(value, 'core', [(0, 1), (1, 0)])  3.42 us
    pallas_call x1, Pallas kernels, zone_partials(): pl.pallas_call(zone_kernel, out_shape=(half, half, jax.ShapeDtypeStruct(d...  3.18 us
    ppermute x1, starting transfers between devices, exchanged_away(): lax.ppermute(value, ('chip', 'core'), edges + [(j, i) for i, j in edges])  1.91 us
    pallas_call x1, Pallas kernels, slots_of(): pl.pallas_call(slot_kernel, out_shape=(jax.ShapeDtypeStruct((count, LANES...  1.68 us
    pallas_call x1, Pallas kernels, inner_part(): pl.pallas_call(inner_kernel, out_shape=(shape, shape, jax.ShapeDtypeStruc...  1.56 us
    pallas_call x1, Pallas kernels, fetched(): pl.pallas_call(front_kernel, out_shape=kept + (edge, edge), in_specs=[HBM...  1.21 us
  transfers between devices with their start and end apart: 3, of which 2 were waited for; matrix products, arithmetic and copies ran while one was open for 0% of the time, Pallas kernels for 9%

profile of v4, /device:TPU:1, one launch (start us, length us, event | category | flops | bytes accessed | tf_op | source)
XLA Modules:
  0.0 45.0 jit_solution(51366386257196962)
XLA Ops:
  0.6 1.2 %fetch_and_edges.1 = (f32[64,512]{1,0:T(8,128)S(1)}, f32[64,512]{1,0:T(8,128)S(1)}, f32[64,512]{1,0:T(8,128)S(1)}, s32[64,512]{1,0:T(8,128)S(1)}, s32[254,128]{1...) custom-call(f32[64,512]{1,0:T(8,128)} %bitcast.11, f32[64,512]{1,0:T(8,128)} %bitcast.12, ...), custom_call_target="tpu_custom_call" | custom-call | tf_op jit(solution)/shard_map/fetch_and_edges/pallas_call | solution.py:86
  1.8 3.3 %collective-permute-start = (f32[12,512]{1,0:T(8,128)S(1)}, f32[12,512]{1,0:T(8,128)S(1)}, u32[]{:S(2)}, u32[]{:S(2)}) collective-permute-start(f32[12,512]{1,0:T(8,128)S(1)} %get-tuple-element.29), channel_id=1, source_target_pairs={{0,1},{1,0},{2,3},{3,2},{4,5},{5,4},{6,7},{7,6},{8,9},{9,8},{10,11... | collective-permute-start | bytes 73736 | tf_op jit(solution)/shard_map/ppermute | solution.py:588
  5.2 1.9 %collective-permute-start.1 = (f32[12,512]{1,0:T(8,128)S(1)}, f32[12,512]{1,0:T(8,128)S(1)}, u32[]{:S(2)}, u32[]{:S(2)}) collective-permute-start(f32[12,512]{1,0:T(8,128)S(1)} %get-tuple-element.30), channel_id=1, source_target_pairs={{1,2},{3,4},{5,6},{7,8},{9,10},{11,12},{13,14},{15,16},{17,18},{19... | collective-permute-start | bytes 73736 | tf_op jit(solution)/shard_map/ppermute | solution.py:594
  7.1 1.7 %slot_lookup.1 = (s32[256,128]{1,0:T(8,128)S(1)}, f32[256,128]{1,0:T(8,128)S(1)}, f32[256,128]{1,0:T(8,128)S(1)}, f32[8,128]{1,0:T(8,128)S(1)}) custom-call(s32[254,128]{1,0:T(8,128)S(1)} %get-tuple-element.35.owner_ref, s32[64,512]{1,0:T(8,128)S(1)} %get-tuple-element.31.label_ref), custom_call_target="tpu_custom_call" | custom-call | flops 1073741824 | bytes 524288 | tf_op jit(solution)/shard_map/slot_lookup/pallas_call | solution.py:205
  8.8 1.6 %inner_rows.1 = (f32[64,512]{1,0:T(8,128)S(1)}, f32[64,512]{1,0:T(8,128)S(1)}, f32[16,32]{1,0:T(8,128)S(1)}) custom-call(f32[64,512]{1,0:T(8,128)S(1)} %get-tuple-element.26.depth_ref, f32[64,512]{1,0:T(8,128)S(1)} %get-tuple-element.27.rough_ref_, f32[64,512]{1,0:T(8,128)S(1)} %get-tuple-element.28.seed_ref, s32[64,512]{1,0:T(8,128)S(1)} %get-tuple-element.31.label_ref), custom_call_target="tpu_custom_call" | custom-call | flops 1073741824 | bytes 655360 | tf_op jit(solution)/shard_map/inner_rows/pallas_call | solution.py:369
  10.3 0.0 collective-permute-done.chip_ref
  10.3 0.1 collective-permute-done.1.away_ref
  10.4 0.0 copy-start
  10.4 0.0 copy-start.1
  10.4 0.0 copy-start.2
  10.4 3.2 %zone_partials.1 = (f32[128,256]{1,0:T(8,128)S(1)}, f32[128,256]{1,0:T(8,128)S(1)}, f32[64,512]{1,0:T(8,128)S(1)}) custom-call(f32[64,512]{1,0:T(8,128)S(1)} %get-tuple-element.26.depth_ref, f32[64,512]{1,0:T(8,128)S(1)} %get-tuple-element.27.rough_ref_, f32[64,512]{1,0:T(8,128)S(1)} %get-tuple-element.28.seed_ref, ...), custom_call_target="tpu_custom_call" | custom-call | tf_op jit(solution)/shard_map/zone_partials/pallas_call | solution.py:477
  13.6 0.1 collective-permute-start.2
  13.7 0.0 copy-done
  13.7 0.0 copy-done.1
  13.7 0.0 copy-done.2
  13.7 0.8 %reach_maps.1 = (f32[32,128]{1,0:T(8,128)S(1)}, f32[32,128]{1,0:T(8,128)S(1)}, f32[2,128]{1,0:T(2,128)S(1)}) custom-call(f32[64,512]{1,0:T(8,128)S(1)} %get-tuple-element.42.adjoint_ref, s32[32,128]{1,0:T(8,128)S(1)} %copy-done, f32[32,128]{1,0:T(8,128)S(1)} %copy-done.1, f32[32,128]{1,0:T(8,128)S(1)} %copy-done.2), custom_call_target="tpu_custom_call" | custom-call | tf_op jit(solution)/shard_map/reach_maps/pallas_call | solution.py:577
  14.5 0.5 %collective-permute-done.2.other_ref = f32[128,256]{1,0:T(8,128)S(1)} collective-permute-done((f32[128,256]{1,0:T(8,128)S(1)}, f32[128,256]{1,0:T(8,128)S(1)}, u32[]{:S(2)}, u32[]{:S(2)}) %collective-permute-start.2) | collective-permute-done | bytes 131104 | tf_op jit(solution)/shard_map/ppermute | solution.py:588
  15.1 29.2 %all_to_all.5 = f32[128,4,128]{2,1,0:T(4,128)S(1)} all-to-all(f32[128,4,128]{2,1,0:T(4,128)S(1)} %bitcast.10), channel_id=1, replica_groups=mesh['basin'=4,'chip'=32,'core'=2] {'basin','chip'}, dimensions={0} | all-to-all | bytes 524288 | tf_op jit(solution)/shard_map/all_to_all | solution.py:617
  44.3 0.7 %results.1 = (f32[1,127]{1,0:T(1,128)}, f32[1,127]{1,0:T(1,128)}, f32[32,128]{1,0:T(8,128)}) custom-call(f32[512,128]{1,0:T(8,128)S(1)} %bitcast.9, f32[32,128]{1,0:T(8,128)S(1)} %get-tuple-element.44.rate_ref, f32[32,128]{1,0:T(8,128)S(1)} %get-tuple-element.45.push_ref), custom_call_target="tpu_custom_call" | custom-call | tf_op jit(solution)/shard_map/results/pallas_call | solution.py:534
  (1 shorter events, 0.0 us)
Async XLA Ops:
  1.8 8.5 %collective-permute-start = (f32[12,512]{1,0:T(8,128)S(1)}, f32[12,512]{1,0:T(8,128)S(1)}, u32[]{:S(2)}, u32[]{:S(2)}) collective-permute-start(f32[12,512]{1,0:T(8,128)S(1)} %get-tuple-element.29), channel_id=1, source_target_pairs={{0,1},{1,0},{2,3},{3,2},{4,5},{5,4},{6,7},{7,6},{8,9},{9,8},{10,11... | collective-permute-start | bytes 73736 | tf_op jit(solution)/shard_map/ppermute | solution.py:588
  5.2 5.2 %collective-permute-start.1 = (f32[12,512]{1,0:T(8,128)S(1)}, f32[12,512]{1,0:T(8,128)S(1)}, u32[]{:S(2)}, u32[]{:S(2)}) collective-permute-start(f32[12,512]{1,0:T(8,128)S(1)} %get-tuple-element.30), channel_id=1, source_target_pairs={{1,2},{3,4},{5,6},{7,8},{9,10},{11,12},{13,14},{15,16},{17,18},{19... | collective-permute-start | bytes 73736 | tf_op jit(solution)/shard_map/ppermute | solution.py:594
  10.4 3.3 %copy-start = (s32[32,128]{1,0:T(8,128)S(1)}, s32[32,128]{1,0:T(8,128)}, u32[]{:S(2)}) copy-start(s32[32,128]{1,0:T(8,128)} %cell_ref.1) | copy-start | bytes 49156
  10.4 3.3 %copy-start.1 = (f32[32,128]{1,0:T(8,128)S(1)}, f32[32,128]{1,0:T(8,128)}, u32[]{:S(2)}) copy-start(f32[32,128]{1,0:T(8,128)} %keep_ref.1) | copy-start | bytes 49156
  10.4 3.3 %copy-start.2 = (f32[32,128]{1,0:T(8,128)S(1)}, f32[32,128]{1,0:T(8,128)}, u32[]{:S(2)}) copy-start(f32[32,128]{1,0:T(8,128)} %forcing_ref.1) | copy-start | bytes 49156
  13.6 1.4 %collective-permute-start.2 = (f32[128,256]{1,0:T(8,128)S(1)}, f32[128,256]{1,0:T(8,128)S(1)}, u32[]{:S(2)}, u32[]{:S(2)}) collective-permute-start(f32[128,256]{1,0:T(8,128)S(1)} %get-tuple-element.41), channel_id=1, source_target_pairs={{0,1},{1,0},{2,3},{3,2},{4,5},{5,4},{6,7},{7,6},{8,9},{9,8},{10,11... | collective-permute-start | bytes 393224 | tf_op jit(solution)/shard_map/ppermute | solution.py:588

commit v5 on v4

--- a/solution.py
+++ b/solution.py
@@ -402,6 +402,9 @@
     cell_ref,
 ):
     first_core = lax.axis_index("core") == 0
+    chip_index, chips = lax.axis_index("chip"), lax.axis_size("chip")
+    has_low = jnp.where(first_core & (chip_index == 0), 0.0, 1.0)
+    has_high = jnp.where(first_core | (chip_index < chips - 1), 1.0, 0.0)
     rows = depth_ref.shape[0]
     near = RIM + HALO
 
@@ -410,6 +413,8 @@
         chip, away = chip_ref[halo, :], away_ref[halo, :]
         low = jnp.where(first_core, away, chip)
         high = jnp.where(first_core, chip, away)
+        if part == 1:
+            low, high = low * has_low, high * has_high
         return jnp.concatenate([low, ref[0:near, :], ref[rows - near : rows, :], high], axis=0)
 
     rim_grad, rim_adjoint = window(rim(0, depth_ref), rim(1, rough_ref_), rim(2, seed_ref))
@@ -589,9 +594,9 @@
 
 
 def exchanged_away(value):
-    chips, cores = lax.axis_size("chip"), lax.axis_size("core")
-    edges = [(i, i + 1) for i in range(1, chips * cores - 1, 2)]
-    return lax.ppermute(value, ("chip", "core"), edges + [(j, i) for i, j in edges])
+    tiles = lax.axis_size("chip") * lax.axis_size("core")
+    pairs = [(i, (i + 1 if i % 2 else i - 1) % tiles) for i in range(tiles)]
+    return lax.ppermute(value, ("chip", "core"), pairs)
 
 
 def per_device(

time: 45 us -> 44 us (0.978)
  blocking collectives: 29.2 us -> 23.5 us
  starting transfers between devices: 5.33 us -> 10.1 us
    ppermute x2, starting transfers between devices: 3.42 us -> 10.1 us  [swapped(): return lax.ppermute(value, 'core', [(0, 1), (1, 0)])]
    all_to_all x1, blocking collectives: 29.2 us -> 23.5 us  [per_device(): arrived = lax.all_to_all(sent, ('basin', 'chip'), 0, 0, tiled=True)]
    ppermute x1, starting transfers between devices: 1.91 us -> 0.01 us  [exchanged_away(): return lax.ppermute(value, ('chip', 'core'), pairs)]
where the time goes in v5:
time: 44 us; the launch traced here: 43.6 us
  blocking collectives  23.5 us (53%)
  starting transfers between devices  10.1 us (23%)
  Pallas kernels  9.15 us (21%)
  between operations  0.66 us (2%)
    all_to_all x1, blocking collectives, per_device(): arrived = lax.all_to_all(sent, ('basin', 'chip'), 0, 0, tiled=True)  23.5 us
    ppermute x2, starting transfers between devices, swapped(): return lax.ppermute(value, 'core', [(0, 1), (1, 0)])  10.1 us
    pallas_call x1, Pallas kernels, zone_partials(): pl.pallas_call(zone_kernel, out_shape=(half, half, jax.ShapeDtypeStruct(d...  3.18 us
    pallas_call x1, Pallas kernels, slots_of(): pl.pallas_call(slot_kernel, out_shape=(jax.ShapeDtypeStruct((count, LANES...  1.68 us
    pallas_call x1, Pallas kernels, inner_part(): pl.pallas_call(inner_kernel, out_shape=(shape, shape, jax.ShapeDtypeStruc...  1.56 us
    pallas_call x1, Pallas kernels, fetched(): pl.pallas_call(front_kernel, out_shape=kept + (edge, edge), in_specs=[HBM...  1.21 us
  transfers between devices with their start and end apart: 3, of which 2 were waited for; matrix products, arithmetic and copies ran while one was open for 0% of the time, Pallas kernels for 9%

profile of v5, /device:TPU:1, one launch (start us, length us, event | category | flops | bytes accessed | tf_op | source)
XLA Modules:
  0.0 43.6 jit_solution(11347084929285809754)
XLA Ops:
  0.6 1.2 %fetch_and_edges.1 = (f32[64,512]{1,0:T(8,128)S(1)}, f32[64,512]{1,0:T(8,128)S(1)}, f32[64,512]{1,0:T(8,128)S(1)}, s32[64,512]{1,0:T(8,128)S(1)}, s32[254,128]{1...) custom-call(f32[64,512]{1,0:T(8,128)} %bitcast.11, f32[64,512]{1,0:T(8,128)} %bitcast.12, ...), custom_call_target="tpu_custom_call" | custom-call | tf_op jit(solution)/shard_map/fetch_and_edges/pallas_call | solution.py:86
  1.8 3.3 %collective-permute-start = (f32[12,512]{1,0:T(8,128)S(1)}, f32[12,512]{1,0:T(8,128)S(1)}, u32[]{:S(2)}, u32[]{:S(2)}) collective-permute-start(f32[12,512]{1,0:T(8,128)S(1)} %get-tuple-element.29), channel_id=1, source_target_pairs={{0,1},{1,0},{2,3},{3,2},{4,5},{5,4},{6,7},{7,6},{8,9},{9,8},{10,11... | collective-permute-start | bytes 73736 | tf_op jit(solution)/shard_map/ppermute | solution.py:593
  5.2 0.0 collective-permute-start.1
  5.2 1.7 %slot_lookup.1 = (s32[256,128]{1,0:T(8,128)S(1)}, f32[256,128]{1,0:T(8,128)S(1)}, f32[256,128]{1,0:T(8,128)S(1)}, f32[8,128]{1,0:T(8,128)S(1)}) custom-call(s32[254,128]{1,0:T(8,128)S(1)} %get-tuple-element.35.owner_ref, s32[64,512]{1,0:T(8,128)S(1)} %get-tuple-element.31.label_ref), custom_call_target="tpu_custom_call" | custom-call | flops 1073741824 | bytes 524288 | tf_op jit(solution)/shard_map/slot_lookup/pallas_call | solution.py:205
  6.9 1.6 %inner_rows.1 = (f32[64,512]{1,0:T(8,128)S(1)}, f32[64,512]{1,0:T(8,128)S(1)}, f32[16,32]{1,0:T(8,128)S(1)}) custom-call(f32[64,512]{1,0:T(8,128)S(1)} %get-tuple-element.26.depth_ref, f32[64,512]{1,0:T(8,128)S(1)} %get-tuple-element.27.rough_ref_, f32[64,512]{1,0:T(8,128)S(1)} %get-tuple-element.28.seed_ref, s32[64,512]{1,0:T(8,128)S(1)} %get-tuple-element.31.label_ref), custom_call_target="tpu_custom_call" | custom-call | flops 1073741824 | bytes 655360 | tf_op jit(solution)/shard_map/inner_rows/pallas_call | solution.py:369
  8.4 0.0 collective-permute-done.chip_ref
  8.4 0.1 collective-permute-done.1.away_ref
  8.5 0.0 copy-start
  8.5 0.0 copy-start.1
  8.5 0.0 copy-start.2
  8.5 3.2 %zone_partials.1 = (f32[128,256]{1,0:T(8,128)S(1)}, f32[128,256]{1,0:T(8,128)S(1)}, f32[64,512]{1,0:T(8,128)S(1)}) custom-call(f32[64,512]{1,0:T(8,128)S(1)} %get-tuple-element.26.depth_ref, f32[64,512]{1,0:T(8,128)S(1)} %get-tuple-element.27.rough_ref_, f32[64,512]{1,0:T(8,128)S(1)} %get-tuple-element.28.seed_ref, ...), custom_call_target="tpu_custom_call" | custom-call | tf_op jit(solution)/shard_map/zone_partials/pallas_call | solution.py:482
  11.7 6.7 %collective-permute-start.2 = (f32[128,256]{1,0:T(8,128)S(1)}, f32[128,256]{1,0:T(8,128)S(1)}, u32[]{:S(2)}, u32[]{:S(2)}) collective-permute-start(f32[128,256]{1,0:T(8,128)S(1)} %get-tuple-element.41), channel_id=1, source_target_pairs={{0,1},{1,0},{2,3},{3,2},{4,5},{5,4},{6,7},{7,6},{8,9},{9,8},{10,11... | collective-permute-start | bytes 393224 | tf_op jit(solution)/shard_map/ppermute | solution.py:593
  18.4 0.0 copy-done
  18.4 0.0 copy-done.1
  18.4 0.0 copy-done.2
  18.4 0.8 %reach_maps.1 = (f32[32,128]{1,0:T(8,128)S(1)}, f32[32,128]{1,0:T(8,128)S(1)}, f32[2,128]{1,0:T(2,128)S(1)}) custom-call(f32[64,512]{1,0:T(8,128)S(1)} %get-tuple-element.42.adjoint_ref, s32[32,128]{1,0:T(8,128)S(1)} %copy-done, f32[32,128]{1,0:T(8,128)S(1)} %copy-done.1, f32[32,128]{1,0:T(8,128)S(1)} %copy-done.2), custom_call_target="tpu_custom_call" | custom-call | tf_op jit(solution)/shard_map/reach_maps/pallas_call | solution.py:582
  19.3 0.2 collective-permute-done.2.other_ref
  19.4 23.5 %all_to_all.5 = f32[128,4,128]{2,1,0:T(4,128)S(1)} all-to-all(f32[128,4,128]{2,1,0:T(4,128)S(1)} %bitcast.10), channel_id=1, replica_groups=mesh['basin'=4,'chip'=32,'core'=2] {'basin','chip'}, dimensions={0} | all-to-all | bytes 524288 | tf_op jit(solution)/shard_map/all_to_all | solution.py:622
  43.0 0.7 %results.1 = (f32[1,127]{1,0:T(1,128)}, f32[1,127]{1,0:T(1,128)}, f32[32,128]{1,0:T(8,128)}) custom-call(f32[512,128]{1,0:T(8,128)S(1)} %bitcast.9, f32[32,128]{1,0:T(8,128)S(1)} %get-tuple-element.44.rate_ref, f32[32,128]{1,0:T(8,128)S(1)} %get-tuple-element.45.push_ref), custom_call_target="tpu_custom_call" | custom-call | tf_op jit(solution)/shard_map/results/pallas_call | solution.py:539
  (1 shorter events, 0.0 us)
Async XLA Ops:
  1.8 6.6 %collective-permute-start = (f32[12,512]{1,0:T(8,128)S(1)}, f32[12,512]{1,0:T(8,128)S(1)}, u32[]{:S(2)}, u32[]{:S(2)}) collective-permute-start(f32[12,512]{1,0:T(8,128)S(1)} %get-tuple-element.29), channel_id=1, source_target_pairs={{0,1},{1,0},{2,3},{3,2},{4,5},{5,4},{6,7},{7,6},{8,9},{9,8},{10,11... | collective-permute-start | bytes 73736 | tf_op jit(solution)/shard_map/ppermute | solution.py:593
  5.2 3.3 %collective-permute-start.1 = (f32[12,512]{1,0:T(8,128)S(1)}, f32[12,512]{1,0:T(8,128)S(1)}, u32[]{:S(2)}, u32[]{:S(2)}) collective-permute-start(f32[12,512]{1,0:T(8,128)S(1)} %get-tuple-element.30), channel_id=1, source_target_pairs={{0,63},{1,2},{2,1},{3,4},{4,3},{5,6},{6,5},{7,8},{8,7},{9,10},{10,... | collective-permute-start | bytes 73736 | tf_op jit(solution)/shard_map/ppermute | solution.py:599
  8.5 9.9 %copy-start = (s32[32,128]{1,0:T(8,128)S(1)}, s32[32,128]{1,0:T(8,128)}, u32[]{:S(2)}) copy-start(s32[32,128]{1,0:T(8,128)} %cell_ref.1) | copy-start | bytes 49156
  8.5 9.9 %copy-start.1 = (f32[32,128]{1,0:T(8,128)S(1)}, f32[32,128]{1,0:T(8,128)}, u32[]{:S(2)}) copy-start(f32[32,128]{1,0:T(8,128)} %keep_ref.1) | copy-start | bytes 49156
  8.5 9.9 %copy-start.2 = (f32[32,128]{1,0:T(8,128)S(1)}, f32[32,128]{1,0:T(8,128)}, u32[]{:S(2)}) copy-start(f32[32,128]{1,0:T(8,128)} %forcing_ref.1) | copy-start | bytes 49156
  11.7 7.7 %collective-permute-start.2 = (f32[128,256]{1,0:T(8,128)S(1)}, f32[128,256]{1,0:T(8,128)S(1)}, u32[]{:S(2)}, u32[]{:S(2)}) collective-permute-start(f32[128,256]{1,0:T(8,128)S(1)} %get-tuple-element.41), channel_id=1, source_target_pairs={{0,1},{1,0},{2,3},{3,2},{4,5},{5,4},{6,7},{7,6},{8,9},{9,8},{10,11... | collective-permute-start | bytes 393224 | tf_op jit(solution)/shard_map/ppermute | solution.py:593

commit v6 on v5

--- a/solution.py
+++ b/solution.py
@@ -97,13 +97,37 @@
 ABSENT = 2**15 - 1
 
 
+def split_rows(x):
+    rows = x.shape[0]
+    inner = stacked(x[RIM : rows - RIM])
+    rim = stacked(jnp.concatenate([x[:RIM], x[rows - RIM :]], axis=0))
+    return inner, rim
+
+
+def compacted(x, moves):
+    bit = 0
+    while 2**bit < x.shape[0]:
+        x = jnp.where((moves & 2**bit) != 0, from_below(x, 2**bit), x)
+        bit += 1
+    return x
+
+
+def set_strays(stray_ref, grad, moves):
+    grad = compacted(grad, moves)
+    stray_ref[0], stray_ref[1] = halves(grad)
+    stray_ref[2], stray_ref[3] = halves(grad * grad)
+
+
 def own_first_zone():
     chip = lax.axis_index("basin") * lax.axis_size("chip") + lax.axis_index("chip")
     return (chip * lax.axis_size("core") + lax.axis_index("core")) * SPAN
 
 
-BASE_ROWS = 48
-CHUNK = 8
+INNER_ROWS = 40
+RIM_ROWS = 16
+INNER_STEP = 8
+RIM_STEP = 4
+RIM = 2 * HALO
 
 
 def slot_kernel(
@@ -144,33 +168,43 @@
     home_ref[0:1, :] = home_device[0:1]
     home_ref[1:2, :] = home_lane[0:1]
 
-    label = stacked(label_ref[...])
-    count = label.shape[0]
-    offset = label - first_zone
-    at_home = (offset >= 0) & (offset < SPAN)
-    at_home_count = jnp.where(at_home, 1.0, 0.0)
-    row_ids = lax.broadcasted_iota(jnp.int32, (count, count), 0)
-    column_ids = lax.broadcasted_iota(jnp.int32, (count, count), 1)
-    earlier = jnp.where(column_ids < row_ids, 1.0, 0.0).astype(jnp.bfloat16)
-    gaps = jnp.dot(
-        earlier, at_home_count.astype(jnp.bfloat16), preferred_element_type=jnp.float32
-    ).astype(jnp.int32)
-    packed = jnp.where(at_home, ABSENT, gaps * (ABSENT + 1) + label)
-    moves = jnp.zeros(packed.shape, jnp.int32)
-    bit = 0
-    while 2**bit < count:
-        marker = (ABSENT + 1) * 2**bit
-        near = from_below(packed, 2**bit)
-        taken = (near & marker) != 0
-        left = (packed & marker) != 0
-        packed = jnp.where(taken, near, jnp.where(left, ABSENT, packed))
-        moves = jnp.where(taken, moves + 2**bit, moves)
-        bit += 1
-    moves_ref[...] = moves
-    packed_ref[...] = packed & ABSENT
-    most = count - jnp.min(jnp.sum(at_home_count, axis=0, keepdims=True)).astype(jnp.int32)
-    chunks = jnp.maximum((most - BASE_ROWS + CHUNK - 1) // CHUNK, 0)
-    home_ref[2:3, :] = jnp.full((1, LANES), chunks.astype(jnp.float32))
+    def compact(label):
+        count = label.shape[0]
+        offset = label - first_zone
+        at_home = (offset >= 0) & (offset < SPAN)
+        at_home_count = jnp.where(at_home, 1.0, 0.0)
+        row_ids = lax.broadcasted_iota(jnp.int32, (count, count), 0)
+        column_ids = lax.broadcasted_iota(jnp.int32, (count, count), 1)
+        earlier = jnp.where(column_ids < row_ids, 1.0, 0.0).astype(jnp.bfloat16)
+        gaps = jnp.dot(
+            earlier, at_home_count.astype(jnp.bfloat16), preferred_element_type=jnp.float32
+        ).astype(jnp.int32)
+        packed = jnp.where(at_home, ABSENT, gaps * (ABSENT + 1) + label)
+        moves = jnp.zeros(packed.shape, jnp.int32)
+        bit = 0
+        while 2**bit < count:
+            marker = (ABSENT + 1) * 2**bit
+            near = from_below(packed, 2**bit)
+            taken = (near & marker) != 0
+            left = (packed & marker) != 0
+            packed = jnp.where(taken, near, jnp.where(left, ABSENT, packed))
+            moves = jnp.where(taken, moves + 2**bit, moves)
+            bit += 1
+        most = count - jnp.min(jnp.sum(at_home_count, axis=0, keepdims=True)).astype(jnp.int32)
+        return packed & ABSENT, moves, most
+
+    inner_label, rim_label = split_rows(label_ref[...])
+    inner_count = inner_label.shape[0]
+    packed, moves, inner_most = compact(inner_label)
+    packed_ref[0:inner_count, :] = packed
+    moves_ref[0:inner_count, :] = moves
+    packed, moves, rim_most = compact(rim_label)
+    packed_ref[inner_count:, :] = packed
+    moves_ref[inner_count:, :] = moves
+    inner_steps = jnp.maximum((inner_most - INNER_ROWS + INNER_STEP - 1) // INNER_STEP, 0)
+    rim_steps = jnp.maximum((rim_most - RIM_ROWS + RIM_STEP - 1) // RIM_STEP, 0)
+    home_ref[2:3, :] = jnp.full((1, LANES), inner_steps.astype(jnp.float32))
+    home_ref[3:4, :] = jnp.full((1, LANES), rim_steps.astype(jnp.float32))
 
     def look_up(first, rows):
         for start in range(0, rows, 4):
@@ -191,12 +225,18 @@
                 device_ref[place, :] = owner[:, i * LANES : (i + 1) * LANES]
                 lane_ref[place, :] = lane[:, i * LANES : (i + 1) * LANES]
 
-    def one_chunk(index, carry):
-        look_up(BASE_ROWS + index * CHUNK, CHUNK)
+    def more_inner(index, carry):
+        look_up(INNER_ROWS + index * INNER_STEP, INNER_STEP)
         return carry
 
-    look_up(0, BASE_ROWS)
-    lax.fori_loop(0, chunks, one_chunk, 0)
+    def more_rim(index, carry):
+        look_up(inner_count + RIM_ROWS + index * RIM_STEP, RIM_STEP)
+        return carry
+
+    look_up(0, INNER_ROWS)
+    look_up(inner_count, RIM_ROWS)
+    lax.fori_loop(0, inner_steps, more_inner, 0)
+    lax.fori_loop(0, rim_steps, more_rim, 0)
 
 
 def slots_of(owner_slot, label):
@@ -346,38 +386,75 @@
     )
 
 
-RIM = 2 * HALO
+def stray_rows(refs, first, start, count):
+    device_ref, lane_ref, stray_ref = refs
+    rows = []
+    for step in range(count):
+        slot = pl.ds(first + start + step, 1)
+        value = pl.ds(start + step, 1)
+        values = [stray_ref[part, value, :] for part in range(4)]
+        rows.append((device_ref[slot, :], lane_ref[slot, :], *values))
+    return rows
 
 
 def inner_kernel(
-    depth_ref, rough_ref_, seed_ref, label_ref, grad_ref, adjoint_ref, home_ref, cell_ref
+    depth_ref,
+    rough_ref_,
+    seed_ref,
+    label_ref,
+    moves_ref,
+    device_ref,
+    lane_ref,
+    home_ref,
+    total_ref,
+    adjoint_ref,
+    products_ref,
+    cell_ref,
+    stray_ref,
 ):
     grad, adjoint = window(depth_ref[...], rough_ref_[...], seed_ref[...])
-    grad_ref[...] = grad
     adjoint_ref[...] = adjoint
     rows = grad.shape[0]
     inside = slice(RIM, rows - RIM)
+    inner_grad, _ = split_rows(grad)
+    set_strays(stray_ref, inner_grad, moves_ref[0 : inner_grad.shape[0], :])
     set_cells(cell_ref, (label_ref[...] - own_first_zone())[inside], grad[inside])
     home = home_products(cell_ref, 0, HOME_ROWS)
     for first in range(HOME_ROWS, rows - 2 * RIM, HOME_ROWS):
         home = home + home_products(cell_ref, first, HOME_ROWS)
-    home_ref[...] = home
-
-
-def inner_part(depth, rough, seed, label):
-    shape = jax.ShapeDtypeStruct(depth.shape, jnp.float32)
+    products_ref[...] = home
+    refs = device_ref, lane_ref, stray_ref
+    total_ref[...] = zone_sums(stray_rows(refs, 0, 0, INNER_ROWS))
+
+    def more(index, carry):
+        start = INNER_ROWS + index * INNER_STEP
+        total_ref[...] += zone_sums(stray_rows(refs, 0, start, INNER_STEP))
+        return carry
+
+    lax.fori_loop(0, jnp.max(home_ref[2:3, :]).astype(jnp.int32), more, 0)
+
+
+def inner_part(depth, rough, seed, label, *slots):
+    inner_rows = depth.shape[0] - 2 * RIM
     return pl.pallas_call(
         inner_kernel,
-        out_shape=(shape, shape, jax.ShapeDtypeStruct((16, 32), jnp.float32)),
-        in_specs=[VMEM] * 4,
+        out_shape=(
+            jax.ShapeDtypeStruct((256, 2 * LANES), jnp.float32),
+            jax.ShapeDtypeStruct(depth.shape, jnp.float32),
+            jax.ShapeDtypeStruct((16, 32), jnp.float32),
+        ),
+        in_specs=[VMEM] * (4 + len(slots)),
         out_specs=(VMEM,) * 3,
-        scratch_shapes=[pltpu.VMEM((6, depth.shape[0] - 2 * RIM, depth.shape[1]), jnp.float32)],
+        scratch_shapes=[
+            pltpu.VMEM((6, inner_rows, depth.shape[1]), jnp.float32),
+            pltpu.VMEM((4, inner_rows * depth.shape[1] // LANES, LANES), jnp.float32),
+        ],
         compiler_params=ROOMY,
         cost_estimate=pl.CostEstimate(
-            flops=2 * 256 * 64 * depth.size, bytes_accessed=20 * depth.size, transcendentals=0
+            flops=2 * 256 * 128 * depth.size, bytes_accessed=20 * depth.size, transcendentals=0
         ),
         name="inner_rows",
-    )(depth, rough, seed, label)
+    )(depth, rough, seed, label, *slots)
 
 
 def zone_kernel(
@@ -386,7 +463,7 @@
     seed_ref,
     chip_ref,
     away_ref,
-    inner_grad_ref,
+    inner_total_ref,
     inner_adjoint_ref,
     inner_home_ref,
     label_ref,
@@ -430,17 +507,9 @@
         jnp.concatenate([offset[:RIM], offset[rows - RIM :]], axis=0),
         jnp.concatenate([rim_grad[top], rim_grad[bottom]], axis=0),
     )
-    grad = jnp.concatenate(
-        [rim_grad[top], inner_grad_ref[inside, :], rim_grad[bottom]], axis=0
-    )
-    grad = stacked(grad)
-    moves = moves_ref[...]
-    bit = 0
-    while 2**bit < grad.shape[0]:
-        grad = jnp.where((moves & 2**bit) != 0, from_below(grad, 2**bit), grad)
-        bit += 1
-    stray_ref[0], stray_ref[1] = halves(grad)
-    stray_ref[2], stray_ref[3] = halves(grad * grad)
+    first = moves_ref.shape[0] - stray_ref.shape[1]
+    rim_grad = jnp.concatenate([rim_grad[top], rim_grad[bottom]], axis=0)
+    set_strays(stray_ref, stacked(rim_grad), moves_ref[first:, :])
     home = inner_home_ref[...] + home_products(cell_ref, 0, 2 * RIM)
     part = lax.broadcasted_iota(jnp.int32, (32, 2 * LANES), 0)
     zone = lax.broadcasted_iota(jnp.int32, (32, 2 * LANES), 1)
@@ -456,23 +525,17 @@
     home = jnp.sum(jnp.where(((zone >> 3) & 15) == group, home, 0.0), axis=0, keepdims=True)
     home = halves(home[:, :LANES]) + halves(home[:, LANES:])
 
-    def stray_rows(start, count):
-        rows = [pl.ds(start + step, 1) for step in range(count)]
-        return [
-            (device_ref[row, :], lane_ref[row, :], *(stray_ref[i, row, :] for i in range(4)))
-            for row in rows
-        ]
-
-    total_ref[...] = zone_sums(
-        stray_rows(0, BASE_ROWS) + [(home_ref[0:1, :], home_ref[1:2, :], *home)]
-    )
-
-    def one_chunk(index, carry):
-        total_ref[...] += zone_sums(stray_rows(BASE_ROWS + index * CHUNK, CHUNK))
+    refs = device_ref, lane_ref, stray_ref
+    total_ref[...] = inner_total_ref[...] + zone_sums(
+        stray_rows(refs, first, 0, RIM_ROWS) + [(home_ref[0:1, :], home_ref[1:2, :], *home)]
+    )
+
+    def more(index, carry):
+        start = RIM_ROWS + index * RIM_STEP
+        total_ref[...] += zone_sums(stray_rows(refs, first, start, RIM_STEP))
         return carry
 
-    chunks = jnp.max(home_ref[2:3, :]).astype(jnp.int32)
-    lax.fori_loop(0, chunks, one_chunk, 0)
+    lax.fori_loop(0, jnp.max(home_ref[3:4, :]).astype(jnp.int32), more, 0)
     own_ref[...] = total_ref[0:LANES, :]
     other_ref[...] = total_ref[LANES:, :]
 
@@ -486,7 +549,7 @@
         out_specs=(VMEM,) * 3,
         scratch_shapes=[
             pltpu.VMEM((256, 2 * LANES), jnp.float32),
-            pltpu.VMEM((4, depth.size // LANES, LANES), jnp.float32),
+            pltpu.VMEM((4, 2 * RIM * depth.shape[1] // LANES, LANES), jnp.float32),
             pltpu.VMEM((6, 2 * RIM, depth.shape[1]), jnp.float32),
         ],
         compiler_params=ROOMY,
@@ -612,7 +675,7 @@
     from_away = exchanged_away(to_away)
     from_chip = swapped(to_chip)
     moves, device, lane, home = slots_of(owner_slot, label)
-    inner = inner_part(depth, rough, seed, label)
+    inner = inner_part(depth, rough, seed, label, moves, device, lane, home)
     own, other, adjoint = zone_partials(
         depth, rough, seed, from_chip, from_away, *inner, label, moves, device, lane, home
     )

time: 44 us -> 43.1 us (0.980)
  blocking collectives: 23.5 us -> 22.2 us
    pallas_call x1, Pallas kernels: 1.56 us -> 3 us  [inner_part(): pl.pallas_call(inner_kernel, out_shape=(jax.ShapeDtypeStruct((256, 2 * LA...]
    all_to_all x1, blocking collectives: 23.5 us -> 22.2 us  [per_device(): arrived = lax.all_to_all(sent, ('basin', 'chip'), 0, 0, tiled=True)]
    pallas_call x1, Pallas kernels: 3.18 us -> 1.95 us  [zone_partials(): pl.pallas_call(zone_kernel, out_shape=(half, half, jax.ShapeDtypeStruct(d...]
  transfers between devices with their start and end apart: 3 -> 3, of which waited for: 2 -> 1; matrix products, arithmetic and copies ran while one was open for 0% -> 0% of each run, Pallas kernels for 9% -> 13%
where the time goes in v6:
time: 43.1 us; the launch traced here: 42.6 us
  blocking collectives  22.2 us (52%)
  starting transfers between devices  10.1 us (23%)
  Pallas kernels  9.44 us (22%)
  between operations  0.71 us (2%)
    all_to_all x1, blocking collectives, per_device(): arrived = lax.all_to_all(sent, ('basin', 'chip'), 0, 0, tiled=True)  22.2 us
    ppermute x2, starting transfers between devices, swapped(): return lax.ppermute(value, 'core', [(0, 1), (1, 0)])  10.1 us
    pallas_call x1, Pallas kernels, inner_part(): pl.pallas_call(inner_kernel, out_shape=(jax.ShapeDtypeStruct((256, 2 * LA...  3 us
    pallas_call x1, Pallas kernels, zone_partials(): pl.pallas_call(zone_kernel, out_shape=(half, half, jax.ShapeDtypeStruct(d...  1.95 us
    pallas_call x1, Pallas kernels, slots_of(): pl.pallas_call(slot_kernel, out_shape=(jax.ShapeDtypeStruct((count, LANES...  1.77 us
    pallas_call x1, Pallas kernels, fetched(): pl.pallas_call(front_kernel, out_shape=kept + (edge, edge), in_specs=[HBM...  1.21 us
  transfers between devices with their start and end apart: 3, of which 1 were waited for; matrix products, arithmetic and copies ran while one was open for 0% of the time, Pallas kernels for 13%

profile of v6, /device:TPU:1, one launch (start us, length us, event | category | flops | bytes accessed | tf_op | source)
XLA Modules:
  0.0 42.6 jit_solution(14105119958197216313)
XLA Ops:
  0.6 1.2 %fetch_and_edges.1 = (f32[64,512]{1,0:T(8,128)S(1)}, f32[64,512]{1,0:T(8,128)S(1)}, f32[64,512]{1,0:T(8,128)S(1)}, s32[64,512]{1,0:T(8,128)S(1)}, s32[254,128]{1...) custom-call(f32[64,512]{1,0:T(8,128)} %bitcast.11, f32[64,512]{1,0:T(8,128)} %bitcast.12, ...), custom_call_target="tpu_custom_call" | custom-call | tf_op jit(solution)/shard_map/fetch_and_edges/pallas_call | solution.py:86
  1.8 3.3 %collective-permute-start = (f32[12,512]{1,0:T(8,128)S(1)}, f32[12,512]{1,0:T(8,128)S(1)}, u32[]{:S(2)}, u32[]{:S(2)}) collective-permute-start(f32[12,512]{1,0:T(8,128)S(1)} %get-tuple-element.29), channel_id=1, source_target_pairs={{0,1},{1,0},{2,3},{3,2},{4,5},{5,4},{6,7},{7,6},{8,9},{9,8},{10,11... | collective-permute-start | bytes 73736 | tf_op jit(solution)/shard_map/ppermute | solution.py:656
  5.2 0.0 collective-permute-start.1
  5.2 1.8 %slot_lookup.1 = (s32[256,128]{1,0:T(8,128)S(1)}, f32[256,128]{1,0:T(8,128)S(1)}, f32[256,128]{1,0:T(8,128)S(1)}, f32[8,128]{1,0:T(8,128)S(1)}) custom-call(s32[254,128]{1,0:T(8,128)S(1)} %get-tuple-element.32.owner_ref, s32[64,512]{1,0:T(8,128)S(1)} %get-tuple-element.31.label_ref), custom_call_target="tpu_custom_call" | custom-call | flops 1073741824 | bytes 524288 | tf_op jit(solution)/shard_map/slot_lookup/pallas_call | solution.py:245
  7.0 3.0 %inner_rows.1 = (f32[256,256]{1,0:T(8,128)S(1)}, f32[64,512]{1,0:T(8,128)S(1)}, f32[16,32]{1,0:T(8,128)S(1)}) custom-call(f32[64,512]{1,0:T(8,128)S(1)} %get-tuple-element.26.depth_ref, f32[64,512]{1,0:T(8,128)S(1)} %get-tuple-element.27.rough_ref_, f32[64,512]{1,0:T(8,128)S(1)} %get-tuple-element.28.seed_ref, s32[64,512]{1,0:T(8,128)S(1)} %get-tuple-element.31.label_ref, ...), custom_call_target="tpu_custom_call" | custom-call | flops 2147483648 | bytes 655360 | tf_op jit(solution)/shard_map/inner_rows/pallas_call | solution.py:439
  10.0 0.0 collective-permute-done.chip_ref
  10.0 0.0 collective-permute-done.1.away_ref
  10.0 0.0 copy-start
  10.0 0.0 copy-start.1
  10.0 0.0 copy-start.2
  10.0 1.9 %zone_partials.1 = (f32[128,256]{1,0:T(8,128)S(1)}, f32[128,256]{1,0:T(8,128)S(1)}, f32[64,512]{1,0:T(8,128)S(1)}) custom-call(f32[64,512]{1,0:T(8,128)S(1)} %get-tuple-element.26.depth_ref, f32[64,512]{1,0:T(8,128)S(1)} %get-tuple-element.27.rough_ref_, f32[64,512]{1,0:T(8,128)S(1)} %get-tuple-element.28.seed_ref, ...), custom_call_target="tpu_custom_call" | custom-call | tf_op jit(solution)/shard_map/zone_partials/pallas_call | solution.py:545
  12.0 6.8 %collective-permute-start.2 = (f32[128,256]{1,0:T(8,128)S(1)}, f32[128,256]{1,0:T(8,128)S(1)}, u32[]{:S(2)}, u32[]{:S(2)}) collective-permute-start(f32[128,256]{1,0:T(8,128)S(1)} %get-tuple-element.41), channel_id=1, source_target_pairs={{0,1},{1,0},{2,3},{3,2},{4,5},{5,4},{6,7},{7,6},{8,9},{9,8},{10,11... | collective-permute-start | bytes 393224 | tf_op jit(solution)/shard_map/ppermute | solution.py:656
  18.7 0.0 copy-done
  18.7 0.0 copy-done.1
  18.7 0.0 copy-done.2
  18.7 0.8 %reach_maps.1 = (f32[32,128]{1,0:T(8,128)S(1)}, f32[32,128]{1,0:T(8,128)S(1)}, f32[2,128]{1,0:T(2,128)S(1)}) custom-call(f32[64,512]{1,0:T(8,128)S(1)} %get-tuple-element.42.adjoint_ref, s32[32,128]{1,0:T(8,128)S(1)} %copy-done, f32[32,128]{1,0:T(8,128)S(1)} %copy-done.1, f32[32,128]{1,0:T(8,128)S(1)} %copy-done.2), custom_call_target="tpu_custom_call" | custom-call | tf_op jit(solution)/shard_map/reach_maps/pallas_call | solution.py:645
  19.6 0.2 collective-permute-done.2.other_ref
  19.8 22.2 %all_to_all.5 = f32[128,4,128]{2,1,0:T(4,128)S(1)} all-to-all(f32[128,4,128]{2,1,0:T(4,128)S(1)} %bitcast.10), channel_id=1, replica_groups=mesh['basin'=4,'chip'=32,'core'=2] {'basin','chip'}, dimensions={0} | all-to-all | bytes 524288 | tf_op jit(solution)/shard_map/all_to_all | solution.py:685
  41.9 0.7 %results.1 = (f32[1,127]{1,0:T(1,128)}, f32[1,127]{1,0:T(1,128)}, f32[32,128]{1,0:T(8,128)}) custom-call(f32[512,128]{1,0:T(8,128)S(1)} %bitcast.9, f32[32,128]{1,0:T(8,128)S(1)} %get-tuple-element.44.rate_ref, f32[32,128]{1,0:T(8,128)S(1)} %get-tuple-element.45.push_ref), custom_call_target="tpu_custom_call" | custom-call | tf_op jit(solution)/shard_map/results/pallas_call | solution.py:602
  (1 shorter events, 0.0 us)
Async XLA Ops:
  1.8 8.1 %collective-permute-start = (f32[12,512]{1,0:T(8,128)S(1)}, f32[12,512]{1,0:T(8,128)S(1)}, u32[]{:S(2)}, u32[]{:S(2)}) collective-permute-start(f32[12,512]{1,0:T(8,128)S(1)} %get-tuple-element.29), channel_id=1, source_target_pairs={{0,1},{1,0},{2,3},{3,2},{4,5},{5,4},{6,7},{7,6},{8,9},{9,8},{10,11... | collective-permute-start | bytes 73736 | tf_op jit(solution)/shard_map/ppermute | solution.py:656
  5.2 4.8 %collective-permute-start.1 = (f32[12,512]{1,0:T(8,128)S(1)}, f32[12,512]{1,0:T(8,128)S(1)}, u32[]{:S(2)}, u32[]{:S(2)}) collective-permute-start(f32[12,512]{1,0:T(8,128)S(1)} %get-tuple-element.30), channel_id=1, source_target_pairs={{0,63},{1,2},{2,1},{3,4},{4,3},{5,6},{6,5},{7,8},{8,7},{9,10},{10,... | collective-permute-start | bytes 73736 | tf_op jit(solution)/shard_map/ppermute | solution.py:662
  10.0 8.8 %copy-start = (s32[32,128]{1,0:T(8,128)S(1)}, s32[32,128]{1,0:T(8,128)}, u32[]{:S(2)}) copy-start(s32[32,128]{1,0:T(8,128)} %cell_ref.1) | copy-start | bytes 49156
  10.0 8.8 %copy-start.1 = (f32[32,128]{1,0:T(8,128)S(1)}, f32[32,128]{1,0:T(8,128)}, u32[]{:S(2)}) copy-start(f32[32,128]{1,0:T(8,128)} %keep_ref.1) | copy-start | bytes 49156
  10.0 8.7 %copy-start.2 = (f32[32,128]{1,0:T(8,128)S(1)}, f32[32,128]{1,0:T(8,128)}, u32[]{:S(2)}) copy-start(f32[32,128]{1,0:T(8,128)} %forcing_ref.1) | copy-start | bytes 49156
  12.0 7.8 %collective-permute-start.2 = (f32[128,256]{1,0:T(8,128)S(1)}, f32[128,256]{1,0:T(8,128)S(1)}, u32[]{:S(2)}, u32[]{:S(2)}) collective-permute-start(f32[128,256]{1,0:T(8,128)S(1)} %get-tuple-element.41), channel_id=1, source_target_pairs={{0,1},{1,0},{2,3},{3,2},{4,5},{5,4},{6,7},{7,6},{8,9},{9,8},{10,11... | collective-permute-start | bytes 393224 | tf_op jit(solution)/shard_map/ppermute | solution.py:656

commit v7 on v6

--- a/solution.py
+++ b/solution.py
@@ -673,8 +673,9 @@
         owner_slot.reshape(-1, LANES),
     )
     from_away = exchanged_away(to_away)
+    moves, device, lane, home = slots_of(owner_slot, label)
+    to_chip, home = lax.optimization_barrier((to_chip, home))
     from_chip = swapped(to_chip)
-    moves, device, lane, home = slots_of(owner_slot, label)
     inner = inner_part(depth, rough, seed, label, moves, device, lane, home)
     own, other, adjoint = zone_partials(
         depth, rough, seed, from_chip, from_away, *inner, label, moves, device, lane, home

time: 43.1 us -> 43.3 us (level)
    ppermute x1, starting transfers between devices: 0.01 us -> 3.11 us  [exchanged_away(): return lax.ppermute(value, ('chip', 'core'), pairs)]
    ppermute x2, starting transfers between devices: 10.1 us -> 7.21 us  [swapped(): return lax.ppermute(value, 'core', [(0, 1), (1, 0)])]
where the time goes in v7:
time: 43.3 us; the launch traced here: 43.1 us
  blocking collectives  22.4 us (52%)
  starting transfers between devices  10.3 us (24%)
  Pallas kernels  9.43 us (22%)
  between operations  0.71 us (2%)
    all_to_all x1, blocking collectives, per_device(): arrived = lax.all_to_all(sent, ('basin', 'chip'), 0, 0, tiled=True)  22.4 us
    ppermute x2, starting transfers between devices, swapped(): return lax.ppermute(value, 'core', [(0, 1), (1, 0)])  7.21 us
    ppermute x1, starting transfers between devices, exchanged_away(): return lax.ppermute(value, ('chip', 'core'), pairs)  3.11 us
    pallas_call x1, Pallas kernels, inner_part(): pl.pallas_call(inner_kernel, out_shape=(jax.ShapeDtypeStruct((256, 2 * LA...  3 us
    pallas_call x1, Pallas kernels, zone_partials(): pl.pallas_call(zone_kernel, out_shape=(half, half, jax.ShapeDtypeStruct(d...  1.95 us
    pallas_call x1, Pallas kernels, slots_of(): pl.pallas_call(slot_kernel, out_shape=(jax.ShapeDtypeStruct((count, LANES...  1.76 us
    pallas_call x1, Pallas kernels, fetched(): pl.pallas_call(front_kernel, out_shape=kept + (edge, edge), in_specs=[HBM...  1.21 us
  transfers between devices with their start and end apart: 3, of which 1 were waited for; matrix products, arithmetic and copies ran while one was open for 0% of the time, Pallas kernels for 13%

profile of v7, /device:TPU:1, one launch (start us, length us, event | category | flops | bytes accessed | tf_op | source)
XLA Modules:
  0.0 43.1 jit_solution(4386400950648283262)
XLA Ops:
  0.6 1.2 %fetch_and_edges.1 = (f32[64,512]{1,0:T(8,128)S(1)}, f32[64,512]{1,0:T(8,128)S(1)}, f32[64,512]{1,0:T(8,128)S(1)}, s32[64,512]{1,0:T(8,128)S(1)}, s32[254,128]{1...) custom-call(f32[64,512]{1,0:T(8,128)} %bitcast.11, f32[64,512]{1,0:T(8,128)} %bitcast.12, ...), custom_call_target="tpu_custom_call" | custom-call | tf_op jit(solution)/shard_map/fetch_and_edges/pallas_call | solution.py:86
  1.8 3.1 %collective-permute-start.1 = (f32[12,512]{1,0:T(8,128)S(1)}, f32[12,512]{1,0:T(8,128)S(1)}, u32[]{:S(2)}, u32[]{:S(2)}) collective-permute-start(f32[12,512]{1,0:T(8,128)S(1)} %get-tuple-element.36), channel_id=1, source_target_pairs={{0,63},{1,2},{2,1},{3,4},{4,3},{5,6},{6,5},{7,8},{8,7},{9,10},{10,... | collective-permute-start | bytes 73736 | tf_op jit(solution)/shard_map/ppermute | solution.py:662
  5.0 1.8 %slot_lookup.1 = (s32[256,128]{1,0:T(8,128)S(1)}, f32[256,128]{1,0:T(8,128)S(1)}, f32[256,128]{1,0:T(8,128)S(1)}, f32[8,128]{1,0:T(8,128)S(1)}) custom-call(s32[254,128]{1,0:T(8,128)S(1)} %get-tuple-element.32.owner_ref, s32[64,512]{1,0:T(8,128)S(1)} %get-tuple-element.33.label_ref), custom_call_target="tpu_custom_call" | custom-call | flops 1073741824 | bytes 524288 | tf_op jit(solution)/shard_map/slot_lookup/pallas_call | solution.py:245
  6.7 6.6 %collective-permute-start = (f32[12,512]{1,0:T(8,128)S(1)}, f32[12,512]{1,0:T(8,128)S(1)}, u32[]{:S(2)}, u32[]{:S(2)}) collective-permute-start(f32[12,512]{1,0:T(8,128)S(1)} %get-tuple-element.35), channel_id=1, source_target_pairs={{0,1},{1,0},{2,3},{3,2},{4,5},{5,4},{6,7},{7,6},{8,9},{9,8},{10,11... | collective-permute-start | bytes 73736 | tf_op jit(solution)/shard_map/ppermute | solution.py:656
  13.4 3.0 %inner_rows.1 = (f32[256,256]{1,0:T(8,128)S(1)}, f32[64,512]{1,0:T(8,128)S(1)}, f32[16,32]{1,0:T(8,128)S(1)}) custom-call(f32[64,512]{1,0:T(8,128)S(1)} %get-tuple-element.28.depth_ref, f32[64,512]{1,0:T(8,128)S(1)} %get-tuple-element.29.rough_ref_, f32[64,512]{1,0:T(8,128)S(1)} %get-tuple-element.30.seed_ref, s32[64,512]{1,0:T(8,128)S(1)} %get-tuple-element.33.label_ref, ...), custom_call_target="tpu_custom_call" | custom-call | flops 2147483648 | bytes 655360 | tf_op jit(solution)/shard_map/inner_rows/pallas_call | solution.py:439
  16.4 0.0 collective-permute-done.1.away_ref
  16.4 0.0 collective-permute-done.chip_ref
  16.4 0.0 copy-start
  16.4 0.0 copy-start.1
  16.4 0.0 copy-start.2
  16.4 1.9 %zone_partials.1 = (f32[128,256]{1,0:T(8,128)S(1)}, f32[128,256]{1,0:T(8,128)S(1)}, f32[64,512]{1,0:T(8,128)S(1)}) custom-call(f32[64,512]{1,0:T(8,128)S(1)} %get-tuple-element.28.depth_ref, f32[64,512]{1,0:T(8,128)S(1)} %get-tuple-element.29.rough_ref_, f32[64,512]{1,0:T(8,128)S(1)} %get-tuple-element.30.seed_ref, ...), custom_call_target="tpu_custom_call" | custom-call | tf_op jit(solution)/shard_map/zone_partials/pallas_call | solution.py:545
  18.4 0.6 %collective-permute-start.2 = (f32[128,256]{1,0:T(8,128)S(1)}, f32[128,256]{1,0:T(8,128)S(1)}, u32[]{:S(2)}, u32[]{:S(2)}) collective-permute-start(f32[128,256]{1,0:T(8,128)S(1)} %get-tuple-element.45), channel_id=1, source_target_pairs={{0,1},{1,0},{2,3},{3,2},{4,5},{5,4},{6,7},{7,6},{8,9},{9,8},{10,11... | collective-permute-start | bytes 393224 | tf_op jit(solution)/shard_map/ppermute | solution.py:656
  19.0 0.0 copy-done
  19.0 0.0 copy-done.1
  19.0 0.0 copy-done.2
  19.0 0.8 %reach_maps.1 = (f32[32,128]{1,0:T(8,128)S(1)}, f32[32,128]{1,0:T(8,128)S(1)}, f32[2,128]{1,0:T(2,128)S(1)}) custom-call(f32[64,512]{1,0:T(8,128)S(1)} %get-tuple-element.46.adjoint_ref, s32[32,128]{1,0:T(8,128)S(1)} %copy-done, f32[32,128]{1,0:T(8,128)S(1)} %copy-done.1, f32[32,128]{1,0:T(8,128)S(1)} %copy-done.2), custom_call_target="tpu_custom_call" | custom-call | tf_op jit(solution)/shard_map/reach_maps/pallas_call | solution.py:645
  19.8 0.2 collective-permute-done.2.other_ref
  20.0 22.4 %all_to_all.5 = f32[128,4,128]{2,1,0:T(4,128)S(1)} all-to-all(f32[128,4,128]{2,1,0:T(4,128)S(1)} %bitcast.10), channel_id=1, replica_groups=mesh['basin'=4,'chip'=32,'core'=2] {'basin','chip'}, dimensions={0} | all-to-all | bytes 524288 | tf_op jit(solution)/shard_map/all_to_all | solution.py:686
  42.4 0.7 %results.1 = (f32[1,127]{1,0:T(1,128)}, f32[1,127]{1,0:T(1,128)}, f32[32,128]{1,0:T(8,128)}) custom-call(f32[512,128]{1,0:T(8,128)S(1)} %bitcast.9, f32[32,128]{1,0:T(8,128)S(1)} %get-tuple-element.48.rate_ref, f32[32,128]{1,0:T(8,128)S(1)} %get-tuple-element.49.push_ref), custom_call_target="tpu_custom_call" | custom-call | tf_op jit(solution)/shard_map/results/pallas_call | solution.py:602
  (1 shorter events, 0.0 us)
Async XLA Ops:
  1.8 14.5 %collective-permute-start.1 = (f32[12,512]{1,0:T(8,128)S(1)}, f32[12,512]{1,0:T(8,128)S(1)}, u32[]{:S(2)}, u32[]{:S(2)}) collective-permute-start(f32[12,512]{1,0:T(8,128)S(1)} %get-tuple-element.36), channel_id=1, source_target_pairs={{0,63},{1,2},{2,1},{3,4},{4,3},{5,6},{6,5},{7,8},{8,7},{9,10},{10,... | collective-permute-start | bytes 73736 | tf_op jit(solution)/shard_map/ppermute | solution.py:662
  6.7 9.6 %collective-permute-start = (f32[12,512]{1,0:T(8,128)S(1)}, f32[12,512]{1,0:T(8,128)S(1)}, u32[]{:S(2)}, u32[]{:S(2)}) collective-permute-start(f32[12,512]{1,0:T(8,128)S(1)} %get-tuple-element.35), channel_id=1, source_target_pairs={{0,1},{1,0},{2,3},{3,2},{4,5},{5,4},{6,7},{7,6},{8,9},{9,8},{10,11... | collective-permute-start | bytes 73736 | tf_op jit(solution)/shard_map/ppermute | solution.py:656
  16.4 2.6 %copy-start = (s32[32,128]{1,0:T(8,128)S(1)}, s32[32,128]{1,0:T(8,128)}, u32[]{:S(2)}) copy-start(s32[32,128]{1,0:T(8,128)} %cell_ref.1) | copy-start | bytes 49156
  16.4 2.6 %copy-start.1 = (f32[32,128]{1,0:T(8,128)S(1)}, f32[32,128]{1,0:T(8,128)}, u32[]{:S(2)}) copy-start(f32[32,128]{1,0:T(8,128)} %keep_ref.1) | copy-start | bytes 49156
  16.4 2.6 %copy-start.2 = (f32[32,128]{1,0:T(8,128)S(1)}, f32[32,128]{1,0:T(8,128)}, u32[]{:S(2)}) copy-start(f32[32,128]{1,0:T(8,128)} %forcing_ref.1) | copy-start | bytes 49156
  18.4 1.6 %collective-permute-start.2 = (f32[128,256]{1,0:T(8,128)S(1)}, f32[128,256]{1,0:T(8,128)S(1)}, u32[]{:S(2)}, u32[]{:S(2)}) collective-permute-start(f32[128,256]{1,0:T(8,128)S(1)} %get-tuple-element.45), channel_id=1, source_target_pairs={{0,1},{1,0},{2,3},{3,2},{4,5},{5,4},{6,7},{7,6},{8,9},{9,8},{10,11... | collective-permute-start | bytes 393224 | tf_op jit(solution)/shard_map/ppermute | solution.py:656

commit v8 on v7

--- a/solution.py
+++ b/solution.py
@@ -124,8 +124,8 @@
 
 
 INNER_ROWS = 40
-RIM_ROWS = 16
-INNER_STEP = 8
+RIM_ROWS = 20
+INNER_STEP = 4
 RIM_STEP = 4
 RIM = 2 * HALO
 

time: 43.3 us -> 43 us (level)
  starting transfers between devices: 10.3 us -> 9.53 us
    ppermute x2, starting transfers between devices: 7.21 us -> 6.41 us  [swapped(): return lax.ppermute(value, 'core', [(0, 1), (1, 0)])]
where the time goes in v8:
time: 43 us; the launch traced here: 42.9 us
  blocking collectives  22.5 us (52%)
  Pallas kernels  9.64 us (22%)
  starting transfers between devices  9.53 us (22%)
  between operations  0.72 us (2%)
  waiting for transfers between devices  0.5 us (1%)
    all_to_all x1, blocking collectives, per_device(): arrived = lax.all_to_all(sent, ('basin', 'chip'), 0, 0, tiled=True)  22.5 us
    ppermute x2, starting transfers between devices, swapped(): return lax.ppermute(value, 'core', [(0, 1), (1, 0)])  6.41 us
    ppermute x1, starting transfers between devices, exchanged_away(): return lax.ppermute(value, ('chip', 'core'), pairs)  3.11 us
    pallas_call x1, Pallas kernels, inner_part(): pl.pallas_call(inner_kernel, out_shape=(jax.ShapeDtypeStruct((256, 2 * LA...  3 us
    pallas_call x1, Pallas kernels, zone_partials(): pl.pallas_call(zone_kernel, out_shape=(half, half, jax.ShapeDtypeStruct(d...  2.08 us
    pallas_call x1, Pallas kernels, slots_of(): pl.pallas_call(slot_kernel, out_shape=(jax.ShapeDtypeStruct((count, LANES...  1.84 us
    pallas_call x1, Pallas kernels, fetched(): pl.pallas_call(front_kernel, out_shape=kept + (edge, edge), in_specs=[HBM...  1.21 us
  transfers between devices with their start and end apart: 3, of which 1 were waited for; matrix products, arithmetic and copies ran while one was open for 0% of the time, Pallas kernels for 13%

profile of v8, /device:TPU:1, one launch (start us, length us, event | category | flops | bytes accessed | tf_op | source)
XLA Modules:
  0.0 42.9 jit_solution(703615857627804419)
XLA Ops:
  0.6 1.2 %fetch_and_edges.1 = (f32[64,512]{1,0:T(8,128)S(1)}, f32[64,512]{1,0:T(8,128)S(1)}, f32[64,512]{1,0:T(8,128)S(1)}, s32[64,512]{1,0:T(8,128)S(1)}, s32[254,128]{1...) custom-call(f32[64,512]{1,0:T(8,128)} %bitcast.11, f32[64,512]{1,0:T(8,128)} %bitcast.12, ...), custom_call_target="tpu_custom_call" | custom-call | tf_op jit(solution)/shard_map/fetch_and_edges/pallas_call | solution.py:86
  1.8 3.1 %collective-permute-start.1 = (f32[12,512]{1,0:T(8,128)S(1)}, f32[12,512]{1,0:T(8,128)S(1)}, u32[]{:S(2)}, u32[]{:S(2)}) collective-permute-start(f32[12,512]{1,0:T(8,128)S(1)} %get-tuple-element.36), channel_id=1, source_target_pairs={{0,63},{1,2},{2,1},{3,4},{4,3},{5,6},{6,5},{7,8},{8,7},{9,10},{10,... | collective-permute-start | bytes 73736 | tf_op jit(solution)/shard_map/ppermute | solution.py:662
  5.0 1.8 %slot_lookup.1 = (s32[256,128]{1,0:T(8,128)S(1)}, f32[256,128]{1,0:T(8,128)S(1)}, f32[256,128]{1,0:T(8,128)S(1)}, f32[8,128]{1,0:T(8,128)S(1)}) custom-call(s32[254,128]{1,0:T(8,128)S(1)} %get-tuple-element.32.owner_ref, s32[64,512]{1,0:T(8,128)S(1)} %get-tuple-element.33.label_ref), custom_call_target="tpu_custom_call" | custom-call | flops 1073741824 | bytes 524288 | tf_op jit(solution)/shard_map/slot_lookup/pallas_call | solution.py:245
  6.8 6.3 %collective-permute-start = (f32[12,512]{1,0:T(8,128)S(1)}, f32[12,512]{1,0:T(8,128)S(1)}, u32[]{:S(2)}, u32[]{:S(2)}) collective-permute-start(f32[12,512]{1,0:T(8,128)S(1)} %get-tuple-element.35), channel_id=1, source_target_pairs={{0,1},{1,0},{2,3},{3,2},{4,5},{5,4},{6,7},{7,6},{8,9},{9,8},{10,11... | collective-permute-start | bytes 73736 | tf_op jit(solution)/shard_map/ppermute | solution.py:656
  13.1 3.0 %inner_rows.1 = (f32[256,256]{1,0:T(8,128)S(1)}, f32[64,512]{1,0:T(8,128)S(1)}, f32[16,32]{1,0:T(8,128)S(1)}) custom-call(f32[64,512]{1,0:T(8,128)S(1)} %get-tuple-element.28.depth_ref, f32[64,512]{1,0:T(8,128)S(1)} %get-tuple-element.29.rough_ref_, f32[64,512]{1,0:T(8,128)S(1)} %get-tuple-element.30.seed_ref, s32[64,512]{1,0:T(8,128)S(1)} %get-tuple-element.33.label_ref, ...), custom_call_target="tpu_custom_call" | custom-call | flops 2147483648 | bytes 655360 | tf_op jit(solution)/shard_map/inner_rows/pallas_call | solution.py:439
  16.1 0.0 collective-permute-done.1.away_ref
  16.1 0.0 collective-permute-done.chip_ref
  16.1 0.0 copy-start
  16.1 0.0 copy-start.1
  16.2 0.0 copy-start.2
  16.2 2.1 %zone_partials.1 = (f32[128,256]{1,0:T(8,128)S(1)}, f32[128,256]{1,0:T(8,128)S(1)}, f32[64,512]{1,0:T(8,128)S(1)}) custom-call(f32[64,512]{1,0:T(8,128)S(1)} %get-tuple-element.28.depth_ref, f32[64,512]{1,0:T(8,128)S(1)} %get-tuple-element.29.rough_ref_, f32[64,512]{1,0:T(8,128)S(1)} %get-tuple-element.30.seed_ref, ...), custom_call_target="tpu_custom_call" | custom-call | tf_op jit(solution)/shard_map/zone_partials/pallas_call | solution.py:545
  18.3 0.1 collective-permute-start.2
  18.4 0.0 copy-done
  18.4 0.0 copy-done.1
  18.4 0.0 copy-done.2
  18.4 0.8 %reach_maps.1 = (f32[32,128]{1,0:T(8,128)S(1)}, f32[32,128]{1,0:T(8,128)S(1)}, f32[2,128]{1,0:T(2,128)S(1)}) custom-call(f32[64,512]{1,0:T(8,128)S(1)} %get-tuple-element.46.adjoint_ref, s32[32,128]{1,0:T(8,128)S(1)} %copy-done, f32[32,128]{1,0:T(8,128)S(1)} %copy-done.1, f32[32,128]{1,0:T(8,128)S(1)} %copy-done.2), custom_call_target="tpu_custom_call" | custom-call | tf_op jit(solution)/shard_map/reach_maps/pallas_call | solution.py:645
  19.2 0.5 %collective-permute-done.2.other_ref = f32[128,256]{1,0:T(8,128)S(1)} collective-permute-done((f32[128,256]{1,0:T(8,128)S(1)}, f32[128,256]{1,0:T(8,128)S(1)}, u32[]{:S(2)}, u32[]{:S(2)}) %collective-permute-start.2) | collective-permute-done | bytes 131104 | tf_op jit(solution)/shard_map/ppermute | solution.py:656
  19.7 22.5 %all_to_all.5 = f32[128,4,128]{2,1,0:T(4,128)S(1)} all-to-all(f32[128,4,128]{2,1,0:T(4,128)S(1)} %bitcast.10), channel_id=1, replica_groups=mesh['basin'=4,'chip'=32,'core'=2] {'basin','chip'}, dimensions={0} | all-to-all | bytes 524288 | tf_op jit(solution)/shard_map/all_to_all | solution.py:686
  42.2 0.7 %results.1 = (f32[1,127]{1,0:T(1,128)}, f32[1,127]{1,0:T(1,128)}, f32[32,128]{1,0:T(8,128)}) custom-call(f32[512,128]{1,0:T(8,128)S(1)} %bitcast.9, f32[32,128]{1,0:T(8,128)S(1)} %get-tuple-element.48.rate_ref, f32[32,128]{1,0:T(8,128)S(1)} %get-tuple-element.49.push_ref), custom_call_target="tpu_custom_call" | custom-call | tf_op jit(solution)/shard_map/results/pallas_call | solution.py:602
  (1 shorter events, 0.0 us)
Async XLA Ops:
  1.8 14.3 %collective-permute-start.1 = (f32[12,512]{1,0:T(8,128)S(1)}, f32[12,512]{1,0:T(8,128)S(1)}, u32[]{:S(2)}, u32[]{:S(2)}) collective-permute-start(f32[12,512]{1,0:T(8,128)S(1)} %get-tuple-element.36), channel_id=1, source_target_pairs={{0,63},{1,2},{2,1},{3,4},{4,3},{5,6},{6,5},{7,8},{8,7},{9,10},{10,... | collective-permute-start | bytes 73736 | tf_op jit(solution)/shard_map/ppermute | solution.py:662
  6.8 9.3 %collective-permute-start = (f32[12,512]{1,0:T(8,128)S(1)}, f32[12,512]{1,0:T(8,128)S(1)}, u32[]{:S(2)}, u32[]{:S(2)}) collective-permute-start(f32[12,512]{1,0:T(8,128)S(1)} %get-tuple-element.35), channel_id=1, source_target_pairs={{0,1},{1,0},{2,3},{3,2},{4,5},{5,4},{6,7},{7,6},{8,9},{9,8},{10,11... | collective-permute-start | bytes 73736 | tf_op jit(solution)/shard_map/ppermute | solution.py:656
  16.1 2.2 %copy-start = (s32[32,128]{1,0:T(8,128)S(1)}, s32[32,128]{1,0:T(8,128)}, u32[]{:S(2)}) copy-start(s32[32,128]{1,0:T(8,128)} %cell_ref.1) | copy-start | bytes 49156
  16.1 2.2 %copy-start.1 = (f32[32,128]{1,0:T(8,128)S(1)}, f32[32,128]{1,0:T(8,128)}, u32[]{:S(2)}) copy-start(f32[32,128]{1,0:T(8,128)} %keep_ref.1) | copy-start | bytes 49156
  16.2 2.2 %copy-start.2 = (f32[32,128]{1,0:T(8,128)S(1)}, f32[32,128]{1,0:T(8,128)}, u32[]{:S(2)}) copy-start(f32[32,128]{1,0:T(8,128)} %forcing_ref.1) | copy-start | bytes 49156
  18.3 1.4 %collective-permute-start.2 = (f32[128,256]{1,0:T(8,128)S(1)}, f32[128,256]{1,0:T(8,128)S(1)}, u32[]{:S(2)}, u32[]{:S(2)}) collective-permute-start(f32[128,256]{1,0:T(8,128)S(1)} %get-tuple-element.45), channel_id=1, source_target_pairs={{0,1},{1,0},{2,3},{3,2},{4,5},{5,4},{6,7},{7,6},{8,9},{9,8},{10,11... | collective-permute-start | bytes 393224 | tf_op jit(solution)/shard_map/ppermute | solution.py:656

commit v9 on v8

--- a/solution.py
+++ b/solution.py
@@ -151,7 +151,10 @@
         lanes = slots - owners * SPAN
         chips = jnp.floor(owners * 0.5)
         swapped = jnp.abs((owners - 2.0 * chips) - core)
-        return jnp.where(owners < 256.0, chips + 128.0 * swapped, 256.0), lanes
+        basins, per_basin = lax.axis_size("basin"), lax.axis_size("chip")
+        basin = jnp.floor(chips * (1.0 / per_basin))
+        place = (chips - per_basin * basin) * basins + basin
+        return jnp.where(owners < 256.0, place + 128.0 * swapped, 256.0), lanes
 
     owners, lanes = placed(jnp.transpose(table_ref[...]))
     turned_ref[:, 0:256] = (owners * LANES).astype(jnp.bfloat16)
@@ -586,11 +589,11 @@
     grad_ref[...] = (sums[0:1, :] + sums[4:5, :])[:, :SPAN]
     curve_ref[...] = (sums[1:2, :] + sums[5:6, :])[:, :SPAN]
     basin, chip = lax.axis_index("basin"), lax.axis_index("chip")
-    basins, chips = lax.axis_size("basin"), lax.axis_size("chip")
+    basins = lax.axis_size("basin")
     incoming = jnp.zeros((1, LANES), jnp.float32)
     for hop in reversed(range(1, basins)):
         there = jnp.where(basin + hop < basins, 1.0, 0.0)
-        row = 4 * (jnp.minimum(basin + hop, basins - 1) * chips + chip)
+        row = 4 * (chip * basins + jnp.minimum(basin + hop, basins - 1))
         rate = arrived_ref[pl.ds(row + 2, 1), :]
         push = arrived_ref[pl.ds(row + 3, 1), :]
         incoming = there * (rate * incoming + push)
@@ -683,7 +686,7 @@
     other = swapped(other)
     rate, push, edge = reach_maps(adjoint, levee_cell, retention, forcing)
     sent = parcels(own, other, edge).reshape(-1, 4, LANES)
-    arrived = lax.all_to_all(sent, ("basin", "chip"), 0, 0, tiled=True)
+    arrived = lax.all_to_all(sent, ("chip", "basin"), 0, 0, tiled=True)
     grad, curve, reach_adjoint = results(arrived.reshape(-1, LANES), rate, push)
     return (grad.reshape(-1), curve.reshape(-1), reach_adjoint)
 

time: 43 us -> 41.9 us (0.974)
  blocking collectives: 22.5 us -> 21.3 us
    all_to_all x1, blocking collectives: 22.5 us -> 21.3 us  [per_device(): arrived = lax.all_to_all(sent, ('chip', 'basin'), 0, 0, tiled=True)]
  transfers between devices with their start and end apart: 3 -> 3, of which waited for: 1 -> 1; matrix products, arithmetic and copies ran while one was open for 0% -> 0% of each run, Pallas kernels for 13% -> 14%
where the time goes in v9:
time: 41.9 us; the launch traced here: 41.7 us
  blocking collectives  21.3 us (51%)
  Pallas kernels  9.68 us (23%)
  starting transfers between devices  9.53 us (23%)
  between operations  0.72 us (2%)
  waiting for transfers between devices  0.49 us (1%)
    all_to_all x1, blocking collectives, per_device(): arrived = lax.all_to_all(sent, ('chip', 'basin'), 0, 0, tiled=True)  21.3 us
    ppermute x2, starting transfers between devices, swapped(): return lax.ppermute(value, 'core', [(0, 1), (1, 0)])  6.41 us
    ppermute x1, starting transfers between devices, exchanged_away(): return lax.ppermute(value, ('chip', 'core'), pairs)  3.11 us
    pallas_call x1, Pallas kernels, inner_part(): pl.pallas_call(inner_kernel, out_shape=(jax.ShapeDtypeStruct((256, 2 * LA...  3 us
    pallas_call x1, Pallas kernels, zone_partials(): pl.pallas_call(zone_kernel, out_shape=(half, half, jax.ShapeDtypeStruct(d...  2.08 us
    pallas_call x1, Pallas kernels, slots_of(): pl.pallas_call(slot_kernel, out_shape=(jax.ShapeDtypeStruct((count, LANES...  1.87 us
    pallas_call x1, Pallas kernels, fetched(): pl.pallas_call(front_kernel, out_shape=kept + (edge, edge), in_specs=[HBM...  1.21 us
  transfers between devices with their start and end apart: 3, of which 1 were waited for; matrix products, arithmetic and copies ran while one was open for 0% of the time, Pallas kernels for 14%

profile of v9, /device:TPU:1, one launch (start us, length us, event | category | flops | bytes accessed | tf_op | source)
XLA Modules:
  0.0 41.7 jit_solution(7718966103029727406)
XLA Ops:
  0.6 1.2 %fetch_and_edges.1 = (f32[64,512]{1,0:T(8,128)S(1)}, f32[64,512]{1,0:T(8,128)S(1)}, f32[64,512]{1,0:T(8,128)S(1)}, s32[64,512]{1,0:T(8,128)S(1)}, s32[254,128]{1...) custom-call(f32[64,512]{1,0:T(8,128)} %bitcast.11, f32[64,512]{1,0:T(8,128)} %bitcast.12, ...), custom_call_target="tpu_custom_call" | custom-call | tf_op jit(solution)/shard_map/fetch_and_edges/pallas_call | solution.py:86
  1.8 3.1 %collective-permute-start.1 = (f32[12,512]{1,0:T(8,128)S(1)}, f32[12,512]{1,0:T(8,128)S(1)}, u32[]{:S(2)}, u32[]{:S(2)}) collective-permute-start(f32[12,512]{1,0:T(8,128)S(1)} %get-tuple-element.36), channel_id=1, source_target_pairs={{0,63},{1,2},{2,1},{3,4},{4,3},{5,6},{6,5},{7,8},{8,7},{9,10},{10,... | collective-permute-start | bytes 73736 | tf_op jit(solution)/shard_map/ppermute | solution.py:665
  5.0 1.9 %slot_lookup.1 = (s32[256,128]{1,0:T(8,128)S(1)}, f32[256,128]{1,0:T(8,128)S(1)}, f32[256,128]{1,0:T(8,128)S(1)}, f32[8,128]{1,0:T(8,128)S(1)}) custom-call(s32[254,128]{1,0:T(8,128)S(1)} %get-tuple-element.32.owner_ref, s32[64,512]{1,0:T(8,128)S(1)} %get-tuple-element.33.label_ref), custom_call_target="tpu_custom_call" | custom-call | flops 1073741824 | bytes 524288 | tf_op jit(solution)/shard_map/slot_lookup/pallas_call | solution.py:248
  6.8 6.3 %collective-permute-start = (f32[12,512]{1,0:T(8,128)S(1)}, f32[12,512]{1,0:T(8,128)S(1)}, u32[]{:S(2)}, u32[]{:S(2)}) collective-permute-start(f32[12,512]{1,0:T(8,128)S(1)} %get-tuple-element.35), channel_id=1, source_target_pairs={{0,1},{1,0},{2,3},{3,2},{4,5},{5,4},{6,7},{7,6},{8,9},{9,8},{10,11... | collective-permute-start | bytes 73736 | tf_op jit(solution)/shard_map/ppermute | solution.py:659
  13.1 3.0 %inner_rows.1 = (f32[256,256]{1,0:T(8,128)S(1)}, f32[64,512]{1,0:T(8,128)S(1)}, f32[16,32]{1,0:T(8,128)S(1)}) custom-call(f32[64,512]{1,0:T(8,128)S(1)} %get-tuple-element.28.depth_ref, f32[64,512]{1,0:T(8,128)S(1)} %get-tuple-element.29.rough_ref_, f32[64,512]{1,0:T(8,128)S(1)} %get-tuple-element.30.seed_ref, s32[64,512]{1,0:T(8,128)S(1)} %get-tuple-element.33.label_ref, ...), custom_call_target="tpu_custom_call" | custom-call | flops 2147483648 | bytes 655360 | tf_op jit(solution)/shard_map/inner_rows/pallas_call | solution.py:442
  16.1 0.0 collective-permute-done.1.away_ref
  16.2 0.0 collective-permute-done.chip_ref
  16.2 0.0 copy-start
  16.2 0.0 copy-start.1
  16.2 0.0 copy-start.2
  16.2 2.1 %zone_partials.1 = (f32[128,256]{1,0:T(8,128)S(1)}, f32[128,256]{1,0:T(8,128)S(1)}, f32[64,512]{1,0:T(8,128)S(1)}) custom-call(f32[64,512]{1,0:T(8,128)S(1)} %get-tuple-element.28.depth_ref, f32[64,512]{1,0:T(8,128)S(1)} %get-tuple-element.29.rough_ref_, f32[64,512]{1,0:T(8,128)S(1)} %get-tuple-element.30.seed_ref, ...), custom_call_target="tpu_custom_call" | custom-call | tf_op jit(solution)/shard_map/zone_partials/pallas_call | solution.py:548
  18.3 0.1 collective-permute-start.2
  18.4 0.0 copy-done
  18.4 0.0 copy-done.1
  18.4 0.0 copy-done.2
  18.4 0.8 %reach_maps.1 = (f32[32,128]{1,0:T(8,128)S(1)}, f32[32,128]{1,0:T(8,128)S(1)}, f32[2,128]{1,0:T(2,128)S(1)}) custom-call(f32[64,512]{1,0:T(8,128)S(1)} %get-tuple-element.46.adjoint_ref, s32[32,128]{1,0:T(8,128)S(1)} %copy-done, f32[32,128]{1,0:T(8,128)S(1)} %copy-done.1, f32[32,128]{1,0:T(8,128)S(1)} %copy-done.2), custom_call_target="tpu_custom_call" | custom-call | tf_op jit(solution)/shard_map/reach_maps/pallas_call | solution.py:648
  19.2 0.5 %collective-permute-done.2.other_ref = f32[128,256]{1,0:T(8,128)S(1)} collective-permute-done((f32[128,256]{1,0:T(8,128)S(1)}, f32[128,256]{1,0:T(8,128)S(1)}, u32[]{:S(2)}, u32[]{:S(2)}) %collective-permute-start.2) | collective-permute-done | bytes 131104 | tf_op jit(solution)/shard_map/ppermute | solution.py:659
  19.8 21.3 %all_to_all.5 = f32[128,4,128]{2,1,0:T(4,128)S(1)} all-to-all(f32[128,4,128]{2,1,0:T(4,128)S(1)} %bitcast.10), channel_id=1, replica_groups=mesh['basin'=4,'chip'=32,'core'=2] {'chip','basin'}, dimensions={0} | all-to-all | bytes 524288 | tf_op jit(solution)/shard_map/all_to_all | solution.py:689
  41.0 0.7 %results.1 = (f32[1,127]{1,0:T(1,128)}, f32[1,127]{1,0:T(1,128)}, f32[32,128]{1,0:T(8,128)}) custom-call(f32[512,128]{1,0:T(8,128)S(1)} %bitcast.9, f32[32,128]{1,0:T(8,128)S(1)} %get-tuple-element.48.rate_ref, f32[32,128]{1,0:T(8,128)S(1)} %get-tuple-element.49.push_ref), custom_call_target="tpu_custom_call" | custom-call | tf_op jit(solution)/shard_map/results/pallas_call | solution.py:605
  (1 shorter events, 0.0 us)
Async XLA Ops:
  1.8 14.3 %collective-permute-start.1 = (f32[12,512]{1,0:T(8,128)S(1)}, f32[12,512]{1,0:T(8,128)S(1)}, u32[]{:S(2)}, u32[]{:S(2)}) collective-permute-start(f32[12,512]{1,0:T(8,128)S(1)} %get-tuple-element.36), channel_id=1, source_target_pairs={{0,63},{1,2},{2,1},{3,4},{4,3},{5,6},{6,5},{7,8},{8,7},{9,10},{10,... | collective-permute-start | bytes 73736 | tf_op jit(solution)/shard_map/ppermute | solution.py:665
  6.8 9.3 %collective-permute-start = (f32[12,512]{1,0:T(8,128)S(1)}, f32[12,512]{1,0:T(8,128)S(1)}, u32[]{:S(2)}, u32[]{:S(2)}) collective-permute-start(f32[12,512]{1,0:T(8,128)S(1)} %get-tuple-element.35), channel_id=1, source_target_pairs={{0,1},{1,0},{2,3},{3,2},{4,5},{5,4},{6,7},{7,6},{8,9},{9,8},{10,11... | collective-permute-start | bytes 73736 | tf_op jit(solution)/shard_map/ppermute | solution.py:659
  16.2 2.2 %copy-start = (s32[32,128]{1,0:T(8,128)S(1)}, s32[32,128]{1,0:T(8,128)}, u32[]{:S(2)}) copy-start(s32[32,128]{1,0:T(8,128)} %cell_ref.1) | copy-start | bytes 49156
  16.2 2.2 %copy-start.1 = (f32[32,128]{1,0:T(8,128)S(1)}, f32[32,128]{1,0:T(8,128)}, u32[]{:S(2)}) copy-start(f32[32,128]{1,0:T(8,128)} %keep_ref.1) | copy-start | bytes 49156
  16.2 2.2 %copy-start.2 = (f32[32,128]{1,0:T(8,128)S(1)}, f32[32,128]{1,0:T(8,128)}, u32[]{:S(2)}) copy-start(f32[32,128]{1,0:T(8,128)} %forcing_ref.1) | copy-start | bytes 49156
  18.3 1.4 %collective-permute-start.2 = (f32[128,256]{1,0:T(8,128)S(1)}, f32[128,256]{1,0:T(8,128)S(1)}, u32[]{:S(2)}, u32[]{:S(2)}) collective-permute-start(f32[128,256]{1,0:T(8,128)S(1)} %get-tuple-element.45), channel_id=1, source_target_pairs={{0,1},{1,0},{2,3},{3,2},{4,5},{5,4},{6,7},{7,6},{8,9},{9,8},{10,11... | collective-permute-start | bytes 393224 | tf_op jit(solution)/shard_map/ppermute | solution.py:659

commit v10 on v9

--- a/solution.py
+++ b/solution.py
@@ -118,8 +118,14 @@
     stray_ref[2], stray_ref[3] = halves(grad * grad)
 
 
+def chip_place():
+    count = lax.axis_size("y") * lax.axis_size("z")
+    return lax.axis_index("y") * lax.axis_size("z") + lax.axis_index("z"), count
+
+
 def own_first_zone():
-    chip = lax.axis_index("basin") * lax.axis_size("chip") + lax.axis_index("chip")
+    index, count = chip_place()
+    chip = lax.axis_index("basin") * count + index
     return (chip * lax.axis_size("core") + lax.axis_index("core")) * SPAN
 
 
@@ -151,9 +157,10 @@
         lanes = slots - owners * SPAN
         chips = jnp.floor(owners * 0.5)
         swapped = jnp.abs((owners - 2.0 * chips) - core)
-        basins, per_basin = lax.axis_size("basin"), lax.axis_size("chip")
-        basin = jnp.floor(chips * (1.0 / per_basin))
-        place = (chips - per_basin * basin) * basins + basin
+        basins, height, depth = (lax.axis_size(axis) for axis in ("basin", "y", "z"))
+        line = jnp.floor(chips * (1.0 / depth))
+        basin = jnp.floor(chips * (1.0 / (height * depth)))
+        place = ((chips - depth * line) * height + (line - height * basin)) * basins + basin
         return jnp.where(owners < 256.0, place + 128.0 * swapped, 256.0), lanes
 
     owners, lanes = placed(jnp.transpose(table_ref[...]))
@@ -482,7 +489,7 @@
     cell_ref,
 ):
     first_core = lax.axis_index("core") == 0
-    chip_index, chips = lax.axis_index("chip"), lax.axis_size("chip")
+    chip_index, chips = chip_place()
     has_low = jnp.where(first_core & (chip_index == 0), 0.0, 1.0)
     has_high = jnp.where(first_core | (chip_index < chips - 1), 1.0, 0.0)
     rows = depth_ref.shape[0]
@@ -588,7 +595,8 @@
         sums = sums + arrived_ref[start : start + 8, :]
     grad_ref[...] = (sums[0:1, :] + sums[4:5, :])[:, :SPAN]
     curve_ref[...] = (sums[1:2, :] + sums[5:6, :])[:, :SPAN]
-    basin, chip = lax.axis_index("basin"), lax.axis_index("chip")
+    basin = lax.axis_index("basin")
+    chip = lax.axis_index("z") * lax.axis_size("y") + lax.axis_index("y")
     basins = lax.axis_size("basin")
     incoming = jnp.zeros((1, LANES), jnp.float32)
     for hop in reversed(range(1, basins)):
@@ -660,9 +668,9 @@
 
 
 def exchanged_away(value):
-    tiles = lax.axis_size("chip") * lax.axis_size("core")
+    tiles = chip_place()[1] * lax.axis_size("core")
     pairs = [(i, (i + 1 if i % 2 else i - 1) % tiles) for i in range(tiles)]
-    return lax.ppermute(value, ("chip", "core"), pairs)
+    return lax.ppermute(value, ("y", "z", "core"), pairs)
 
 
 def per_device(
@@ -686,7 +694,7 @@
     other = swapped(other)
     rate, push, edge = reach_maps(adjoint, levee_cell, retention, forcing)
     sent = parcels(own, other, edge).reshape(-1, 4, LANES)
-    arrived = lax.all_to_all(sent, ("chip", "basin"), 0, 0, tiled=True)
+    arrived = lax.all_to_all(sent, ("z", "y", "basin"), 0, 0, tiled=True)
     grad, curve, reach_adjoint = results(arrived.reshape(-1, LANES), rate, push)
     return (grad.reshape(-1), curve.reshape(-1), reach_adjoint)
 
@@ -694,12 +702,12 @@
 def solution(mesh):
     basins, tiles = mesh.devices.shape
     fine = jax.sharding.Mesh(
-        mesh.devices.reshape(basins, tiles // 2, 2), ("basin", "chip", "core")
-    )
-    tile = ("chip", "core")
+        mesh.devices.reshape(basins, tiles // 16, 8, 2), ("basin", "y", "z", "core")
+    )
+    tile = ("y", "z", "core")
     cells = P("basin", tile, None)
     reaches = P("basin", tile)
-    zones = P(("basin", "chip", "core"))
+    zones = P(("basin", "y", "z", "core"))
     return jax.shard_map(
         per_device,
         mesh=fine,

time: 41.9 us -> 43.1 us (1.029)
  blocking collectives: 21.3 us -> 22.2 us
    all_to_all x1, blocking collectives: 21.3 us -> 22.2 us  [per_device(): arrived = lax.all_to_all(sent, ('z', 'y', 'basin'), 0, 0, tiled=True)]
  transfers between devices with their start and end apart: 3 -> 3, of which waited for: 1 -> 1; matrix products, arithmetic and copies ran while one was open for 0% -> 0% of each run, Pallas kernels for 14% -> 13%
where the time goes in v10:
time: 43.1 us; the launch traced here: 42.7 us
  blocking collectives  22.2 us (52%)
  Pallas kernels  9.69 us (22%)
  starting transfers between devices  9.53 us (22%)
  between operations  0.72 us (2%)
  waiting for transfers between devices  0.49 us (1%)
    all_to_all x1, blocking collectives, per_device(): arrived = lax.all_to_all(sent, ('z', 'y', 'basin'), 0, 0, tiled=True)  22.2 us
    ppermute x2, starting transfers between devices, swapped(): return lax.ppermute(value, 'core', [(0, 1), (1, 0)])  6.41 us
    ppermute x1, starting transfers between devices, exchanged_away(): return lax.ppermute(value, ('y', 'z', 'core'), pairs)  3.11 us
    pallas_call x1, Pallas kernels, inner_part(): pl.pallas_call(inner_kernel, out_shape=(jax.ShapeDtypeStruct((256, 2 * LA...  2.99 us
    pallas_call x1, Pallas kernels, zone_partials(): pl.pallas_call(zone_kernel, out_shape=(half, half, jax.ShapeDtypeStruct(d...  2.08 us
    pallas_call x1, Pallas kernels, slots_of(): pl.pallas_call(slot_kernel, out_shape=(jax.ShapeDtypeStruct((count, LANES...  1.88 us
    pallas_call x1, Pallas kernels, fetched(): pl.pallas_call(front_kernel, out_shape=kept + (edge, edge), in_specs=[HBM...  1.21 us
  transfers between devices with their start and end apart: 3, of which 1 were waited for; matrix products, arithmetic and copies ran while one was open for 0% of the time, Pallas kernels for 13%

profile of v10, /device:TPU:1, one launch (start us, length us, event | category | flops | bytes accessed | tf_op | source)
XLA Modules:
  0.0 42.7 jit_solution(10485696668735281310)
XLA Ops:
  0.6 1.2 %fetch_and_edges.1 = (f32[64,512]{1,0:T(8,128)S(1)}, f32[64,512]{1,0:T(8,128)S(1)}, f32[64,512]{1,0:T(8,128)S(1)}, s32[64,512]{1,0:T(8,128)S(1)}, s32[254,128]{1...) custom-call(f32[64,512]{1,0:T(8,128)} %bitcast.11, f32[64,512]{1,0:T(8,128)} %bitcast.12, ...), custom_call_target="tpu_custom_call" | custom-call | tf_op jit(solution)/shard_map/fetch_and_edges/pallas_call | solution.py:86
  1.8 3.1 %collective-permute-start.1 = (f32[12,512]{1,0:T(8,128)S(1)}, f32[12,512]{1,0:T(8,128)S(1)}, u32[]{:S(2)}, u32[]{:S(2)}) collective-permute-start(f32[12,512]{1,0:T(8,128)S(1)} %get-tuple-element.36), channel_id=1, source_target_pairs={{0,63},{1,2},{2,1},{3,4},{4,3},{5,6},{6,5},{7,8},{8,7},{9,10},{10,... | collective-permute-start | bytes 73736 | tf_op jit(solution)/shard_map/ppermute | solution.py:673
  5.0 1.9 %slot_lookup.1 = (s32[256,128]{1,0:T(8,128)S(1)}, f32[256,128]{1,0:T(8,128)S(1)}, f32[256,128]{1,0:T(8,128)S(1)}, f32[8,128]{1,0:T(8,128)S(1)}) custom-call(s32[254,128]{1,0:T(8,128)S(1)} %get-tuple-element.32.owner_ref, s32[64,512]{1,0:T(8,128)S(1)} %get-tuple-element.33.label_ref), custom_call_target="tpu_custom_call" | custom-call | flops 1073741824 | bytes 524288 | tf_op jit(solution)/shard_map/slot_lookup/pallas_call | solution.py:255
  6.9 6.3 %collective-permute-start = (f32[12,512]{1,0:T(8,128)S(1)}, f32[12,512]{1,0:T(8,128)S(1)}, u32[]{:S(2)}, u32[]{:S(2)}) collective-permute-start(f32[12,512]{1,0:T(8,128)S(1)} %get-tuple-element.35), channel_id=1, source_target_pairs={{0,1},{1,0},{2,3},{3,2},{4,5},{5,4},{6,7},{7,6},{8,9},{9,8},{10,11... | collective-permute-start | bytes 73736 | tf_op jit(solution)/shard_map/ppermute | solution.py:667
  13.2 3.0 %inner_rows.1 = (f32[256,256]{1,0:T(8,128)S(1)}, f32[64,512]{1,0:T(8,128)S(1)}, f32[16,32]{1,0:T(8,128)S(1)}) custom-call(f32[64,512]{1,0:T(8,128)S(1)} %get-tuple-element.28.depth_ref, f32[64,512]{1,0:T(8,128)S(1)} %get-tuple-element.29.rough_ref_, f32[64,512]{1,0:T(8,128)S(1)} %get-tuple-element.30.seed_ref, s32[64,512]{1,0:T(8,128)S(1)} %get-tuple-element.33.label_ref, ...), custom_call_target="tpu_custom_call" | custom-call | flops 2147483648 | bytes 655360 | tf_op jit(solution)/shard_map/inner_rows/pallas_call | solution.py:449
  16.2 0.0 collective-permute-done.1.away_ref
  16.2 0.0 collective-permute-done.chip_ref
  16.2 0.0 copy-start
  16.2 0.0 copy-start.1
  16.2 0.0 copy-start.2
  16.2 2.1 %zone_partials.1 = (f32[128,256]{1,0:T(8,128)S(1)}, f32[128,256]{1,0:T(8,128)S(1)}, f32[64,512]{1,0:T(8,128)S(1)}) custom-call(f32[64,512]{1,0:T(8,128)S(1)} %get-tuple-element.28.depth_ref, f32[64,512]{1,0:T(8,128)S(1)} %get-tuple-element.29.rough_ref_, f32[64,512]{1,0:T(8,128)S(1)} %get-tuple-element.30.seed_ref, ...), custom_call_target="tpu_custom_call" | custom-call | tf_op jit(solution)/shard_map/zone_partials/pallas_call | solution.py:555
  18.3 0.1 collective-permute-start.2
  18.4 0.0 copy-done
  18.4 0.0 copy-done.1
  18.4 0.0 copy-done.2
  18.4 0.8 %reach_maps.1 = (f32[32,128]{1,0:T(8,128)S(1)}, f32[32,128]{1,0:T(8,128)S(1)}, f32[2,128]{1,0:T(2,128)S(1)}) custom-call(f32[64,512]{1,0:T(8,128)S(1)} %get-tuple-element.46.adjoint_ref, s32[32,128]{1,0:T(8,128)S(1)} %copy-done, f32[32,128]{1,0:T(8,128)S(1)} %copy-done.1, f32[32,128]{1,0:T(8,128)S(1)} %copy-done.2), custom_call_target="tpu_custom_call" | custom-call | tf_op jit(solution)/shard_map/reach_maps/pallas_call | solution.py:656
  19.3 0.5 %collective-permute-done.2.other_ref = f32[128,256]{1,0:T(8,128)S(1)} collective-permute-done((f32[128,256]{1,0:T(8,128)S(1)}, f32[128,256]{1,0:T(8,128)S(1)}, u32[]{:S(2)}, u32[]{:S(2)}) %collective-permute-start.2) | collective-permute-done | bytes 131104 | tf_op jit(solution)/shard_map/ppermute | solution.py:667
  19.8 22.2 %all_to_all.5 = f32[128,4,128]{2,1,0:T(4,128)S(1)} all-to-all(f32[128,4,128]{2,1,0:T(4,128)S(1)} %bitcast.10), channel_id=1, replica_groups=mesh['basin'=4,'y'=4,'z'=8,'core'=2] {'z','y','basin'}, dimensions={0} | all-to-all | bytes 524288 | tf_op jit(solution)/shard_map/all_to_all | solution.py:697
  42.0 0.7 %results.1 = (f32[1,127]{1,0:T(1,128)}, f32[1,127]{1,0:T(1,128)}, f32[32,128]{1,0:T(8,128)}) custom-call(f32[512,128]{1,0:T(8,128)S(1)} %bitcast.9, f32[32,128]{1,0:T(8,128)S(1)} %get-tuple-element.48.rate_ref, f32[32,128]{1,0:T(8,128)S(1)} %get-tuple-element.49.push_ref), custom_call_target="tpu_custom_call" | custom-call | tf_op jit(solution)/shard_map/results/pallas_call | solution.py:613
  (1 shorter events, 0.0 us)
Async XLA Ops:
  1.8 14.3 %collective-permute-start.1 = (f32[12,512]{1,0:T(8,128)S(1)}, f32[12,512]{1,0:T(8,128)S(1)}, u32[]{:S(2)}, u32[]{:S(2)}) collective-permute-start(f32[12,512]{1,0:T(8,128)S(1)} %get-tuple-element.36), channel_id=1, source_target_pairs={{0,63},{1,2},{2,1},{3,4},{4,3},{5,6},{6,5},{7,8},{8,7},{9,10},{10,... | collective-permute-start | bytes 73736 | tf_op jit(solution)/shard_map/ppermute | solution.py:673
  6.9 9.3 %collective-permute-start = (f32[12,512]{1,0:T(8,128)S(1)}, f32[12,512]{1,0:T(8,128)S(1)}, u32[]{:S(2)}, u32[]{:S(2)}) collective-permute-start(f32[12,512]{1,0:T(8,128)S(1)} %get-tuple-element.35), channel_id=1, source_target_pairs={{0,1},{1,0},{2,3},{3,2},{4,5},{5,4},{6,7},{7,6},{8,9},{9,8},{10,11... | collective-permute-start | bytes 73736 | tf_op jit(solution)/shard_map/ppermute | solution.py:667
  16.2 2.2 %copy-start = (s32[32,128]{1,0:T(8,128)S(1)}, s32[32,128]{1,0:T(8,128)}, u32[]{:S(2)}) copy-start(s32[32,128]{1,0:T(8,128)} %cell_ref.1) | copy-start | bytes 49156
  16.2 2.2 %copy-start.1 = (f32[32,128]{1,0:T(8,128)S(1)}, f32[32,128]{1,0:T(8,128)}, u32[]{:S(2)}) copy-start(f32[32,128]{1,0:T(8,128)} %keep_ref.1) | copy-start | bytes 49156
  16.2 2.2 %copy-start.2 = (f32[32,128]{1,0:T(8,128)S(1)}, f32[32,128]{1,0:T(8,128)}, u32[]{:S(2)}) copy-start(f32[32,128]{1,0:T(8,128)} %forcing_ref.1) | copy-start | bytes 49156
  18.3 1.4 %collective-permute-start.2 = (f32[128,256]{1,0:T(8,128)S(1)}, f32[128,256]{1,0:T(8,128)S(1)}, u32[]{:S(2)}, u32[]{:S(2)}) collective-permute-start(f32[128,256]{1,0:T(8,128)S(1)} %get-tuple-element.45), channel_id=1, source_target_pairs={{0,1},{1,0},{2,3},{3,2},{4,5},{5,4},{6,7},{7,6},{8,9},{9,8},{10,11... | collective-permute-start | bytes 393224 | tf_op jit(solution)/shard_map/ppermute | solution.py:667

commit v11 on v9

--- a/solution.py
+++ b/solution.py
@@ -676,9 +676,8 @@
         owner_slot.reshape(-1, LANES),
     )
     from_away = exchanged_away(to_away)
+    from_chip = swapped(to_chip)
     moves, device, lane, home = slots_of(owner_slot, label)
-    to_chip, home = lax.optimization_barrier((to_chip, home))
-    from_chip = swapped(to_chip)
     inner = inner_part(depth, rough, seed, label, moves, device, lane, home)
     own, other, adjoint = zone_partials(
         depth, rough, seed, from_chip, from_away, *inner, label, moves, device, lane, home

time: 41.9 us -> 42 us (level)
  starting transfers between devices: 9.53 us -> 10.1 us
    ppermute x2, starting transfers between devices: 6.41 us -> 10.1 us  [swapped(): return lax.ppermute(value, 'core', [(0, 1), (1, 0)])]
    ppermute x1, starting transfers between devices: 3.11 us -> 0.01 us  [exchanged_away(): return lax.ppermute(value, ('chip', 'core'), pairs)]
where the time goes in v11:
time: 42 us; the launch traced here: 41.9 us
  blocking collectives  21.2 us (50%)
  starting transfers between devices  10.1 us (24%)
  Pallas kernels  9.68 us (23%)
  between operations  0.71 us (2%)
    all_to_all x1, blocking collectives, per_device(): arrived = lax.all_to_all(sent, ('chip', 'basin'), 0, 0, tiled=True)  21.2 us
    ppermute x2, starting transfers between devices, swapped(): return lax.ppermute(value, 'core', [(0, 1), (1, 0)])  10.1 us
    pallas_call x1, Pallas kernels, inner_part(): pl.pallas_call(inner_kernel, out_shape=(jax.ShapeDtypeStruct((256, 2 * LA...  3 us
    pallas_call x1, Pallas kernels, zone_partials(): pl.pallas_call(zone_kernel, out_shape=(half, half, jax.ShapeDtypeStruct(d...  2.08 us
    pallas_call x1, Pallas kernels, slots_of(): pl.pallas_call(slot_kernel, out_shape=(jax.ShapeDtypeStruct((count, LANES...  1.87 us
    pallas_call x1, Pallas kernels, fetched(): pl.pallas_call(front_kernel, out_shape=kept + (edge, edge), in_specs=[HBM...  1.21 us
  transfers between devices with their start and end apart: 3, of which 1 were waited for; matrix products, arithmetic and copies ran while one was open for 0% of the time, Pallas kernels for 14%

profile of v11, /device:TPU:1, one launch (start us, length us, event | category | flops | bytes accessed | tf_op | source)
XLA Modules:
  0.0 41.9 jit_solution(13849545311146543751)
XLA Ops:
  0.6 1.2 %fetch_and_edges.1 = (f32[64,512]{1,0:T(8,128)S(1)}, f32[64,512]{1,0:T(8,128)S(1)}, f32[64,512]{1,0:T(8,128)S(1)}, s32[64,512]{1,0:T(8,128)S(1)}, s32[254,128]{1...) custom-call(f32[64,512]{1,0:T(8,128)} %bitcast.11, f32[64,512]{1,0:T(8,128)} %bitcast.12, ...), custom_call_target="tpu_custom_call" | custom-call | tf_op jit(solution)/shard_map/fetch_and_edges/pallas_call | solution.py:86
  1.8 3.3 %collective-permute-start = (f32[12,512]{1,0:T(8,128)S(1)}, f32[12,512]{1,0:T(8,128)S(1)}, u32[]{:S(2)}, u32[]{:S(2)}) collective-permute-start(f32[12,512]{1,0:T(8,128)S(1)} %get-tuple-element.29), channel_id=1, source_target_pairs={{0,1},{1,0},{2,3},{3,2},{4,5},{5,4},{6,7},{7,6},{8,9},{9,8},{10,11... | collective-permute-start | bytes 73736 | tf_op jit(solution)/shard_map/ppermute | solution.py:659
  5.2 0.0 collective-permute-start.1
  5.2 1.9 %slot_lookup.1 = (s32[256,128]{1,0:T(8,128)S(1)}, f32[256,128]{1,0:T(8,128)S(1)}, f32[256,128]{1,0:T(8,128)S(1)}, f32[8,128]{1,0:T(8,128)S(1)}) custom-call(s32[254,128]{1,0:T(8,128)S(1)} %get-tuple-element.32.owner_ref, s32[64,512]{1,0:T(8,128)S(1)} %get-tuple-element.31.label_ref), custom_call_target="tpu_custom_call" | custom-call | flops 1073741824 | bytes 524288 | tf_op jit(solution)/shard_map/slot_lookup/pallas_call | solution.py:248
  7.1 3.0 %inner_rows.1 = (f32[256,256]{1,0:T(8,128)S(1)}, f32[64,512]{1,0:T(8,128)S(1)}, f32[16,32]{1,0:T(8,128)S(1)}) custom-call(f32[64,512]{1,0:T(8,128)S(1)} %get-tuple-element.26.depth_ref, f32[64,512]{1,0:T(8,128)S(1)} %get-tuple-element.27.rough_ref_, f32[64,512]{1,0:T(8,128)S(1)} %get-tuple-element.28.seed_ref, s32[64,512]{1,0:T(8,128)S(1)} %get-tuple-element.31.label_ref, ...), custom_call_target="tpu_custom_call" | custom-call | flops 2147483648 | bytes 655360 | tf_op jit(solution)/shard_map/inner_rows/pallas_call | solution.py:442
  10.1 0.0 collective-permute-done.chip_ref
  10.1 0.0 collective-permute-done.1.away_ref
  10.1 0.0 copy-start
  10.1 0.0 copy-start.1
  10.1 0.0 copy-start.2
  10.1 2.1 %zone_partials.1 = (f32[128,256]{1,0:T(8,128)S(1)}, f32[128,256]{1,0:T(8,128)S(1)}, f32[64,512]{1,0:T(8,128)S(1)}) custom-call(f32[64,512]{1,0:T(8,128)S(1)} %get-tuple-element.26.depth_ref, f32[64,512]{1,0:T(8,128)S(1)} %get-tuple-element.27.rough_ref_, f32[64,512]{1,0:T(8,128)S(1)} %get-tuple-element.28.seed_ref, ...), custom_call_target="tpu_custom_call" | custom-call | tf_op jit(solution)/shard_map/zone_partials/pallas_call | solution.py:548
  12.2 6.8 %collective-permute-start.2 = (f32[128,256]{1,0:T(8,128)S(1)}, f32[128,256]{1,0:T(8,128)S(1)}, u32[]{:S(2)}, u32[]{:S(2)}) collective-permute-start(f32[128,256]{1,0:T(8,128)S(1)} %get-tuple-element.41), channel_id=1, source_target_pairs={{0,1},{1,0},{2,3},{3,2},{4,5},{5,4},{6,7},{7,6},{8,9},{9,8},{10,11... | collective-permute-start | bytes 393224 | tf_op jit(solution)/shard_map/ppermute | solution.py:659
  19.0 0.0 copy-done
  19.0 0.0 copy-done.1
  19.0 0.0 copy-done.2
  19.0 0.8 %reach_maps.1 = (f32[32,128]{1,0:T(8,128)S(1)}, f32[32,128]{1,0:T(8,128)S(1)}, f32[2,128]{1,0:T(2,128)S(1)}) custom-call(f32[64,512]{1,0:T(8,128)S(1)} %get-tuple-element.42.adjoint_ref, s32[32,128]{1,0:T(8,128)S(1)} %copy-done, f32[32,128]{1,0:T(8,128)S(1)} %copy-done.1, f32[32,128]{1,0:T(8,128)S(1)} %copy-done.2), custom_call_target="tpu_custom_call" | custom-call | tf_op jit(solution)/shard_map/reach_maps/pallas_call | solution.py:648
  19.8 0.2 collective-permute-done.2.other_ref
  20.0 21.2 %all_to_all.5 = f32[128,4,128]{2,1,0:T(4,128)S(1)} all-to-all(f32[128,4,128]{2,1,0:T(4,128)S(1)} %bitcast.10), channel_id=1, replica_groups=mesh['basin'=4,'chip'=32,'core'=2] {'chip','basin'}, dimensions={0} | all-to-all | bytes 524288 | tf_op jit(solution)/shard_map/all_to_all | solution.py:688
  41.2 0.7 %results.1 = (f32[1,127]{1,0:T(1,128)}, f32[1,127]{1,0:T(1,128)}, f32[32,128]{1,0:T(8,128)}) custom-call(f32[512,128]{1,0:T(8,128)S(1)} %bitcast.9, f32[32,128]{1,0:T(8,128)S(1)} %get-tuple-element.44.rate_ref, f32[32,128]{1,0:T(8,128)S(1)} %get-tuple-element.45.push_ref), custom_call_target="tpu_custom_call" | custom-call | tf_op jit(solution)/shard_map/results/pallas_call | solution.py:605
  (1 shorter events, 0.0 us)
Async XLA Ops:
  1.8 8.2 %collective-permute-start = (f32[12,512]{1,0:T(8,128)S(1)}, f32[12,512]{1,0:T(8,128)S(1)}, u32[]{:S(2)}, u32[]{:S(2)}) collective-permute-start(f32[12,512]{1,0:T(8,128)S(1)} %get-tuple-element.29), channel_id=1, source_target_pairs={{0,1},{1,0},{2,3},{3,2},{4,5},{5,4},{6,7},{7,6},{8,9},{9,8},{10,11... | collective-permute-start | bytes 73736 | tf_op jit(solution)/shard_map/ppermute | solution.py:659
  5.2 4.9 %collective-permute-start.1 = (f32[12,512]{1,0:T(8,128)S(1)}, f32[12,512]{1,0:T(8,128)S(1)}, u32[]{:S(2)}, u32[]{:S(2)}) collective-permute-start(f32[12,512]{1,0:T(8,128)S(1)} %get-tuple-element.30), channel_id=1, source_target_pairs={{0,63},{1,2},{2,1},{3,4},{4,3},{5,6},{6,5},{7,8},{8,7},{9,10},{10,... | collective-permute-start | bytes 73736 | tf_op jit(solution)/shard_map/ppermute | solution.py:665
  10.1 8.9 %copy-start = (s32[32,128]{1,0:T(8,128)S(1)}, s32[32,128]{1,0:T(8,128)}, u32[]{:S(2)}) copy-start(s32[32,128]{1,0:T(8,128)} %cell_ref.1) | copy-start | bytes 49156
  10.1 8.9 %copy-start.1 = (f32[32,128]{1,0:T(8,128)S(1)}, f32[32,128]{1,0:T(8,128)}, u32[]{:S(2)}) copy-start(f32[32,128]{1,0:T(8,128)} %keep_ref.1) | copy-start | bytes 49156
  10.1 8.9 %copy-start.2 = (f32[32,128]{1,0:T(8,128)S(1)}, f32[32,128]{1,0:T(8,128)}, u32[]{:S(2)}) copy-start(f32[32,128]{1,0:T(8,128)} %forcing_ref.1) | copy-start | bytes 49156
  12.2 7.8 %collective-permute-start.2 = (f32[128,256]{1,0:T(8,128)S(1)}, f32[128,256]{1,0:T(8,128)S(1)}, u32[]{:S(2)}, u32[]{:S(2)}) collective-permute-start(f32[128,256]{1,0:T(8,128)S(1)} %get-tuple-element.41), channel_id=1, source_target_pairs={{0,1},{1,0},{2,3},{3,2},{4,5},{5,4},{6,7},{7,6},{8,9},{9,8},{10,11... | collective-permute-start | bytes 393224 | tf_op jit(solution)/shard_map/ppermute | solution.py:659

commit v12 on v10

--- a/solution.py
+++ b/solution.py
@@ -160,7 +160,7 @@
         basins, height, depth = (lax.axis_size(axis) for axis in ("basin", "y", "z"))
         line = jnp.floor(chips * (1.0 / depth))
         basin = jnp.floor(chips * (1.0 / (height * depth)))
-        place = ((chips - depth * line) * height + (line - height * basin)) * basins + basin
+        place = ((line - height * basin) * basins + basin) * depth + (chips - depth * line)
         return jnp.where(owners < 256.0, place + 128.0 * swapped, 256.0), lanes
 
     owners, lanes = placed(jnp.transpose(table_ref[...]))
@@ -596,12 +596,13 @@
     grad_ref[...] = (sums[0:1, :] + sums[4:5, :])[:, :SPAN]
     curve_ref[...] = (sums[1:2, :] + sums[5:6, :])[:, :SPAN]
     basin = lax.axis_index("basin")
-    chip = lax.axis_index("z") * lax.axis_size("y") + lax.axis_index("y")
+    height, level, depth = lax.axis_index("y"), lax.axis_index("z"), lax.axis_size("z")
     basins = lax.axis_size("basin")
     incoming = jnp.zeros((1, LANES), jnp.float32)
     for hop in reversed(range(1, basins)):
         there = jnp.where(basin + hop < basins, 1.0, 0.0)
-        row = 4 * (chip * basins + jnp.minimum(basin + hop, basins - 1))
+        below_here = height * basins + jnp.minimum(basin + hop, basins - 1)
+        row = 4 * (below_here * depth + level)
         rate = arrived_ref[pl.ds(row + 2, 1), :]
         push = arrived_ref[pl.ds(row + 3, 1), :]
         incoming = there * (rate * incoming + push)
@@ -694,7 +695,7 @@
     other = swapped(other)
     rate, push, edge = reach_maps(adjoint, levee_cell, retention, forcing)
     sent = parcels(own, other, edge).reshape(-1, 4, LANES)
-    arrived = lax.all_to_all(sent, ("z", "y", "basin"), 0, 0, tiled=True)
+    arrived = lax.all_to_all(sent, ("y", "basin", "z"), 0, 0, tiled=True)
     grad, curve, reach_adjoint = results(arrived.reshape(-1, LANES), rate, push)
     return (grad.reshape(-1), curve.reshape(-1), reach_adjoint)
 

time: 43.1 us -> 43.6 us (1.012)
  no operation moved by 1% of the time
where the time goes in v12:
time: 43.6 us; the launch traced here: 42.9 us
  blocking collectives  22.5 us (52%)
  Pallas kernels  9.69 us (22%)
  starting transfers between devices  9.53 us (22%)
  between operations  0.72 us (2%)
  waiting for transfers between devices  0.5 us (1%)
    all_to_all x1, blocking collectives, per_device(): arrived = lax.all_to_all(sent, ('y', 'basin', 'z'), 0, 0, tiled=True)  22.5 us
    ppermute x2, starting transfers between devices, swapped(): return lax.ppermute(value, 'core', [(0, 1), (1, 0)])  6.41 us
    ppermute x1, starting transfers between devices, exchanged_away(): return lax.ppermute(value, ('y', 'z', 'core'), pairs)  3.11 us
    pallas_call x1, Pallas kernels, inner_part(): pl.pallas_call(inner_kernel, out_shape=(jax.ShapeDtypeStruct((256, 2 * LA...  2.99 us
    pallas_call x1, Pallas kernels, zone_partials(): pl.pallas_call(zone_kernel, out_shape=(half, half, jax.ShapeDtypeStruct(d...  2.08 us
    pallas_call x1, Pallas kernels, slots_of(): pl.pallas_call(slot_kernel, out_shape=(jax.ShapeDtypeStruct((count, LANES...  1.89 us
    pallas_call x1, Pallas kernels, fetched(): pl.pallas_call(front_kernel, out_shape=kept + (edge, edge), in_specs=[HBM...  1.21 us
  transfers between devices with their start and end apart: 3, of which 1 were waited for; matrix products, arithmetic and copies ran while one was open for 0% of the time, Pallas kernels for 13%

profile of v12, /device:TPU:1, one launch (start us, length us, event | category | flops | bytes accessed | tf_op | source)
XLA Modules:
  0.0 42.9 jit_solution(1546788775591214043)
XLA Ops:
  0.6 1.2 %fetch_and_edges.1 = (f32[64,512]{1,0:T(8,128)S(1)}, f32[64,512]{1,0:T(8,128)S(1)}, f32[64,512]{1,0:T(8,128)S(1)}, s32[64,512]{1,0:T(8,128)S(1)}, s32[254,128]{1...) custom-call(f32[64,512]{1,0:T(8,128)} %bitcast.11, f32[64,512]{1,0:T(8,128)} %bitcast.12, ...), custom_call_target="tpu_custom_call" | custom-call | tf_op jit(solution)/shard_map/fetch_and_edges/pallas_call | solution.py:86
  1.8 3.1 %collective-permute-start.1 = (f32[12,512]{1,0:T(8,128)S(1)}, f32[12,512]{1,0:T(8,128)S(1)}, u32[]{:S(2)}, u32[]{:S(2)}) collective-permute-start(f32[12,512]{1,0:T(8,128)S(1)} %get-tuple-element.36), channel_id=1, source_target_pairs={{0,63},{1,2},{2,1},{3,4},{4,3},{5,6},{6,5},{7,8},{8,7},{9,10},{10,... | collective-permute-start | bytes 73736 | tf_op jit(solution)/shard_map/ppermute | solution.py:674
  5.0 1.9 %slot_lookup.1 = (s32[256,128]{1,0:T(8,128)S(1)}, f32[256,128]{1,0:T(8,128)S(1)}, f32[256,128]{1,0:T(8,128)S(1)}, f32[8,128]{1,0:T(8,128)S(1)}) custom-call(s32[254,128]{1,0:T(8,128)S(1)} %get-tuple-element.32.owner_ref, s32[64,512]{1,0:T(8,128)S(1)} %get-tuple-element.33.label_ref), custom_call_target="tpu_custom_call" | custom-call | flops 1073741824 | bytes 524288 | tf_op jit(solution)/shard_map/slot_lookup/pallas_call | solution.py:255
  6.9 6.3 %collective-permute-start = (f32[12,512]{1,0:T(8,128)S(1)}, f32[12,512]{1,0:T(8,128)S(1)}, u32[]{:S(2)}, u32[]{:S(2)}) collective-permute-start(f32[12,512]{1,0:T(8,128)S(1)} %get-tuple-element.35), channel_id=1, source_target_pairs={{0,1},{1,0},{2,3},{3,2},{4,5},{5,4},{6,7},{7,6},{8,9},{9,8},{10,11... | collective-permute-start | bytes 73736 | tf_op jit(solution)/shard_map/ppermute | solution.py:668
  13.2 3.0 %inner_rows.1 = (f32[256,256]{1,0:T(8,128)S(1)}, f32[64,512]{1,0:T(8,128)S(1)}, f32[16,32]{1,0:T(8,128)S(1)}) custom-call(f32[64,512]{1,0:T(8,128)S(1)} %get-tuple-element.28.depth_ref, f32[64,512]{1,0:T(8,128)S(1)} %get-tuple-element.29.rough_ref_, f32[64,512]{1,0:T(8,128)S(1)} %get-tuple-element.30.seed_ref, s32[64,512]{1,0:T(8,128)S(1)} %get-tuple-element.33.label_ref, ...), custom_call_target="tpu_custom_call" | custom-call | flops 2147483648 | bytes 655360 | tf_op jit(solution)/shard_map/inner_rows/pallas_call | solution.py:449
  16.2 0.0 collective-permute-done.1.away_ref
  16.2 0.0 collective-permute-done.chip_ref
  16.2 0.0 copy-start
  16.2 0.0 copy-start.1
  16.2 0.0 copy-start.2
  16.2 2.1 %zone_partials.1 = (f32[128,256]{1,0:T(8,128)S(1)}, f32[128,256]{1,0:T(8,128)S(1)}, f32[64,512]{1,0:T(8,128)S(1)}) custom-call(f32[64,512]{1,0:T(8,128)S(1)} %get-tuple-element.28.depth_ref, f32[64,512]{1,0:T(8,128)S(1)} %get-tuple-element.29.rough_ref_, f32[64,512]{1,0:T(8,128)S(1)} %get-tuple-element.30.seed_ref, ...), custom_call_target="tpu_custom_call" | custom-call | tf_op jit(solution)/shard_map/zone_partials/pallas_call | solution.py:555
  18.3 0.1 collective-permute-start.2
  18.4 0.0 copy-done
  18.4 0.0 copy-done.1
  18.4 0.0 copy-done.2
  18.4 0.8 %reach_maps.1 = (f32[32,128]{1,0:T(8,128)S(1)}, f32[32,128]{1,0:T(8,128)S(1)}, f32[2,128]{1,0:T(2,128)S(1)}) custom-call(f32[64,512]{1,0:T(8,128)S(1)} %get-tuple-element.46.adjoint_ref, s32[32,128]{1,0:T(8,128)S(1)} %copy-done, f32[32,128]{1,0:T(8,128)S(1)} %copy-done.1, f32[32,128]{1,0:T(8,128)S(1)} %copy-done.2), custom_call_target="tpu_custom_call" | custom-call | tf_op jit(solution)/shard_map/reach_maps/pallas_call | solution.py:657
  19.3 0.5 %collective-permute-done.2.other_ref = f32[128,256]{1,0:T(8,128)S(1)} collective-permute-done((f32[128,256]{1,0:T(8,128)S(1)}, f32[128,256]{1,0:T(8,128)S(1)}, u32[]{:S(2)}, u32[]{:S(2)}) %collective-permute-start.2) | collective-permute-done | bytes 131104 | tf_op jit(solution)/shard_map/ppermute | solution.py:668
  19.8 22.5 %all_to_all.5 = f32[128,4,128]{2,1,0:T(4,128)S(1)} all-to-all(f32[128,4,128]{2,1,0:T(4,128)S(1)} %bitcast.10), channel_id=1, replica_groups=mesh['basin'=4,'y'=4,'z'=8,'core'=2] {'y','basin','z'}, dimensions={0} | all-to-all | bytes 524288 | tf_op jit(solution)/shard_map/all_to_all | solution.py:698
  42.3 0.7 %results.1 = (f32[1,127]{1,0:T(1,128)}, f32[1,127]{1,0:T(1,128)}, f32[32,128]{1,0:T(8,128)}) custom-call(f32[512,128]{1,0:T(8,128)S(1)} %bitcast.9, f32[32,128]{1,0:T(8,128)S(1)} %get-tuple-element.48.rate_ref, f32[32,128]{1,0:T(8,128)S(1)} %get-tuple-element.49.push_ref), custom_call_target="tpu_custom_call" | custom-call | tf_op jit(solution)/shard_map/results/pallas_call | solution.py:614
  (1 shorter events, 0.0 us)
Async XLA Ops:
  1.8 14.3 %collective-permute-start.1 = (f32[12,512]{1,0:T(8,128)S(1)}, f32[12,512]{1,0:T(8,128)S(1)}, u32[]{:S(2)}, u32[]{:S(2)}) collective-permute-start(f32[12,512]{1,0:T(8,128)S(1)} %get-tuple-element.36), channel_id=1, source_target_pairs={{0,63},{1,2},{2,1},{3,4},{4,3},{5,6},{6,5},{7,8},{8,7},{9,10},{10,... | collective-permute-start | bytes 73736 | tf_op jit(solution)/shard_map/ppermute | solution.py:674
  6.9 9.3 %collective-permute-start = (f32[12,512]{1,0:T(8,128)S(1)}, f32[12,512]{1,0:T(8,128)S(1)}, u32[]{:S(2)}, u32[]{:S(2)}) collective-permute-start(f32[12,512]{1,0:T(8,128)S(1)} %get-tuple-element.35), channel_id=1, source_target_pairs={{0,1},{1,0},{2,3},{3,2},{4,5},{5,4},{6,7},{7,6},{8,9},{9,8},{10,11... | collective-permute-start | bytes 73736 | tf_op jit(solution)/shard_map/ppermute | solution.py:668
  16.2 2.2 %copy-start = (s32[32,128]{1,0:T(8,128)S(1)}, s32[32,128]{1,0:T(8,128)}, u32[]{:S(2)}) copy-start(s32[32,128]{1,0:T(8,128)} %cell_ref.1) | copy-start | bytes 49156
  16.2 2.2 %copy-start.1 = (f32[32,128]{1,0:T(8,128)S(1)}, f32[32,128]{1,0:T(8,128)}, u32[]{:S(2)}) copy-start(f32[32,128]{1,0:T(8,128)} %keep_ref.1) | copy-start | bytes 49156
  16.2 2.2 %copy-start.2 = (f32[32,128]{1,0:T(8,128)S(1)}, f32[32,128]{1,0:T(8,128)}, u32[]{:S(2)}) copy-start(f32[32,128]{1,0:T(8,128)} %forcing_ref.1) | copy-start | bytes 49156
  18.3 1.4 %collective-permute-start.2 = (f32[128,256]{1,0:T(8,128)S(1)}, f32[128,256]{1,0:T(8,128)S(1)}, u32[]{:S(2)}, u32[]{:S(2)}) collective-permute-start(f32[128,256]{1,0:T(8,128)S(1)} %get-tuple-element.45), channel_id=1, source_target_pairs={{0,1},{1,0},{2,3},{3,2},{4,5},{5,4},{6,7},{7,6},{8,9},{9,8},{10,11... | collective-permute-start | bytes 393224 | tf_op jit(solution)/shard_map/ppermute | solution.py:668
